TPU v7x, 32 devices: a whole 2x2x4 slice. The times are simulated.
32 devices in a mesh: segment: 4 (over y, x), wide: 8 (over z, core).
Axes of the slice: x: 2, y: 2, z: 4, core: 2. Of those that a mesh axis runs over, the one named last changes fastest.
Arguments:
- entering_hidden: bfloat16 [2, 16, 8192], P(None, 'wide'), may hold values from -6 to 6
- row_adapter_index: int32 [2, 16, 1], P(None, 'wide'), may hold values from 0 to 7; in each aligned block of 16 rows (0 to 15, 16 to 31, ..., all dimensions but the last counted through in order) at most 4 rows name the same one
- lengths: int32 [2, 16], P(None, 'wide'), may hold values from 2 to 384
- input_norm_gain: bfloat16 [4, 8192], P('segment'), may hold values from 0.099609375 to 1.8984375
- query_matrix: bfloat16 [4, 8192, 8192], P('segment', None, 'wide'), may hold values from -0.0625 to 0.0625
- key_matrix: bfloat16 [4, 8192, 1024], P('segment', None, 'wide'), may hold values from -0.0625 to 0.0625
- value_matrix: bfloat16 [4, 8192, 1024], P('segment', None, 'wide'), may hold values from -0.0625 to 0.0625
- output_matrix: bfloat16 [4, 8192, 8192], P('segment', None, 'wide'), may hold values from -0.0625 to 0.0625
- adapter_down_maps: bfloat16 [4, 8, 8192, 128], P('segment', 'wide'), may hold values from -0.0625 to 0.0625
- adapter_up_query: bfloat16 [4, 8, 64, 8192], P('segment', 'wide'), may hold values from -0.75 to 0.75
- adapter_up_value: bfloat16 [4, 8, 64, 1024], P('segment', 'wide'), may hold values from -0.75 to 0.75
- rotated_key_cache: bfloat16 [4, 2, 16, 384, 1024], P('segment', None, 'wide'), may hold values from -480 to 480
- cached_values: bfloat16 [4, 2, 16, 384, 1024], P('segment', None, 'wide'), may hold values from -6 to 6
Outputs:
- layer_out: bfloat16 [4, 2, 16, 8192], P('segment', None, 'wide')
Inputs may be any that keep to these rules, and one draw needn't show every extreme that they name: `row_adapter_index`: in each micro-batch no adapter is named by more than 4 rows.
All inputs are finite; a program needn't handle non-finite values.
Results may differ from a plain program's by a relative error of at most 0.038.
Values may be sent and summed in bfloat16 or wider, within the bound.
No kernel may reach another device: no remote copies, remote signals or barrier semaphores. Data moves between devices by JAX's collectives and lax.ppermute only.
A program may use at most 128 MiB of HBM per device.

v0:
```python
import functools

import jax
import jax.numpy as jnp
import numpy as np
from jax import lax
from jax.experimental import pallas as pl
from jax.experimental.pallas import tpu as pltpu
from jax.sharding import PartitionSpec as P

HEADS = 64
KVH = 8
HD = 128
ADAPTER_RANK = 64
CAP = 4


adapter_scale = 0.5
rope_base = 500000.0
epsilon = 1e-05

GROUP = HEADS // KVH
MIB = 1 << 20
STEP = 256
VMEM = pl.BlockSpec(memory_space=pltpu.VMEM)
SMEM = pl.BlockSpec(memory_space=pltpu.SMEM)


def swapped(value, bits):
    count = lax.axis_size("wide")
    return lax.ppermute(value, "wide", [(i, i ^ bits) for i in range(count)])


def then(arrays, work):
    if work is None:
        return arrays, None
    done = work()
    arrays = arrays[::-1]
    arrays = pl.pallas_call(
        lambda *refs: None,
        out_shape=[jax.ShapeDtypeStruct(array.shape, array.dtype) for array in arrays],
        in_specs=[VMEM] * len(arrays) + [pl.BlockSpec(memory_space=pl.ANY)],
        out_specs=[VMEM] * len(arrays),
        input_output_aliases={i: i for i in range(len(arrays))},
        compiler_params=pltpu.CompilerParams(vmem_limit_bytes=MIB),
        name="then",
    )(*arrays, done)
    return arrays[::-1], done


def gathered(value, work=None):
    count = lax.axis_size("wide")
    far = [swapped(value, k) for k in range(2, count, 2)]
    far, done = then(far, work)
    found = [part for one in [value, *far] for part in (one, swapped(one, 1))]
    return found, done


def passed_on(value, s):
    count = lax.axis_size("wide")

    def shifted(bits):
        pairs = [(s * count + i, (s + 1) * count + (i ^ bits)) for i in range(count)]
        return lax.ppermute(value, ("segment", "wide"), pairs)

    far = [shifted(bits) for bits in range(0, count, 2)]
    return [part for one in far for part in (one, swapped(one, 1))]


def exchanged(blocks, work=None):
    far = [swapped(block, 2 * k) for k, block in enumerate(blocks) if k]
    far, done = then(far, work)
    return [blocks[0], *far], done


def resident(weight):
    return pltpu.with_memory_space_constraint(weight, pltpu.VMEM)


def call(body, out_shape, operands, scratch=(), limit=8, kept=(), through=(), cost=1, name=None):
    outs, count = list(out_shape), len(operands) + len(kept)
    inner = body
    if through:

        def inner(*refs):
            inputs = count + len(through)
            shown = inputs + len(outs)
            body(*refs[:count], *refs[inputs:shown], *refs[shown + len(through) :])

    found = pl.pallas_call(
        inner,
        out_shape=outs + [pltpu.VMEM(array.shape, array.dtype) for array in through],
        in_specs=[spec for _, spec in operands] + [VMEM] * (len(kept) + len(through)),
        out_specs=[VMEM] * (len(outs) + len(through)),
        input_output_aliases={count + i: len(outs) + i for i in range(len(through))},
        scratch_shapes=list(scratch),
        compiler_params=pltpu.CompilerParams(vmem_limit_bytes=limit * MIB),
        cost_estimate=pl.CostEstimate(flops=0, transcendentals=0, bytes_accessed=cost * MIB),
        name=name,
    )(*[array for array, _ in operands], *[resident(array) for array in [*kept, *through]])
    return list(found)


def load_kernel(sizes, plan, work, *refs):
    sources, small, outs, more = [], [], [], []
    refs = list(refs)
    for group, size in zip((sources, small, outs, more), sizes, strict=True):
        group.extend(refs[:size])
        del refs[:size]
    copies = [
        pltpu.make_async_copy(source, out, refs[0].at[i])
        for i, (source, out) in enumerate(plan(sources, outs))
    ]
    for copy in copies:
        copy.start()
    work(small, more)
    for copy in copies:
        copy.wait()


def loaded(sources, shapes, plan, copies, small, more, work):
    moved = sum(2 * int(np.prod(shape)) for shape in shapes)
    found = pl.pallas_call(
        functools.partial(
            load_kernel, (len(sources), len(small), len(shapes), len(more)), plan, work
        ),
        out_shape=[pltpu.VMEM(shape, jnp.bfloat16) for shape in shapes] + list(more),
        in_specs=[pl.BlockSpec(memory_space=pl.ANY)] * len(sources) + [spec for _, spec in small],
        out_specs=[VMEM] * (len(shapes) + len(more)),
        scratch_shapes=[pltpu.SemaphoreType.DMA((copies,))],
        compiler_params=pltpu.CompilerParams(vmem_limit_bytes=4 * MIB),
        cost_estimate=pl.CostEstimate(flops=0, transcendentals=0, bytes_accessed=moved),
        name="load",
    )(
        *[pltpu.with_memory_space_constraint(source, pltpu.HBM) for source in sources],
        *[array for array, _ in small],
    )
    return found[: len(shapes)], found[len(shapes) :]


def half_of(other, sources, outs):
    core = (lax.axis_index("wide") + other) % 2
    pairs = []
    for source, out in zip(sources, outs, strict=True):
        for i in range(out.shape[2] // HD):
            there = pl.ds(pl.multiple_of((2 * i + core) * HD, HD), HD)
            pairs.append((source.at[:, :, there], out.at[:, :, pl.ds(i * HD, HD)]))
    return pairs


TOKEN = jax.ShapeDtypeStruct((8, HD), jnp.float32)


def token_of(small, more):
    more[0][...] = small[0][:8, :HD].astype(jnp.float32)


def load_rest_kernel(first, source, after, _, out, token, sem):
    copy = pltpu.make_async_copy(source.at[:, first:], out.at[:, first:], sem)
    copy.start()
    token[...] = after[:8, :HD].astype(jnp.float32)
    copy.wait()


def dot(left, right):
    return jnp.dot(left, right, preferred_element_type=jnp.float32)


def matmul_into(store, source, weight, step):
    def one(i, carry):
        columns = pl.ds(pl.multiple_of(i * step, step), step)
        store(columns, dot(source[...], weight[:, columns]))
        return carry

    lax.fori_loop(0, weight.shape[1] // step, one, 0)


def while_live(tick, body):
    def run(*refs):
        pl.when(lax.axis_index("segment") == tick)(lambda: body(*refs))

    return run


def by_part(owner, chunks, own_rows):
    count = len(chunks)
    parts = chunks[0].shape[0] // own_rows
    total = count * parts * own_rows
    stack = jnp.concatenate([chunk[...] for chunk in chunks], 0)
    out = lax.broadcasted_iota(jnp.int32, (total, total), 0)
    src = lax.broadcasted_iota(jnp.int32, (total, total), 1)
    rows = own_rows
    part_out = out // (rows * count)
    device_out = (out // rows) % count
    part_src = (src // rows) % parts
    device_src = (src // (rows * parts)) ^ owner
    hit = (part_out == part_src) & (device_out == device_src) & (out % rows == src % rows)
    return dot(jnp.where(hit, 1.0, 0.0).astype(jnp.bfloat16), stack)


def adapter_part(owner, ident, normed, adapter, outs, capacity):
    down, up_query, up_value = adapter
    rows = normed.shape[0]
    count = 2 * len(outs)
    low = dot(normed[...], down[0]).astype(jnp.bfloat16)
    place = lax.broadcasted_iota(jnp.int32, (rows, rows), 0)
    other = lax.broadcasted_iota(jnp.int32, (rows, rows), 1)
    mine = jnp.where(ident[:, :1] == owner.astype(jnp.float32), 1.0, 0.0)
    flat = jnp.where(place == other, mine, 0.0).astype(jnp.bfloat16)
    before = jnp.where(place < other, mine, 0.0).astype(jnp.bfloat16)
    ones = jnp.ones((capacity, rows), jnp.bfloat16)
    member = dot(ones, flat)
    rank = dot(ones, before)
    slot = lax.broadcasted_iota(jnp.int32, (capacity, rows), 0).astype(jnp.float32)
    chosen = jnp.where((member > 0.5) & (rank == slot), 1.0, 0.0).astype(jnp.bfloat16)
    picked = dot(chosen, low).astype(jnp.bfloat16)
    query_cols = up_query.shape[2] // count
    value_cols = up_value.shape[2] // count
    for j in range(count):
        out, there = outs[j // 2], owner ^ j
        slots = slice((j % 2) * capacity, (j % 2 + 1) * capacity)
        columns = pl.ds(pl.multiple_of(there * query_cols, query_cols), query_cols)
        for_query = dot(picked[:, :ADAPTER_RANK], up_query[0, :, columns]) * adapter_scale
        out[slots, :query_cols] = for_query.astype(jnp.bfloat16)
        columns = pl.ds(pl.multiple_of(there * value_cols, value_cols), value_cols)
        for_value = dot(picked[:, ADAPTER_RANK:], up_value[0, :, columns]) * adapter_scale
        out[slots, query_cols:] = for_value.astype(jnp.bfloat16)


def open_kernel(hidden, names_ref, entering, names, sem):
    copy = pltpu.make_async_copy(names_ref, names, sem)
    copy.start()
    micro, local_rows, width = hidden.shape
    own_rows = micro * local_rows
    part = entering.shape[1] - HD
    count = width // part
    rows = jnp.concatenate([hidden[m].astype(jnp.float32) for m in range(micro)], 0)
    entering[:, :part] = jnp.concatenate(
        [rows[:, i * part : (i + 1) * part] for i in range(count)], 0
    ).astype(jnp.bfloat16)
    row = lax.broadcasted_iota(jnp.int32, (count * own_rows, HD), 0) % own_rows
    name = jnp.zeros((count * own_rows, HD), jnp.float32)
    copy.wait()
    for r in range(own_rows):
        one = names[r // local_rows, 0, r % local_rows].astype(jnp.float32)
        name = jnp.where(row == r, one, name)
    entering[:, part:] = name.astype(jnp.bfloat16)


def row_lengths(lengths, near_lengths, shape, each=GROUP):
    micro, local_rows = lengths.shape
    own_rows = micro * local_rows
    row = lax.broadcasted_iota(jnp.int32, shape, 0) // each
    found = jnp.zeros(shape, jnp.int32)
    for i in range(2 * own_rows):
        source, r = (lengths, near_lengths)[i // own_rows], i % own_rows
        found = jnp.where(row == i, source[r // local_rows, r % local_rows], found)
    return found


def angle_work(small, more):
    lengths, near_lengths, inverse = small
    cosine, sine = more
    angles = row_lengths(lengths, near_lengths, cosine.shape).astype(jnp.float32) * inverse[...]
    front = lax.broadcasted_iota(jnp.int32, cosine.shape, 1) < HD // 2
    cosine[...] = jnp.cos(angles)
    sine[...] = jnp.where(front, -jnp.sin(angles), jnp.sin(angles))


def enter_kernel(count, own_rows, capacity, tick, *refs):
    chunks, rest = refs[:count], refs[count:]
    _, gain, *adapters, normed, held, ident = rest[:8]
    *correction, spread = rest[8:]
    owner = lax.axis_index("wide")
    rows = count * own_rows
    part = gain.shape[1] // count
    spread[...] = by_part(owner, chunks, own_rows)
    ident[...] = spread[:rows, part:]

    @pl.when(lax.axis_index("segment") == tick)
    def _():
        squares = jnp.zeros((rows, 1), jnp.float32)
        for i in range(count):
            block = spread[i * rows : (i + 1) * rows, :part]
            squares += jnp.sum(block * block, 1, keepdims=True)
        scale = lax.rsqrt(squares / gain.shape[1] + epsilon)
        for i in range(count):
            block = spread[i * rows : (i + 1) * rows, :part]
            columns = slice(i * part, (i + 1) * part)
            weight = gain[:, columns].astype(jnp.float32)
            normed[:, columns] = (block * scale * weight).astype(jnp.bfloat16)
        own = pl.ds(pl.multiple_of(owner * rows, rows), rows)
        held[...] = spread[own, :part].astype(jnp.bfloat16)
        adapter_part(owner, ident, normed, adapters, correction, capacity)


def norm_kernel(count, capacity, *refs):
    chunks, rest = refs[:count][::-1], refs[count:]
    ident, gain, *adapters, normed = rest[:6]
    correction = rest[6:]
    owner = lax.axis_index("wide")
    rows, part = chunks[0].shape
    squares = jnp.zeros((rows, 1), jnp.float32)
    for chunk in chunks:
        block = chunk[...].astype(jnp.float32)
        squares += jnp.sum(block * block, 1, keepdims=True)
    scale = lax.rsqrt(squares / gain.shape[1] + epsilon)
    for k, chunk in enumerate(chunks):
        columns = pl.ds(pl.multiple_of((owner ^ k) * part, part), part)
        weight = gain[:, columns].astype(jnp.float32)
        normed[:, columns] = (chunk[...].astype(jnp.float32) * scale * weight).astype(jnp.bfloat16)
    adapter_part(owner, ident, normed, adapters, correction, capacity)


def project_kernel(normed, query, out):
    def store(columns, product):
        out[:, columns] = product

    matmul_into(store, normed, query, STEP)


def narrow_kernel(normed, key, value, out):
    narrow = key.shape[1]
    out[:, :narrow] = dot(normed[...], key[...])
    out[:, narrow:] = dot(normed[...], value[...])


def project_first_kernel(first, tick, normed, whole_query, _, out, query, sems):
    copies = []
    for i in range(1, query.shape[1] // first):
        here = pl.ds(i * first, first)
        copies.append(
            pltpu.make_async_copy(whole_query.at[:, here], query.at[:, here], sems.at[i - 1])
        )
    for copy in copies[:2]:
        copy.start()
    live = lax.axis_index("segment") == tick
    for i in range(len(copies) + 1):
        if i:
            copies[i - 1].wait()
            if i + 1 < len(copies):
                copies[i + 1].start()

        @pl.when(live)
        def _():
            here = slice(i * first, (i + 1) * first)
            out[:, here] = dot(normed[...], query[:, here])


def received_rows(received):
    half = received[0].shape[0] // 2
    return [ref[(j % 2) * half : (j % 2 + 1) * half, :] for j, ref in enumerate(received)]


def correct_kernel(count, capacity, base, narrow, ident, *refs):
    received, outs = refs[:count], refs[count:]
    owner = lax.axis_index("wide")
    rows = base.shape[0]
    own_rows = rows // count
    slots = count * capacity
    place = lax.broadcasted_iota(jnp.int32, (rows, rows), 0)
    other = lax.broadcasted_iota(jnp.int32, (rows, rows), 1)
    own = ident[:, :1]
    flat = jnp.where(place == other, own, 0.0).astype(jnp.bfloat16)
    line = dot(jnp.ones((rows, rows), jnp.bfloat16), flat)
    rank = jnp.sum(jnp.where((own == line) & (other < place), 1.0, 0.0), 1, keepdims=True)
    slot = lax.broadcasted_iota(jnp.int32, (rows, slots), 1)
    source = ((slot // capacity) ^ owner).astype(jnp.float32)
    hit = (source == own) & ((slot % capacity).astype(jnp.float32) == rank)
    table = jnp.where(hit, 1.0, 0.0).astype(jnp.bfloat16)
    placed = dot(table, jnp.concatenate(received_rows(received), 0))
    query_cols, key_cols = base.shape[1], narrow.shape[1] // 2
    first = base[...] + placed[:, :query_cols]
    middle = narrow[:, :key_cols]
    last = narrow[:, key_cols:] + placed[:, query_cols:]
    packed = jnp.concatenate([first, middle, last], 1).astype(jnp.bfloat16)
    by_destination(owner, packed, own_rows, outs)


def by_destination(owner, packed, own_rows, outs):
    rows = packed.shape[0]
    place = lax.broadcasted_iota(jnp.int32, (rows, rows), 0)
    other = lax.broadcasted_iota(jnp.int32, (rows, rows), 1)
    hit = (((place // own_rows) ^ owner) == other // own_rows) & (
        place % own_rows == other % own_rows
    )
    order = jnp.where(hit, 1.0, 0.0).astype(jnp.bfloat16)
    sorted_rows = dot(order, packed).astype(jnp.bfloat16)
    for k, out in enumerate(outs):
        out[...] = sorted_rows[k * 2 * own_rows : (k + 1) * 2 * own_rows, :]


def attend_kernel(chips, lengths, near_lengths, *refs):
    arrived, rest = refs[:chips][::-1], refs[chips:]
    cosine, sine, keys, values, near_keys, near_values, out, scores, weights = rest
    chip = lax.axis_index("wide") // 2
    own_rows, span = keys.shape[:2]
    chip_rows = 2 * own_rows
    rows = GROUP * chip_rows
    cos, sin = cosine[...], sine[...]
    position = lax.broadcasted_iota(jnp.int32, (2 * rows, span), 1)
    valid = position < row_lengths(lengths, near_lengths, (2 * rows, span), 2 * GROUP)
    score_scale = HD ** (-0.5)

    def turned(vectors):
        return vectors * cos + pltpu.roll(vectors, HD // 2, 1) * sin

    def rounded(vectors):
        return vectors.astype(jnp.bfloat16).astype(jnp.float32)

    pieces = []
    for ref in arrived:
        packed = ref[...].astype(jnp.float32)
        heads = [packed[:, i * HD : (i + 1) * HD] for i in range(GROUP)]
        fresh = [packed[:, GROUP * HD :]] * GROUP
        pieces += [jnp.concatenate(heads, 0), jnp.concatenate(fresh, 0)]
    out_row = lax.broadcasted_iota(jnp.int32, (rows, rows), 0)
    src_row = lax.broadcasted_iota(jnp.int32, (rows, rows), 1)
    same = (out_row // GROUP == src_row % chip_rows) & (out_row % GROUP == src_row // chip_rows)
    order = jnp.where(same, 1.0, 0.0).astype(jnp.bfloat16)
    sorted_rows = dot(order, jnp.concatenate(pieces, 1).astype(jnp.bfloat16))
    band = 2 * GROUP

    def woven(one, two):
        bands = [slice(r * GROUP, (r + 1) * GROUP) for r in range(chip_rows)]
        return jnp.concatenate([part[rows_of] for rows_of in bands for part in (one, two)], 0)

    def pair_lanes(p):
        return pl.ds(pl.multiple_of((chip // 2 ^ p) * 2 * HD, 2 * HD), 2 * HD)

    even = chip % 2 == 0
    zero = jnp.zeros((rows, HD), jnp.float32)
    pairs = range(chips // 2)
    fresh = []
    for p in pairs:
        wide, own, new_values = [], [], []
        for n in range(2):
            piece = sorted_rows[:, (2 * p + n) * 3 * HD : (2 * p + n + 1) * 3 * HD]
            query = rounded(turned(piece[:, :HD]))
            new_key = rounded(turned(piece[:, HD : 2 * HD]))
            own.append(jnp.sum(query * new_key, 1, keepdims=True) * score_scale)
            new_values.append(piece[:, 2 * HD :])
            left = even if n == 0 else jnp.logical_not(even)
            wide.append(
                jnp.concatenate([jnp.where(left, query, zero), jnp.where(left, zero, query)], 1)
            )
        fresh.append((woven(*own), woven(*new_values)))
        wide = woven(*wide).astype(jnp.bfloat16)
        for r in range(chip_rows):
            first = (p * chip_rows + r) * band
            scores[first : first + band, :] = lax.dot_general(
                wide[r * band : (r + 1) * band, :],
                (keys, near_keys)[r // own_rows][r % own_rows, :, pair_lanes(p)],
                (((1,), (1,)), ((), ())),
                preferred_element_type=jnp.float32,
            )
    parts = []
    for p, (own, new_value) in enumerate(fresh):
        here = slice(p * 2 * rows, (p + 1) * 2 * rows)
        found = jnp.where(valid, scores[here, :] * score_scale, -1e30)
        top = jnp.maximum(jnp.max(found, 1, keepdims=True), own)
        past = jnp.where(valid, jnp.exp(found - top), 0.0)
        own = jnp.exp(own - top)
        total = jnp.sum(past, 1, keepdims=True) + own
        weights[here, :] = (past / total).astype(jnp.bfloat16)
        parts.append(rounded(own / total) * new_value)
    for p, own_part in enumerate(parts):
        mixed = []
        for r in range(chip_rows):
            first = (p * chip_rows + r) * band
            found = dot(
                weights[first : first + band, :],
                (values, near_values)[r // own_rows][r % own_rows, :, pair_lanes(p)],
            )
            mine = own_part[r * band : (r + 1) * band, :]
            one = jnp.where(even, found[:GROUP, :HD], found[:GROUP, HD:]) + mine[:GROUP]
            two = jnp.where(even, found[GROUP:, HD:], found[GROUP:, :HD]) + mine[GROUP:]
            both = [jnp.where(even, one, two), jnp.where(even, two, one)]
            mixed.append(jnp.concatenate(both, 1))
        out[:, pair_lanes(p)] = jnp.concatenate(mixed, 0).astype(jnp.bfloat16)


def attended_rows(owner, chunks, own_rows, rows_ref):
    count = len(chunks)
    chips = count // 2
    rows = own_rows * count
    total = rows * GROUP
    out = lax.broadcasted_iota(jnp.int32, (total, total), 0)
    src = lax.broadcasted_iota(jnp.int32, (total, total), 1)
    device_out = (out // own_rows) % count
    chip_rows = 2 * own_rows
    row_src = (src // GROUP) % chip_rows
    near = (out // rows == src % GROUP) & (out % own_rows == row_src % own_rows)
    for core in range(2):
        stack = jnp.concatenate([chunks[2 * k + core][...] for k in range(chips)], 0)
        device_src = owner ^ (2 * (src // (GROUP * chip_rows)) + core) ^ (row_src // own_rows)
        hit = near & (device_out == device_src)
        spread = dot(jnp.where(hit, 1.0, 0.0).astype(jnp.bfloat16), stack).astype(jnp.bfloat16)
        first = (owner ^ core) % 2
        for i in range(chips):
            for j in range(GROUP):
                head = (2 * i + first) * GROUP + j
                rows_ref[:, pl.ds(pl.multiple_of(head * HD, HD), HD)] = spread[
                    j * rows : (j + 1) * rows, i * HD : (i + 1) * HD
                ]


def leave_kernel(count, own_rows, tick, *refs):
    chunks, rest = refs[:count], refs[count:]
    held, result = rest[0], rest[1] if tick else None
    matrix, out, kept, *outs, rows_ref = rest[2 if tick else 1 :]
    kept[...] = result[...] if tick else jnp.zeros_like(kept)

    @pl.when(lax.axis_index("segment") == tick)
    def _():
        attended_rows(lax.axis_index("wide"), chunks, own_rows, rows_ref)

        def store(columns, product):
            total = held[:, columns].astype(jnp.float32) + product
            out[:, columns] = total.astype(jnp.bfloat16)
            kept[:, columns] = total.astype(jnp.bfloat16)

        matmul_into(store, rows_ref, matrix, 2 * STEP)

    if outs:
        by_destination(lax.axis_index("wide"), kept[...], own_rows, outs)


def join_kernel(count, *refs):
    blocks, out = refs[:count][::-1], refs[count]
    for j, block in enumerate(blocks):
        rows = block.shape[0] // 2
        half = block[(j % 2) * rows : (j % 2 + 1) * rows, :]
        width = half.shape[1]
        columns = pl.ds(pl.multiple_of((lax.axis_index("wide") ^ j) * width, width), width)
        for m in range(out.shape[1]):
            local_rows = out.shape[2]
            out[0, m, :, columns] = half[m * local_rows : (m + 1) * local_rows, :]


def on_device_by_head(
    entering_hidden,
    row_adapter_index,
    lengths,
    input_norm_gain,
    query_matrix,
    key_matrix,
    value_matrix,
    output_matrix,
    adapter_down_maps,
    adapter_up_query,
    adapter_up_value,
    rotated_key_cache,
    cached_values,
):
    segments = lax.axis_size("segment")
    count = lax.axis_size("wide")
    micro, local_rows, width = entering_hidden.shape
    own_rows = micro * local_rows
    rows = own_rows * count
    capacity = CAP * micro
    part = width // count
    query_cols, key_cols = query_matrix.shape[2], key_matrix.shape[2]
    packed_cols = query_cols + 2 * key_cols
    span = rotated_key_cache.shape[3]

    chips = count // 2
    head_lanes = chips * HD
    query_weight = query_matrix[0]
    output_weight = output_matrix[0]
    adapters = [adapter_down_maps[0], adapter_up_query[0], adapter_up_value[0]]
    caches = [cache[0].reshape(own_rows, span, -1) for cache in (rotated_key_cache, cached_values)]
    near_lengths = swapped(lengths, 1)
    gain = input_norm_gain
    half = HD // 2
    inverse = np.tile(rope_base ** (-np.arange(half) / half), 2).astype(np.float32)[None]

    def blocks_of(slots, columns):
        return [jax.ShapeDtypeStruct((2 * slots, columns), jnp.bfloat16)] * chips

    normed_shape = jax.ShapeDtypeStruct((rows, width), jnp.bfloat16)
    held_shape = jax.ShapeDtypeStruct((rows, part), jnp.bfloat16)
    ident_shape = jax.ShapeDtypeStruct((rows, HD), jnp.float32)
    base_shape = jax.ShapeDtypeStruct((rows, query_cols), jnp.float32)
    narrow_shape = jax.ShapeDtypeStruct((rows, 2 * key_cols), jnp.float32)
    angle_shape = jax.ShapeDtypeStruct((GROUP * 2 * own_rows, HD), jnp.float32)
    correction_shapes = blocks_of(capacity, query_cols + key_cols)
    query_first = query_cols // 4
    output_first = part // 2

    names = pltpu.with_memory_space_constraint(row_adapter_index.transpose(0, 2, 1), pltpu.HBM)
    (entering,) = call(
        open_kernel,
        [jax.ShapeDtypeStruct((rows, part + HD), jnp.bfloat16)],
        [(entering_hidden, VMEM), (names, pl.BlockSpec(memory_space=pl.ANY))],
        [pltpu.SMEM(names.shape, names.dtype), pltpu.SemaphoreType.DMA],
        name="open",
    )
    projections, output_parts, halves, angles = [], [], [None, None], []
    held = ident = None
    result = None
    blocks = []
    for tick in range(segments):
        if tick == 0:

            def load_first():
                sources = [*adapters, key_matrix[0], value_matrix[0], query_weight, *caches]
                small = [(entering, VMEM)]
                shape = (own_rows, span, head_lanes)
                shapes = [source.shape for source in sources[:6]]
                shapes += [shape] * 2

                def plan(sources, outs):
                    pairs = list(zip(sources[:5], outs[:5]))
                    pairs.append((sources[5].at[:, :query_first], outs[5].at[:, :query_first]))
                    return pairs + half_of(1, sources[6:], outs[6:])

                found, (token,) = loaded(
                    sources, shapes, plan, 6 + 2 * chips, small, [TOKEN], token_of
                )
                adapters[:], projections[:] = found[:3], found[3:6]
                halves[2:] = found[6:]
                return token

            chunks, _ = gathered(entering, load_first)
            normed, held, ident, *found = call(
                functools.partial(enter_kernel, count, own_rows, capacity, tick),
                [normed_shape, held_shape, ident_shape] + correction_shapes,
                [(c, VMEM) for c in chunks]
                + [(near_lengths, pl.BlockSpec(memory_space=pl.ANY)), (gain, VMEM)],
                [pltpu.VMEM((count * rows, part + HD), jnp.float32)],
                kept=adapters,
                through=halves[2:],
                name="enter",
            )
            halves[2:] = [swapped(array, 1) for array in found[chips:]]
        else:
            chunks = passed_on(held, tick - 1)
            held = chunks[0]
            normed, *found = call(
                while_live(tick, functools.partial(norm_kernel, count, capacity)),
                [normed_shape] + correction_shapes,
                [(c, VMEM) for c in chunks[::-1]] + [(ident, VMEM), (gain, VMEM)],
                kept=adapters,
                name="norm",
            )
        correction = found[:chips]

        def project():
            return call(
                while_live(tick, project_kernel),
                [base_shape],
                [(normed, VMEM)],
                kept=projections[2:],
                cost=16,
                name="project",
            )[0]

        def project_first():
            base, projections[2] = pl.pallas_call(
                functools.partial(project_first_kernel, query_first, tick),
                out_shape=[base_shape, pltpu.VMEM(query_weight.shape, jnp.bfloat16)],
                in_specs=[VMEM, pl.BlockSpec(memory_space=pl.ANY), VMEM],
                out_specs=[VMEM, VMEM],
                input_output_aliases={2: 1},
                scratch_shapes=[pltpu.SemaphoreType.DMA((query_cols // query_first - 1,))],
                compiler_params=pltpu.CompilerParams(vmem_limit_bytes=8 * MIB),
                cost_estimate=pl.CostEstimate(
                    flops=0, transcendentals=0, bytes_accessed=16 * MIB
                ),
                name="project",
            )(
                normed,
                pltpu.with_memory_space_constraint(query_weight, pltpu.HBM),
                resident(projections[2]),
            )
            return base

        received, base = exchanged(correction, project if tick else project_first)
        received = [part for one in received for part in (one, swapped(one, 1))]
        (narrow,) = call(
            while_live(tick, narrow_kernel),
            [narrow_shape],
            [(normed, VMEM)],
            kept=projections[:2],
            cost=4,
            name="narrow",
        )
        packed = call(
            while_live(
                tick, functools.partial(correct_kernel, count, capacity)
            ),
            blocks_of(own_rows, packed_cols),
            [(base, VMEM), (narrow, VMEM), (ident, VMEM)] + [(r, VMEM) for r in received],
            name="correct",
        )

        def load_part():
            small = [(lengths, SMEM), (near_lengths, SMEM), (jnp.asarray(inverse), VMEM)]
            found, angles[:] = loaded(
                [output_weight, *caches],
                [output_weight.shape] + [(own_rows, span, head_lanes)] * 2,
                lambda sources, outs: [
                    (sources[0].at[:, :output_first], outs[0].at[:, :output_first])
                ]
                + half_of(0, sources[1:], outs[1:]),
                1 + 2 * chips,
                small,
                [angle_shape, angle_shape],
                angle_work,
            )
            output_parts[:], halves[:2] = found[:1], found[1:]
            return angles[0]

        def load_output():
            output_parts[0], token = pl.pallas_call(
                functools.partial(load_rest_kernel, output_first),
                out_shape=[pltpu.VMEM(output_weight.shape, jnp.bfloat16), TOKEN],
                in_specs=[pl.BlockSpec(memory_space=pl.ANY), VMEM, VMEM],
                out_specs=[VMEM, VMEM],
                input_output_aliases={2: 0},
                scratch_shapes=[pltpu.SemaphoreType.DMA],
                compiler_params=pltpu.CompilerParams(vmem_limit_bytes=4 * MIB),
                cost_estimate=pl.CostEstimate(
                    flops=0, transcendentals=0, bytes_accessed=8 * MIB
                ),
                name="load",
            )(
                pltpu.with_memory_space_constraint(output_weight, pltpu.HBM),
                attended,
                resident(output_parts[0]),
            )
            return token

        arrived, _ = exchanged(packed, None if tick else load_part)
        attended, *_ = call(
            while_live(tick, functools.partial(attend_kernel, chips)),
            [jax.ShapeDtypeStruct((GROUP * 2 * own_rows, head_lanes), jnp.bfloat16)],
            [(lengths, SMEM), (near_lengths, SMEM)]
            + [(a, VMEM) for a in [*arrived[::-1], *angles]],
            [
                pltpu.VMEM((chips * GROUP * 2 * own_rows, span), jnp.float32),
                pltpu.VMEM((chips * GROUP * 2 * own_rows, span), jnp.bfloat16),
            ],
            kept=halves,
            name="attend",
        )
        chunks, _ = gathered(attended, None if tick else load_output)
        last = tick == segments - 1
        held, result, *found = call(
            functools.partial(leave_kernel, count, own_rows, tick),
            [held_shape, held_shape] + (blocks_of(own_rows, part) if last else []),
            [(c, VMEM) for c in chunks]
            + [(held, VMEM)] + ([(result, VMEM)] if tick else []),
            [pltpu.VMEM((rows, width), jnp.bfloat16)],
            kept=output_parts,
            name="leave",
        )
        blocks = found
    far, _ = exchanged(blocks)
    far = [part for one in far for part in (one, swapped(one, 1))]
    (joined,) = call(
        functools.partial(join_kernel, count),
        [jax.ShapeDtypeStruct((1, micro, local_rows, width), jnp.bfloat16)],
        [(one, VMEM) for one in far[::-1]],
        name="join",
    )
    return joined


def passed_along(value, axis, steps):
    count = lax.axis_size(axis)
    leading, last = (max(0, -steps), min(count, count - steps))
    return lax.ppermute(value, axis, [(source, source + steps) for source in range(leading, last)])


def rotary(vectors, positions):
    half = vectors.shape[-1] // 2
    inverse = rope_base ** (-jnp.arange(half, dtype=jnp.float32) / half)
    angles = positions.astype(jnp.float32)[:, None] * inverse[None, :]
    cosine = jnp.cos(angles)[:, None, :]
    sine = jnp.sin(angles)[:, None, :]
    front = vectors[..., :half]
    back = vectors[..., half:]
    return jnp.concatenate([front * cosine - back * sine, back * cosine + front * sine], -1)


def attend(query_vector, new_key, fresh_value, positions, key_block, value_block):
    rows = query_vector.shape[0]
    group = HEADS // KVH
    rotated_rows = rotary(
        query_vector.astype(jnp.float32).reshape(rows, HEADS, HD), positions
    ).astype(jnp.bfloat16)
    rotated_rows = rotated_rows.reshape(rows, KVH, group, HD)
    self_key = rotary(new_key.astype(jnp.float32).reshape(rows, KVH, HD), positions).astype(
        jnp.bfloat16
    )
    keys_past = key_block.reshape(rows, -1, KVH, HD)
    values_past = value_block.reshape(rows, -1, KVH, HD)
    score_scale = HD ** (-0.5)
    past = (
        jnp.einsum("bkgd,bpkd->bkgp", rotated_rows, keys_past, preferred_element_type=jnp.float32)
        * score_scale
    )
    self_scores = (
        jnp.einsum("rice,rie->ric", rotated_rows, self_key, preferred_element_type=jnp.float32)
        * score_scale
    )
    valid = jnp.arange(keys_past.shape[1])[None, :] < positions[:, None]
    past = jnp.where(valid[:, None, None, :], past, -1e30)
    top = jnp.maximum(jnp.max(past, -1), self_scores)
    past_exp = jnp.where(valid[:, None, None, :], jnp.exp(past - top[..., None]), 0.0)
    own_exp = jnp.exp(self_scores - top)
    total = jnp.sum(past_exp, -1) + own_exp
    past_weights = (past_exp / total[..., None]).astype(jnp.bfloat16)
    own_weights = (own_exp / total).astype(jnp.bfloat16)
    mixed = jnp.einsum(
        "bkgp,bpkd->bkgd", past_weights, values_past, preferred_element_type=jnp.float32
    )
    mixed = (
        mixed
        + own_weights.astype(jnp.float32)[..., None]
        * fresh_value.reshape(rows, KVH, HD).astype(jnp.float32)[:, :, None, :]
    )
    return mixed.reshape(rows, HEADS * HD).astype(jnp.bfloat16)


def on_device(
    entering_hidden,
    row_adapter_index,
    lengths,
    input_norm_gain,
    query_matrix,
    key_matrix,
    value_matrix,
    output_matrix,
    adapter_down_maps,
    adapter_up_query,
    adapter_up_value,
    rotated_key_cache,
    cached_values,
):
    segments = lax.axis_size("segment")
    segment = lax.axis_index("segment")
    devices = lax.axis_size("wide")
    owner = lax.axis_index("wide")
    small_batch, local_rows, width = entering_hidden.shape
    listed = lax.all_gather(row_adapter_index, "wide", axis=1, tiled=True)[:, :, 0]
    groups = small_batch // small_batch
    capacity = CAP * small_batch
    kept_entries = adapter_down_maps.shape[1]
    adapters = kept_entries * devices
    mine = owner * kept_entries + jnp.arange(kept_entries)
    gain = input_norm_gain[0].astype(jnp.float32)
    query_cols = query_matrix.shape[2]
    key_cols = key_matrix.shape[2]
    passed = jnp.zeros((small_batch * local_rows, width), jnp.bfloat16)
    results = jnp.zeros((small_batch, local_rows, width), jnp.bfloat16)
    ticks = groups + segments - 1
    for tick in range(ticks):
        if tick < groups:
            fresh = entering_hidden.reshape(small_batch * local_rows, width)
        else:
            fresh = jnp.zeros_like(passed)
        rows = jnp.where(segment == 0, fresh, passed)
        index = tick - segment
        live = (index >= 0) & (index < groups)
        index = jnp.clip(index, 0, groups - 1)
        block_rows = rows.shape[0]
        idents = listed
        idents = idents.reshape(small_batch, devices, local_rows).transpose(1, 0, 2).reshape(-1)
        positions = lengths.reshape(-1)
        key_block = rotated_key_cache[0]
        key_block = key_block.reshape(block_rows, key_block.shape[2], key_block.shape[3])
        value_block = cached_values[0]
        value_block = value_block.reshape(block_rows, value_block.shape[2], value_block.shape[3])
        values = rows.astype(jnp.float32)
        normalized_rows = (
            values * lax.rsqrt(jnp.mean(values * values, 1, keepdims=True) + epsilon) * gain
        ).astype(jnp.bfloat16)
        gathered = lax.all_gather(normalized_rows, "wide", axis=0, tiled=True)
        total_rows = gathered.shape[0]
        matches = (idents[None, :] == mine[:, None]).astype(jnp.int32)
        ranks = jnp.cumsum(matches, 1) - 1
        chosen = (matches[:, None, :] == 1) & (
            ranks[:, None, :] == jnp.arange(capacity)[None, :, None]
        )
        chosen = chosen.reshape(kept_entries * capacity, total_rows)
        selected_rows = jnp.dot(
            chosen.astype(jnp.bfloat16), gathered, preferred_element_type=jnp.float32
        ).astype(jnp.bfloat16)
        selected_rows = selected_rows.reshape(kept_entries, capacity, width)
        reduced = jnp.einsum(
            "bpy,byf->bpf", selected_rows, adapter_down_maps[0], preferred_element_type=jnp.float32
        ).astype(jnp.bfloat16)
        member = (idents[:, None] == jnp.arange(adapters)[None, :]).astype(jnp.int32)
        order = jnp.sum(jnp.cumsum(member, 0) * member, 1) - 1
        slot = idents * capacity + order
        slot_table = slot[:, None] == jnp.arange(adapters * capacity)[None, :]
        query_slots = jnp.einsum(
            "acr,are->ace",
            reduced[..., :ADAPTER_RANK],
            adapter_up_query[0],
            preferred_element_type=jnp.float32,
        )
        value_slots = jnp.einsum(
            "acr,are->ace",
            reduced[..., ADAPTER_RANK:],
            adapter_up_value[0],
            preferred_element_type=jnp.float32,
        )
        joined = jnp.concatenate(
            [
                query_slots.reshape(kept_entries * capacity, devices, -1),
                value_slots.reshape(kept_entries * capacity, devices, -1),
            ],
            2,
        )
        received = lax.all_to_all(joined, "wide", split_axis=1, concat_axis=0, tiled=True)
        received = received.reshape(adapters * capacity, -1)
        placed = jnp.dot(slot_table.astype(jnp.float32), received, precision=lax.Precision.HIGHEST)
        query_adjustment = placed[:, :query_cols]
        value_adjustment = placed[:, query_cols:]
        query_vector = (
            jnp.dot(gathered, query_matrix[0], preferred_element_type=jnp.float32)
            + adapter_scale * query_adjustment
        ).astype(jnp.bfloat16)
        new_key = jnp.dot(gathered, key_matrix[0], preferred_element_type=jnp.float32).astype(
            jnp.bfloat16
        )
        fresh_value = (
            jnp.dot(gathered, value_matrix[0], preferred_element_type=jnp.float32)
            + adapter_scale * value_adjustment
        ).astype(jnp.bfloat16)
        packed = jnp.concatenate([query_vector, new_key, fresh_value], 1)
        arrived = lax.all_to_all(packed, "wide", split_axis=0, concat_axis=1, tiled=True).reshape(
            block_rows, devices, -1
        )
        query_rows_local = arrived[:, :, :query_cols].reshape(block_rows, -1)
        key_rows_local = arrived[:, :, query_cols : query_cols + key_cols].reshape(block_rows, -1)
        value_rows_local = arrived[:, :, query_cols + key_cols :].reshape(block_rows, -1)
        attended = attend(
            query_rows_local, key_rows_local, value_rows_local, positions, key_block, value_block
        )
        columns = jnp.dot(
            lax.all_gather(attended, "wide", axis=0, tiled=True),
            output_matrix[0],
            preferred_element_type=jnp.float32,
        )
        returned = lax.all_to_all(columns, "wide", split_axis=0, concat_axis=1, tiled=True)
        outcome = (values + returned).astype(jnp.bfloat16)
        updated = outcome.reshape(small_batch, local_rows, width)
        results = jnp.where(live, updated, results)
        if tick + 1 < ticks:
            passed = passed_along(outcome, "segment", 1)
    return results[None]


def solution(mesh):
    placed = (
        P(None, "wide", None),
        P(None, "wide", None),
        P(None, "wide"),
        P("segment", None),
        P("segment", None, "wide"),
        P("segment", None, "wide"),
        P("segment", None, "wide"),
        P("segment", None, "wide"),
        P("segment", "wide", None, None),
        P("segment", "wide", None, None),
        P("segment", "wide", None, None),
        P("segment", None, "wide", None, None),
        P("segment", None, "wide", None, None),
    )
    by_head = mesh.shape["wide"] == KVH
    return jax.shard_map(
        on_device_by_head if by_head else on_device,
        mesh=mesh,
        in_specs=placed,
        out_specs=P("segment", None, "wide", None),
        check_vma=False,
    )
```

profile of v0, /device:TPU:7, one launch (start us, length us, event | category | flops | bytes accessed | tf_op | source)
XLA Modules:
  0.0 202.7 jit_solution(3320215699235413025)
XLA Ops:
  1.6 3.4 %collective-permute-start.2 = (bf16[32,1152]{1,0:T(8,128)(2,1)S(1)}, bf16[32,1152]{1,0:T(8,128)(2,1)S(1)}, u32[]{:S(2)}, u32[]{:S(2)}) collective-permute-start(bf16[32,1152]{1,0:T(8,128)(2,1)S(1)} %open.1.refs_8_.refs_0_), channel_id=1, source_target_pairs={{0,6},{1,7},{2,4},{3,5},{4,2},{5,3},{6,0},{7,1},{8,14},{9,15},{10,... | collective-permute-start | bytes 221192 | tf_op jit(solution)/shard_map/ppermute | solution.py:31
  5.3 1.4 collective-permute-start.1
  6.7 5.5 %load.3 = (bf16[1,8192,128]{2,1,0:T(8,128)(2,1)S(1)}, bf16[1,64,8192]{2,1,0:T(8,128)(2,1)S(1)}, bf16[1,64,1024]{2,1,0:T(8,128)(2,1)S(1)}, bf16[8192,128]{1,0:T(8...) custom-call(bf16[1,8192,128]{2,1,0:T(8,128)(2,1)} %bitcast.20, ...), custom_call_target="tpu_custom_call" | custom-call | bytes 27394048 | tf_op jit(solution)/shard_map/load/pallas_call | solution.py:123
  15.1 1.9 collective-permute-start.10
  17.0 1.7 collective-permute-start.11
  18.8 2.0 %collective-permute-start.8 = (bf16[16,1152]{1,0:T(8,128)(2,1)S(1)}, bf16[16,1152]{1,0:T(8,128)(2,1)S(1)}, u32[]{:S(2)}, u32[]{:S(2)}) collective-permute-start(bf16[16,1152]{1,0:T(8,128)(2,1)S(1)} %get-tuple-element.109.refs_3_), channel_id=1, source_target_pairs={{0,1},{1,0},{2,3},{3,2},{4,5},{5,4},{6,7},{7,6},{8,9},{9,8},{10,11... | collective-permute-start | bytes 110600 | tf_op jit(solution)/shard_map/ppermute | solution.py:31
  20.9 4.9 %project.4 = (f32[32,1024]{1,0:T(8,128)S(1)}, bf16[8192,1024]{1,0:T(8,128)(2,1)S(1)}) custom-call(bf16[32,8192]{1,0:T(8,128)(2,1)S(1)} %get-tuple-element.103.normed.refs_0_, bf16[8192,1024]{1,0:T(8,128)(2,1)} %bitcast.13, bf16[8192,1024]{1,0:T(8,128)(2,1)S(1)} %get-tuple-element.104._), custom_call_target="tpu_custom_call", output_to_operand_aliasing={{1}: (2, {})} | custom-call | bytes 16777216 | tf_op jit(solution)/shard_map/project/pallas_call | solution.py:660
  27.6 3.1 %collective-permute-start.15 = (bf16[8,1280]{1,0:T(8,128)(2,1)S(1)}, bf16[8,1280]{1,0:T(8,128)(2,1)S(1)}, u32[]{:S(2)}, u32[]{:S(2)}) collective-permute-start(bf16[8,1280]{1,0:T(8,128)(2,1)S(1)} %get-tuple-element.116), channel_id=1, source_target_pairs={{0,6},{1,7},{2,4},{3,5},{4,2},{5,3},{6,0},{7,1},{8,14},{9,15},{10,... | collective-permute-start | bytes 61448 | tf_op jit(solution)/shard_map/ppermute | solution.py:31
  31.2 5.1 %load.4 = (bf16[8192,1024]{1,0:T(8,128)(2,1)S(1)}, bf16[4,384,512]{2,1,0:T(8,128)(2,1)S(1)}, bf16[4,384,512]{2,1,0:T(8,128)(2,1)S(1)}, f32[64,128]{1,0:T(8,128)S(1)}, f32[64,128]{1,0:T(8,128)S(1)}) custom-call(bf16[8192,1024]{1,0:T(8,128)(2,1)} %bitcast.14, bf16[4,384,1024]{2,1,0:T(8,128)(2,1)} %bitcast.17, bf16[4,384,1024]{2,1,0:T(8,128)(2,1)} %bitcast.19, ...), custom_call_target="tpu_custom_call" | custom-call | bytes 19922944 | tf_op jit(solution)/shard_map/load/pallas_call | solution.py:123
  37.0 3.2 %collective-permute-start.21 = (bf16[64,512]{1,0:T(8,128)(2,1)S(1)}, bf16[64,512]{1,0:T(8,128)(2,1)S(1)}, u32[]{:S(2)}, u32[]{:S(2)}) collective-permute-start(bf16[64,512]{1,0:T(8,128)(2,1)S(1)} %attend.4.after.refs_0_), channel_id=1, source_target_pairs={{0,6},{1,7},{2,4},{3,5},{4,2},{5,3},{6,0},{7,1},{8,14},{9,15},{10,... | collective-permute-start | bytes 196616 | tf_op jit(solution)/shard_map/ppermute | solution.py:31
  40.6 1.8 collective-permute-start.20
  42.4 3.6 %load.5 = (bf16[8192,1024]{1,0:T(8,128)(2,1)S(1)}, f32[8,128]{1,0:T(8,128)S(1)}) custom-call(bf16[8192,1024]{1,0:T(8,128)(2,1)} %bitcast.15, bf16[64,512]{1,0:T(8,128)(2,1)S(1)} %attend.4.after.refs_0_, bf16[8192,1024]{1,0:T(8,128)(2,1)S(1)} %get-tuple-element.129._), custom_call_target="tpu_custom_call", output_to_operand_aliasing={{0}: (2, {})} | custom-call | bytes 8388608 | tf_op jit(solution)/shard_map/load/pallas_call | solution.py:716
  46.0 1.0 collective-permute-start.24
  53.4 2.3 %collective-permute-start.36 = (bf16[16,1152]{1,0:T(8,128)(2,1)S(1)}, bf16[16,1152]{1,0:T(8,128)(2,1)S(1)}, u32[]{:S(2)}, u32[]{:S(2)}) collective-permute-start(bf16[16,1152]{1,0:T(8,128)(2,1)S(1)} %get-tuple-element.140), channel_id=1, source_target_pairs={{0,6},{1,7},{2,4},{3,5},{4,2},{5,3},{6,0},{7,1},{8,14},{9,15},{10,... | collective-permute-start | bytes 110600 | tf_op jit(solution)/shard_map/ppermute | solution.py:31
  55.7 1.3 collective-permute-start.38
  56.9 1.0 collective-permute-start.35
  58.0 1.7 collective-permute-done.37.refs_1_
  59.7 1.5 collective-permute-start.39
  62.6 1.9 collective-permute-start.42
  64.4 1.7 collective-permute-start.44
  67.0 1.3 collective-permute-done.43.refs_3_
  69.4 1.5 collective-permute-start.48
  70.9 1.6 collective-permute-start.50
  72.5 2.4 %collective-permute-start.45 = (bf16[64,512]{1,0:T(8,128)(2,1)S(1)}, bf16[64,512]{1,0:T(8,128)(2,1)S(1)}, u32[]{:S(2)}, u32[]{:S(2)}) collective-permute-start(bf16[64,512]{1,0:T(8,128)(2,1)S(1)} %attend.5.refs_0_), channel_id=1, source_target_pairs={{0,1},{1,0},{2,3},{3,2},{4,5},{5,4},{6,7},{7,6},{8,9},{9,8},{10,11... | collective-permute-start | bytes 196616 | tf_op jit(solution)/shard_map/ppermute | solution.py:31
  74.9 3.2 %collective-permute-start.49 = (bf16[64,512]{1,0:T(8,128)(2,1)S(1)}, bf16[64,512]{1,0:T(8,128)(2,1)S(1)}, u32[]{:S(2)}, u32[]{:S(2)}) collective-permute-start(bf16[64,512]{1,0:T(8,128)(2,1)S(1)} %collective-permute-done.48.refs_4_), channel_id=1, source_target_pairs={{0,1},{1,0},{2,3},{3,2},{4,5},{5,4},{6,7},{7,6},{8,9},{9,8},{10,11... | collective-permute-start | bytes 196616 | tf_op jit(solution)/shard_map/ppermute | solution.py:31
  78.0 1.0 collective-permute-start.51
  84.8 1.7 collective-permute-start.61
  86.7 1.7 collective-permute-start.63
  88.4 1.0 collective-permute-start.60
  89.4 2.1 %collective-permute-done.62.refs_1_ = bf16[16,1152]{1,0:T(8,128)(2,1)S(1)} collective-permute-done((bf16[16,1152]{1,0:T(8,128)(2,1)S(1)}, bf16[16,1152]{1,0:T(8,128)(2,1)S(1)}, u32[]{:S(2)}, u32[]{:S(2)}) %collective-permute-start.62) | collective-permute-done | bytes 36896 | tf_op jit(solution)/shard_map/ppermute | solution.py:31
  93.5 1.7 collective-permute-start.67
  95.6 1.5 collective-permute-start.69
  97.9 1.1 collective-permute-done.68.refs_3_
  99.6 1.0 collective-permute-start.71
  100.6 0.9 collective-permute-start.73
  101.6 1.7 collective-permute-start.75
  103.3 2.3 %collective-permute-start.70 = (bf16[64,512]{1,0:T(8,128)(2,1)S(1)}, bf16[64,512]{1,0:T(8,128)(2,1)S(1)}, u32[]{:S(2)}, u32[]{:S(2)}) collective-permute-start(bf16[64,512]{1,0:T(8,128)(2,1)S(1)} %attend.6.refs_0_), channel_id=1, source_target_pairs={{0,1},{1,0},{2,3},{3,2},{4,5},{5,4},{6,7},{7,6},{8,9},{9,8},{10,11... | collective-permute-start | bytes 196616 | tf_op jit(solution)/shard_map/ppermute | solution.py:31
  105.7 3.2 %collective-permute-start.74 = (bf16[64,512]{1,0:T(8,128)(2,1)S(1)}, bf16[64,512]{1,0:T(8,128)(2,1)S(1)}, u32[]{:S(2)}, u32[]{:S(2)}) collective-permute-start(bf16[64,512]{1,0:T(8,128)(2,1)S(1)} %collective-permute-done.73.refs_4_), channel_id=1, source_target_pairs={{0,1},{1,0},{2,3},{3,2},{4,5},{5,4},{6,7},{7,6},{8,9},{9,8},{10,11... | collective-permute-start | bytes 196616 | tf_op jit(solution)/shard_map/ppermute | solution.py:31
  108.9 1.0 collective-permute-start.76
  110.8 1.3 collective-permute-start.77
  112.1 1.3 collective-permute-start.79
  113.4 1.3 collective-permute-start.81
  114.7 1.3 collective-permute-start.83
  116.0 37.4 %collective-permute-done.77.refs_1_ = bf16[32,1024]{1,0:T(8,128)(2,1)S(1)} collective-permute-done((bf16[32,1024]{1,0:T(8,128)(2,1)S(1)}, bf16[32,1024]{1,0:T(8,128)(2,1)S(1)}, u32[]{:S(2)}, u32[]{:S(2)}) %collective-permute-start.77) | collective-permute-done | bytes 65568 | tf_op jit(solution)/shard_map/ppermute | solution.py:64
  153.4 1.1 collective-permute-start.78
  154.6 3.0 %collective-permute-done.79.refs_3_ = bf16[32,1024]{1,0:T(8,128)(2,1)S(1)} collective-permute-done((bf16[32,1024]{1,0:T(8,128)(2,1)S(1)}, bf16[32,1024]{1,0:T(8,128)(2,1)S(1)}, u32[]{:S(2)}, u32[]{:S(2)}) %collective-permute-start.79) | collective-permute-done | bytes 65568 | tf_op jit(solution)/shard_map/ppermute | solution.py:64
  159.9 1.2 norm.5
  161.1 1.8 collective-permute-start.86
  163.3 1.4 collective-permute-start.88
  164.7 3.4 %project.7.refs_3_.refs_0_ = f32[32,1024]{1,0:T(8,128)S(1)} custom-call(bf16[32,8192]{1,0:T(8,128)(2,1)S(1)} %get-tuple-element.166.refs_0_, bf16[8192,1024]{1,0:T(8,128)(2,1)S(1)} %get-tuple-element.138.refs_1_), custom_call_target="tpu_custom_call" | custom-call | bytes 16777216 | tf_op jit(solution)/shard_map/project/pallas_call | solution.py:90
  168.1 1.2 collective-permute-start.85
  171.7 1.8 collective-permute-start.92
  173.5 1.8 collective-permute-start.94
  176.2 1.1 collective-permute-done.93.refs_3_
  177.3 2.3 %attend.7.refs_0_ = bf16[64,512]{1,0:T(8,128)(2,1)S(1)} custom-call(s32[2,2]{1,0:T(2,128)S(1)} %copy-done.2, s32[2,2]{1,0:T(2,128)S(1)} %collective-permute-done.refs_8_.refs_4_.refs_1_, bf16[8,1280]{1,0:T(8,128)(2,1)S(1)} %collective-permute-done.92.refs_2_, bf16[8,1280]{1,0:T(8,128)(2,1)S(1)} %collective-permute-done.93.refs_3_, ...), custom_call_target="tpu_custom_call" | custom-call | bytes 1048576 | tf_op jit(solution)/shard_map/attend/pallas_call | solution.py:90
  179.6 1.8 collective-permute-start.100
  181.3 1.8 collective-permute-start.98
  183.2 2.2 %collective-permute-start.95 = (bf16[64,512]{1,0:T(8,128)(2,1)S(1)}, bf16[64,512]{1,0:T(8,128)(2,1)S(1)}, u32[]{:S(2)}, u32[]{:S(2)}) collective-permute-start(bf16[64,512]{1,0:T(8,128)(2,1)S(1)} %attend.7.refs_0_), channel_id=1, source_target_pairs={{0,1},{1,0},{2,3},{3,2},{4,5},{5,4},{6,7},{7,6},{8,9},{9,8},{10,11... | collective-permute-start | bytes 196616 | tf_op jit(solution)/shard_map/ppermute | solution.py:31
  185.4 2.3 %collective-permute-start.101 = (bf16[64,512]{1,0:T(8,128)(2,1)S(1)}, bf16[64,512]{1,0:T(8,128)(2,1)S(1)}, u32[]{:S(2)}, u32[]{:S(2)}) collective-permute-start(bf16[64,512]{1,0:T(8,128)(2,1)S(1)} %collective-permute-done.100.refs_6_), channel_id=1, source_target_pairs={{0,1},{1,0},{2,3},{3,2},{4,5},{5,4},{6,7},{7,6},{8,9},{9,8},{10,11... | collective-permute-start | bytes 196616 | tf_op jit(solution)/shard_map/ppermute | solution.py:31
  187.9 1.7 collective-permute-start.99
  190.5 4.1 %leave.7 = (bf16[32,1024]{1,0:T(8,128)(2,1)}, bf16[32,1024]{1,0:T(8,128)(2,1)}, bf16[8,1024]{1,0:T(8,128)(2,1)S(1)}, bf16[8,1024]{1,0:T(8,128)(2,1)S(1)}, bf16[8...) custom-call(bf16[64,512]{1,0:T(8,128)(2,1)S(1)} %attend.7.refs_0_, ...), custom_call_target="tpu_custom_call" | custom-call | bytes 1048576 | tf_op jit(solution)/shard_map/leave/pallas_call | solution.py:90
  196.0 2.1 %collective-permute-start.106 = (bf16[8,1024]{1,0:T(8,128)(2,1)S(1)}, bf16[8,1024]{1,0:T(8,128)(2,1)S(1)}, u32[]{:S(2)}, u32[]{:S(2)}) collective-permute-start(bf16[8,1024]{1,0:T(8,128)(2,1)S(1)} %get-tuple-element.181), channel_id=1, source_target_pairs={{0,2},{1,3},{2,0},{3,1},{4,6},{5,7},{6,4},{7,5},{8,10},{9,11},{10,... | collective-permute-start | bytes 49160 | tf_op jit(solution)/shard_map/ppermute | solution.py:31
  198.1 1.2 collective-permute-start.108
  199.3 1.1 collective-permute-start.103
  (198 shorter events, 39.3 us)
Async XLA Ops:
  1.6 10.6 %collective-permute-start.2 = (bf16[32,1152]{1,0:T(8,128)(2,1)S(1)}, bf16[32,1152]{1,0:T(8,128)(2,1)S(1)}, u32[]{:S(2)}, u32[]{:S(2)}) collective-permute-start(bf16[32,1152]{1,0:T(8,128)(2,1)S(1)} %open.1.refs_8_.refs_0_), channel_id=1, source_target_pairs={{0,6},{1,7},{2,4},{3,5},{4,2},{5,3},{6,0},{7,1},{8,14},{9,15},{10,... | collective-permute-start | bytes 221192 | tf_op jit(solution)/shard_map/ppermute | solution.py:31
  4.9 7.3 %collective-permute-start.3 = (bf16[32,1152]{1,0:T(8,128)(2,1)S(1)}, bf16[32,1152]{1,0:T(8,128)(2,1)S(1)}, u32[]{:S(2)}, u32[]{:S(2)}) collective-permute-start(bf16[32,1152]{1,0:T(8,128)(2,1)S(1)} %open.1.refs_8_.refs_0_), channel_id=1, source_target_pairs={{0,4},{1,5},{2,6},{3,7},{4,0},{5,1},{6,2},{7,3},{8,12},{9,13},{10,... | collective-permute-start | bytes 221192 | tf_op jit(solution)/shard_map/ppermute | solution.py:31
  4.9 7.3 %collective-permute-start.4 = (bf16[32,1152]{1,0:T(8,128)(2,1)S(1)}, bf16[32,1152]{1,0:T(8,128)(2,1)S(1)}, u32[]{:S(2)}, u32[]{:S(2)}) collective-permute-start(bf16[32,1152]{1,0:T(8,128)(2,1)S(1)} %open.1.refs_8_.refs_0_), channel_id=1, source_target_pairs={{0,2},{1,3},{2,0},{3,1},{4,6},{5,7},{6,4},{7,5},{8,10},{9,11},{10,... | collective-permute-start | bytes 221192 | tf_op jit(solution)/shard_map/ppermute | solution.py:31
  5.3 8.8 %collective-permute-start.1 = (bf16[32,1152]{1,0:T(8,128)(2,1)S(1)}, bf16[32,1152]{1,0:T(8,128)(2,1)S(1)}, u32[]{:S(2)}, u32[]{:S(2)}) collective-permute-start(bf16[32,1152]{1,0:T(8,128)(2,1)S(1)} %open.1.refs_8_.refs_0_), channel_id=1, source_target_pairs={{0,1},{1,0},{2,3},{3,2},{4,5},{5,4},{6,7},{7,6},{8,9},{9,8},{10,11... | collective-permute-start | bytes 221192 | tf_op jit(solution)/shard_map/ppermute | solution.py:31
  14.5 21.8 %collective-permute-start.18 = (bf16[4,384,512]{2,1,0:T(8,128)(2,1)S(1)}, bf16[4,384,512]{2,1,0:T(8,128)(2,1)S(1)}, u32[]{:S(2)}, u32[]{:S(2)}) collective-permute-start(bf16[4,384,512]{2,1,0:T(8,128)(2,1)S(1)} %get-tuple-element.127), channel_id=1, source_target_pairs={{0,1},{1,0},{2,3},{3,2},{4,5},{5,4},{6,7},{7,6},{8,9},{9,8},{10,11... | collective-permute-start | bytes 4718600 | tf_op jit(solution)/shard_map/ppermute | solution.py:31
  14.9 21.4 %collective-permute-start.19 = (bf16[4,384,512]{2,1,0:T(8,128)(2,1)S(1)}, bf16[4,384,512]{2,1,0:T(8,128)(2,1)S(1)}, u32[]{:S(2)}, u32[]{:S(2)}) collective-permute-start(bf16[4,384,512]{2,1,0:T(8,128)(2,1)S(1)} %get-tuple-element.128), channel_id=1, source_target_pairs={{0,1},{1,0},{2,3},{3,2},{4,5},{5,4},{6,7},{7,6},{8,9},{9,8},{10,11... | collective-permute-start | bytes 4718600 | tf_op jit(solution)/shard_map/ppermute | solution.py:31
  15.1 3.7 %collective-permute-start.10 = (bf16[16,1152]{1,0:T(8,128)(2,1)S(1)}, bf16[16,1152]{1,0:T(8,128)(2,1)S(1)}, u32[]{:S(2)}, u32[]{:S(2)}) collective-permute-start(bf16[16,1152]{1,0:T(8,128)(2,1)S(1)} %get-tuple-element.111), channel_id=1, source_target_pairs={{0,4},{1,5},{2,6},{3,7},{4,0},{5,1},{6,2},{7,3},{8,12},{9,13},{10,... | collective-permute-start | bytes 110600 | tf_op jit(solution)/shard_map/ppermute | solution.py:31
  17.0 8.8 %collective-permute-start.11 = (bf16[16,1152]{1,0:T(8,128)(2,1)S(1)}, bf16[16,1152]{1,0:T(8,128)(2,1)S(1)}, u32[]{:S(2)}, u32[]{:S(2)}) collective-permute-start(bf16[16,1152]{1,0:T(8,128)(2,1)S(1)} %get-tuple-element.112), channel_id=1, source_target_pairs={{0,2},{1,3},{2,0},{3,1},{4,6},{5,7},{6,4},{7,5},{8,10},{9,11},{10,... | collective-permute-start | bytes 110600 | tf_op jit(solution)/shard_map/ppermute | solution.py:31
  18.7 7.1 %collective-permute-start.9 = (bf16[16,1152]{1,0:T(8,128)(2,1)S(1)}, bf16[16,1152]{1,0:T(8,128)(2,1)S(1)}, u32[]{:S(2)}, u32[]{:S(2)}) collective-permute-start(bf16[16,1152]{1,0:T(8,128)(2,1)S(1)} %get-tuple-element.110), channel_id=1, source_target_pairs={{0,6},{1,7},{2,4},{3,5},{4,2},{5,3},{6,0},{7,1},{8,14},{9,15},{10,... | collective-permute-start | bytes 110600 | tf_op jit(solution)/shard_map/ppermute | solution.py:31
  18.8 7.6 %collective-permute-start.8 = (bf16[16,1152]{1,0:T(8,128)(2,1)S(1)}, bf16[16,1152]{1,0:T(8,128)(2,1)S(1)}, u32[]{:S(2)}, u32[]{:S(2)}) collective-permute-start(bf16[16,1152]{1,0:T(8,128)(2,1)S(1)} %get-tuple-element.109.refs_3_), channel_id=1, source_target_pairs={{0,1},{1,0},{2,3},{3,2},{4,5},{5,4},{6,7},{7,6},{8,9},{9,8},{10,11... | collective-permute-start | bytes 110600 | tf_op jit(solution)/shard_map/ppermute | solution.py:31
  27.6 8.7 %collective-permute-start.15 = (bf16[8,1280]{1,0:T(8,128)(2,1)S(1)}, bf16[8,1280]{1,0:T(8,128)(2,1)S(1)}, u32[]{:S(2)}, u32[]{:S(2)}) collective-permute-start(bf16[8,1280]{1,0:T(8,128)(2,1)S(1)} %get-tuple-element.116), channel_id=1, source_target_pairs={{0,6},{1,7},{2,4},{3,5},{4,2},{5,3},{6,0},{7,1},{8,14},{9,15},{10,... | collective-permute-start | bytes 61448 | tf_op jit(solution)/shard_map/ppermute | solution.py:31
  30.7 5.6 %collective-permute-start.16 = (bf16[8,1280]{1,0:T(8,128)(2,1)S(1)}, bf16[8,1280]{1,0:T(8,128)(2,1)S(1)}, u32[]{:S(2)}, u32[]{:S(2)}) collective-permute-start(bf16[8,1280]{1,0:T(8,128)(2,1)S(1)} %get-tuple-element.117), channel_id=1, source_target_pairs={{0,4},{1,5},{2,6},{3,7},{4,0},{5,1},{6,2},{7,3},{8,12},{9,13},{10,... | collective-permute-start | bytes 61448 | tf_op jit(solution)/shard_map/ppermute | solution.py:31
  30.7 5.6 %collective-permute-start.17 = (bf16[8,1280]{1,0:T(8,128)(2,1)S(1)}, bf16[8,1280]{1,0:T(8,128)(2,1)S(1)}, u32[]{:S(2)}, u32[]{:S(2)}) collective-permute-start(bf16[8,1280]{1,0:T(8,128)(2,1)S(1)} %get-tuple-element.118), channel_id=1, source_target_pairs={{0,2},{1,3},{2,0},{3,1},{4,6},{5,7},{6,4},{7,5},{8,10},{9,11},{10,... | collective-permute-start | bytes 61448 | tf_op jit(solution)/shard_map/ppermute | solution.py:31
  37.0 9.0 %collective-permute-start.21 = (bf16[64,512]{1,0:T(8,128)(2,1)S(1)}, bf16[64,512]{1,0:T(8,128)(2,1)S(1)}, u32[]{:S(2)}, u32[]{:S(2)}) collective-permute-start(bf16[64,512]{1,0:T(8,128)(2,1)S(1)} %attend.4.after.refs_0_), channel_id=1, source_target_pairs={{0,6},{1,7},{2,4},{3,5},{4,2},{5,3},{6,0},{7,1},{8,14},{9,15},{10,... | collective-permute-start | bytes 196616 | tf_op jit(solution)/shard_map/ppermute | solution.py:31
  40.1 5.9 %collective-permute-start.22 = (bf16[64,512]{1,0:T(8,128)(2,1)S(1)}, bf16[64,512]{1,0:T(8,128)(2,1)S(1)}, u32[]{:S(2)}, u32[]{:S(2)}) collective-permute-start(bf16[64,512]{1,0:T(8,128)(2,1)S(1)} %attend.4.after.refs_0_), channel_id=1, source_target_pairs={{0,4},{1,5},{2,6},{3,7},{4,0},{5,1},{6,2},{7,3},{8,12},{9,13},{10,... | collective-permute-start | bytes 196616 | tf_op jit(solution)/shard_map/ppermute | solution.py:31
  40.1 5.9 %collective-permute-start.23 = (bf16[64,512]{1,0:T(8,128)(2,1)S(1)}, bf16[64,512]{1,0:T(8,128)(2,1)S(1)}, u32[]{:S(2)}, u32[]{:S(2)}) collective-permute-start(bf16[64,512]{1,0:T(8,128)(2,1)S(1)} %attend.4.after.refs_0_), channel_id=1, source_target_pairs={{0,2},{1,3},{2,0},{3,1},{4,6},{5,7},{6,4},{7,5},{8,10},{9,11},{10,... | collective-permute-start | bytes 196616 | tf_op jit(solution)/shard_map/ppermute | solution.py:31
  40.6 7.0 %collective-permute-start.20 = (bf16[64,512]{1,0:T(8,128)(2,1)S(1)}, bf16[64,512]{1,0:T(8,128)(2,1)S(1)}, u32[]{:S(2)}, u32[]{:S(2)}) collective-permute-start(bf16[64,512]{1,0:T(8,128)(2,1)S(1)} %attend.4.after.refs_0_), channel_id=1, source_target_pairs={{0,1},{1,0},{2,3},{3,2},{4,5},{5,4},{6,7},{7,6},{8,9},{9,8},{10,11... | collective-permute-start | bytes 196616 | tf_op jit(solution)/shard_map/ppermute | solution.py:31
  48.5 2.7 %collective-permute-start.27 = (bf16[32,1024]{1,0:T(8,128)(2,1)S(1)}, bf16[32,1024]{1,0:T(8,128)(2,1)S(1)}, u32[]{:S(2)}, u32[]{:S(2)}) collective-permute-start(bf16[32,1024]{1,0:T(8,128)(2,1)S(1)} %get-tuple-element.136), channel_id=1, source_target_pairs={{0,14},{1,15},{2,12},{3,13},{4,10},{5,11},{6,8},{7,9}} | collective-permute-start | bytes 196616 | tf_op jit(solution)/shard_map/ppermute | solution.py:64
  53.4 4.6 %collective-permute-start.36 = (bf16[16,1152]{1,0:T(8,128)(2,1)S(1)}, bf16[16,1152]{1,0:T(8,128)(2,1)S(1)}, u32[]{:S(2)}, u32[]{:S(2)}) collective-permute-start(bf16[16,1152]{1,0:T(8,128)(2,1)S(1)} %get-tuple-element.140), channel_id=1, source_target_pairs={{0,6},{1,7},{2,4},{3,5},{4,2},{5,3},{6,0},{7,1},{8,14},{9,15},{10,... | collective-permute-start | bytes 110600 | tf_op jit(solution)/shard_map/ppermute | solution.py:31
  55.7 4.0 %collective-permute-start.37 = (bf16[16,1152]{1,0:T(8,128)(2,1)S(1)}, bf16[16,1152]{1,0:T(8,128)(2,1)S(1)}, u32[]{:S(2)}, u32[]{:S(2)}) collective-permute-start(bf16[16,1152]{1,0:T(8,128)(2,1)S(1)} %get-tuple-element.141), channel_id=1, source_target_pairs={{0,4},{1,5},{2,6},{3,7},{4,0},{5,1},{6,2},{7,3},{8,12},{9,13},{10,... | collective-permute-start | bytes 110600 | tf_op jit(solution)/shard_map/ppermute | solution.py:31
  55.7 4.0 %collective-permute-start.38 = (bf16[16,1152]{1,0:T(8,128)(2,1)S(1)}, bf16[16,1152]{1,0:T(8,128)(2,1)S(1)}, u32[]{:S(2)}, u32[]{:S(2)}) collective-permute-start(bf16[16,1152]{1,0:T(8,128)(2,1)S(1)} %get-tuple-element.142), channel_id=1, source_target_pairs={{0,2},{1,3},{2,0},{3,1},{4,6},{5,7},{6,4},{7,5},{8,10},{9,11},{10,... | collective-permute-start | bytes 110600 | tf_op jit(solution)/shard_map/ppermute | solution.py:31
  56.9 4.7 %collective-permute-start.35 = (bf16[16,1152]{1,0:T(8,128)(2,1)S(1)}, bf16[16,1152]{1,0:T(8,128)(2,1)S(1)}, u32[]{:S(2)}, u32[]{:S(2)}) collective-permute-start(bf16[16,1152]{1,0:T(8,128)(2,1)S(1)} %get-tuple-element.139.refs_3_), channel_id=1, source_target_pairs={{0,1},{1,0},{2,3},{3,2},{4,5},{5,4},{6,7},{7,6},{8,9},{9,8},{10,11... | collective-permute-start | bytes 110600 | tf_op jit(solution)/shard_map/ppermute | solution.py:31
  62.6 4.4 %collective-permute-start.42 = (bf16[8,1280]{1,0:T(8,128)(2,1)S(1)}, bf16[8,1280]{1,0:T(8,128)(2,1)S(1)}, u32[]{:S(2)}, u32[]{:S(2)}) collective-permute-start(bf16[8,1280]{1,0:T(8,128)(2,1)S(1)} %get-tuple-element.146), channel_id=1, source_target_pairs={{0,6},{1,7},{2,4},{3,5},{4,2},{5,3},{6,0},{7,1},{8,14},{9,15},{10,... | collective-permute-start | bytes 61448 | tf_op jit(solution)/shard_map/ppermute | solution.py:31
  64.4 3.9 %collective-permute-start.43 = (bf16[8,1280]{1,0:T(8,128)(2,1)S(1)}, bf16[8,1280]{1,0:T(8,128)(2,1)S(1)}, u32[]{:S(2)}, u32[]{:S(2)}) collective-permute-start(bf16[8,1280]{1,0:T(8,128)(2,1)S(1)} %get-tuple-element.147), channel_id=1, source_target_pairs={{0,4},{1,5},{2,6},{3,7},{4,0},{5,1},{6,2},{7,3},{8,12},{9,13},{10,... | collective-permute-start | bytes 61448 | tf_op jit(solution)/shard_map/ppermute | solution.py:31
  64.4 3.9 %collective-permute-start.44 = (bf16[8,1280]{1,0:T(8,128)(2,1)S(1)}, bf16[8,1280]{1,0:T(8,128)(2,1)S(1)}, u32[]{:S(2)}, u32[]{:S(2)}) collective-permute-start(bf16[8,1280]{1,0:T(8,128)(2,1)S(1)} %get-tuple-element.148), channel_id=1, source_target_pairs={{0,2},{1,3},{2,0},{3,1},{4,6},{5,7},{6,4},{7,5},{8,10},{9,11},{10,... | collective-permute-start | bytes 61448 | tf_op jit(solution)/shard_map/ppermute | solution.py:31
  68.9 6.0 %collective-permute-start.46 = (bf16[64,512]{1,0:T(8,128)(2,1)S(1)}, bf16[64,512]{1,0:T(8,128)(2,1)S(1)}, u32[]{:S(2)}, u32[]{:S(2)}) collective-permute-start(bf16[64,512]{1,0:T(8,128)(2,1)S(1)} %attend.5.refs_0_), channel_id=1, source_target_pairs={{0,2},{1,3},{2,0},{3,1},{4,6},{5,7},{6,4},{7,5},{8,10},{9,11},{10,... | collective-permute-start | bytes 196616 | tf_op jit(solution)/shard_map/ppermute | solution.py:31
  69.4 5.5 %collective-permute-start.48 = (bf16[64,512]{1,0:T(8,128)(2,1)S(1)}, bf16[64,512]{1,0:T(8,128)(2,1)S(1)}, u32[]{:S(2)}, u32[]{:S(2)}) collective-permute-start(bf16[64,512]{1,0:T(8,128)(2,1)S(1)} %attend.5.refs_0_), channel_id=1, source_target_pairs={{0,4},{1,5},{2,6},{3,7},{4,0},{5,1},{6,2},{7,3},{8,12},{9,13},{10,... | collective-permute-start | bytes 196616 | tf_op jit(solution)/shard_map/ppermute | solution.py:31
  70.9 7.2 %collective-permute-start.50 = (bf16[64,512]{1,0:T(8,128)(2,1)S(1)}, bf16[64,512]{1,0:T(8,128)(2,1)S(1)}, u32[]{:S(2)}, u32[]{:S(2)}) collective-permute-start(bf16[64,512]{1,0:T(8,128)(2,1)S(1)} %attend.5.refs_0_), channel_id=1, source_target_pairs={{0,6},{1,7},{2,4},{3,5},{4,2},{5,3},{6,0},{7,1},{8,14},{9,15},{10,... | collective-permute-start | bytes 196616 | tf_op jit(solution)/shard_map/ppermute | solution.py:31
  72.5 6.5 %collective-permute-start.45 = (bf16[64,512]{1,0:T(8,128)(2,1)S(1)}, bf16[64,512]{1,0:T(8,128)(2,1)S(1)}, u32[]{:S(2)}, u32[]{:S(2)}) collective-permute-start(bf16[64,512]{1,0:T(8,128)(2,1)S(1)} %attend.5.refs_0_), channel_id=1, source_target_pairs={{0,1},{1,0},{2,3},{3,2},{4,5},{5,4},{6,7},{7,6},{8,9},{9,8},{10,11... | collective-permute-start | bytes 196616 | tf_op jit(solution)/shard_map/ppermute | solution.py:31
  74.9 4.2 %collective-permute-start.47 = (bf16[64,512]{1,0:T(8,128)(2,1)S(1)}, bf16[64,512]{1,0:T(8,128)(2,1)S(1)}, u32[]{:S(2)}, u32[]{:S(2)}) collective-permute-start(bf16[64,512]{1,0:T(8,128)(2,1)S(1)} %collective-permute-done.46.refs_2_), channel_id=1, source_target_pairs={{0,1},{1,0},{2,3},{3,2},{4,5},{5,4},{6,7},{7,6},{8,9},{9,8},{10,11... | collective-permute-start | bytes 196616 | tf_op jit(solution)/shard_map/ppermute | solution.py:31
  74.9 4.1 %collective-permute-start.49 = (bf16[64,512]{1,0:T(8,128)(2,1)S(1)}, bf16[64,512]{1,0:T(8,128)(2,1)S(1)}, u32[]{:S(2)}, u32[]{:S(2)}) collective-permute-start(bf16[64,512]{1,0:T(8,128)(2,1)S(1)} %collective-permute-done.48.refs_4_), channel_id=1, source_target_pairs={{0,1},{1,0},{2,3},{3,2},{4,5},{5,4},{6,7},{7,6},{8,9},{9,8},{10,11... | collective-permute-start | bytes 196616 | tf_op jit(solution)/shard_map/ppermute | solution.py:31
  84.8 4.6 %collective-permute-start.61 = (bf16[16,1152]{1,0:T(8,128)(2,1)S(1)}, bf16[16,1152]{1,0:T(8,128)(2,1)S(1)}, u32[]{:S(2)}, u32[]{:S(2)}) collective-permute-start(bf16[16,1152]{1,0:T(8,128)(2,1)S(1)} %get-tuple-element.154), channel_id=1, source_target_pairs={{0,6},{1,7},{2,4},{3,5},{4,2},{5,3},{6,0},{7,1},{8,14},{9,15},{10,... | collective-permute-start | bytes 110600 | tf_op jit(solution)/shard_map/ppermute | solution.py:31
  86.6 5.0 %collective-permute-start.62 = (bf16[16,1152]{1,0:T(8,128)(2,1)S(1)}, bf16[16,1152]{1,0:T(8,128)(2,1)S(1)}, u32[]{:S(2)}, u32[]{:S(2)}) collective-permute-start(bf16[16,1152]{1,0:T(8,128)(2,1)S(1)} %get-tuple-element.155), channel_id=1, source_target_pairs={{0,4},{1,5},{2,6},{3,7},{4,0},{5,1},{6,2},{7,3},{8,12},{9,13},{10,... | collective-permute-start | bytes 110600 | tf_op jit(solution)/shard_map/ppermute | solution.py:31
  86.7 4.8 %collective-permute-start.63 = (bf16[16,1152]{1,0:T(8,128)(2,1)S(1)}, bf16[16,1152]{1,0:T(8,128)(2,1)S(1)}, u32[]{:S(2)}, u32[]{:S(2)}) collective-permute-start(bf16[16,1152]{1,0:T(8,128)(2,1)S(1)} %get-tuple-element.156), channel_id=1, source_target_pairs={{0,2},{1,3},{2,0},{3,1},{4,6},{5,7},{6,4},{7,5},{8,10},{9,11},{10,... | collective-permute-start | bytes 110600 | tf_op jit(solution)/shard_map/ppermute | solution.py:31
  88.4 4.3 %collective-permute-start.60 = (bf16[16,1152]{1,0:T(8,128)(2,1)S(1)}, bf16[16,1152]{1,0:T(8,128)(2,1)S(1)}, u32[]{:S(2)}, u32[]{:S(2)}) collective-permute-start(bf16[16,1152]{1,0:T(8,128)(2,1)S(1)} %get-tuple-element.153.refs_3_), channel_id=1, source_target_pairs={{0,1},{1,0},{2,3},{3,2},{4,5},{5,4},{6,7},{7,6},{8,9},{9,8},{10,11... | collective-permute-start | bytes 110600 | tf_op jit(solution)/shard_map/ppermute | solution.py:31
  93.5 4.4 %collective-permute-start.67 = (bf16[8,1280]{1,0:T(8,128)(2,1)S(1)}, bf16[8,1280]{1,0:T(8,128)(2,1)S(1)}, u32[]{:S(2)}, u32[]{:S(2)}) collective-permute-start(bf16[8,1280]{1,0:T(8,128)(2,1)S(1)} %get-tuple-element.160), channel_id=1, source_target_pairs={{0,6},{1,7},{2,4},{3,5},{4,2},{5,3},{6,0},{7,1},{8,14},{9,15},{10,... | collective-permute-start | bytes 61448 | tf_op jit(solution)/shard_map/ppermute | solution.py:31
  95.2 3.8 %collective-permute-start.68 = (bf16[8,1280]{1,0:T(8,128)(2,1)S(1)}, bf16[8,1280]{1,0:T(8,128)(2,1)S(1)}, u32[]{:S(2)}, u32[]{:S(2)}) collective-permute-start(bf16[8,1280]{1,0:T(8,128)(2,1)S(1)} %get-tuple-element.161), channel_id=1, source_target_pairs={{0,4},{1,5},{2,6},{3,7},{4,0},{5,1},{6,2},{7,3},{8,12},{9,13},{10,... | collective-permute-start | bytes 61448 | tf_op jit(solution)/shard_map/ppermute | solution.py:31
  95.6 3.5 %collective-permute-start.69 = (bf16[8,1280]{1,0:T(8,128)(2,1)S(1)}, bf16[8,1280]{1,0:T(8,128)(2,1)S(1)}, u32[]{:S(2)}, u32[]{:S(2)}) collective-permute-start(bf16[8,1280]{1,0:T(8,128)(2,1)S(1)} %get-tuple-element.162), channel_id=1, source_target_pairs={{0,2},{1,3},{2,0},{3,1},{4,6},{5,7},{6,4},{7,5},{8,10},{9,11},{10,... | collective-permute-start | bytes 61448 | tf_op jit(solution)/shard_map/ppermute | solution.py:31
  99.6 5.9 %collective-permute-start.71 = (bf16[64,512]{1,0:T(8,128)(2,1)S(1)}, bf16[64,512]{1,0:T(8,128)(2,1)S(1)}, u32[]{:S(2)}, u32[]{:S(2)}) collective-permute-start(bf16[64,512]{1,0:T(8,128)(2,1)S(1)} %attend.6.refs_0_), channel_id=1, source_target_pairs={{0,2},{1,3},{2,0},{3,1},{4,6},{5,7},{6,4},{7,5},{8,10},{9,11},{10,... | collective-permute-start | bytes 196616 | tf_op jit(solution)/shard_map/ppermute | solution.py:31
  100.6 5.1 %collective-permute-start.73 = (bf16[64,512]{1,0:T(8,128)(2,1)S(1)}, bf16[64,512]{1,0:T(8,128)(2,1)S(1)}, u32[]{:S(2)}, u32[]{:S(2)}) collective-permute-start(bf16[64,512]{1,0:T(8,128)(2,1)S(1)} %attend.6.refs_0_), channel_id=1, source_target_pairs={{0,4},{1,5},{2,6},{3,7},{4,0},{5,1},{6,2},{7,3},{8,12},{9,13},{10,... | collective-permute-start | bytes 196616 | tf_op jit(solution)/shard_map/ppermute | solution.py:31
  101.6 7.4 %collective-permute-start.75 = (bf16[64,512]{1,0:T(8,128)(2,1)S(1)}, bf16[64,512]{1,0:T(8,128)(2,1)S(1)}, u32[]{:S(2)}, u32[]{:S(2)}) collective-permute-start(bf16[64,512]{1,0:T(8,128)(2,1)S(1)} %attend.6.refs_0_), channel_id=1, source_target_pairs={{0,6},{1,7},{2,4},{3,5},{4,2},{5,3},{6,0},{7,1},{8,14},{9,15},{10,... | collective-permute-start | bytes 196616 | tf_op jit(solution)/shard_map/ppermute | solution.py:31
  103.3 6.7 %collective-permute-start.70 = (bf16[64,512]{1,0:T(8,128)(2,1)S(1)}, bf16[64,512]{1,0:T(8,128)(2,1)S(1)}, u32[]{:S(2)}, u32[]{:S(2)}) collective-permute-start(bf16[64,512]{1,0:T(8,128)(2,1)S(1)} %attend.6.refs_0_), channel_id=1, source_target_pairs={{0,1},{1,0},{2,3},{3,2},{4,5},{5,4},{6,7},{7,6},{8,9},{9,8},{10,11... | collective-permute-start | bytes 196616 | tf_op jit(solution)/shard_map/ppermute | solution.py:31
  105.6 4.4 %collective-permute-start.72 = (bf16[64,512]{1,0:T(8,128)(2,1)S(1)}, bf16[64,512]{1,0:T(8,128)(2,1)S(1)}, u32[]{:S(2)}, u32[]{:S(2)}) collective-permute-start(bf16[64,512]{1,0:T(8,128)(2,1)S(1)} %collective-permute-done.71.refs_2_), channel_id=1, source_target_pairs={{0,1},{1,0},{2,3},{3,2},{4,5},{5,4},{6,7},{7,6},{8,9},{9,8},{10,11... | collective-permute-start | bytes 196616 | tf_op jit(solution)/shard_map/ppermute | solution.py:31
  105.7 4.2 %collective-permute-start.74 = (bf16[64,512]{1,0:T(8,128)(2,1)S(1)}, bf16[64,512]{1,0:T(8,128)(2,1)S(1)}, u32[]{:S(2)}, u32[]{:S(2)}) collective-permute-start(bf16[64,512]{1,0:T(8,128)(2,1)S(1)} %collective-permute-done.73.refs_4_), channel_id=1, source_target_pairs={{0,1},{1,0},{2,3},{3,2},{4,5},{5,4},{6,7},{7,6},{8,9},{9,8},{10,11... | collective-permute-start | bytes 196616 | tf_op jit(solution)/shard_map/ppermute | solution.py:31
  110.8 42.6 %collective-permute-start.77 = (bf16[32,1024]{1,0:T(8,128)(2,1)S(1)}, bf16[32,1024]{1,0:T(8,128)(2,1)S(1)}, u32[]{:S(2)}, u32[]{:S(2)}) collective-permute-start(bf16[32,1024]{1,0:T(8,128)(2,1)S(1)} %get-tuple-element.165), channel_id=1, source_target_pairs={{16,30},{17,31},{18,28},{19,29},{20,26},{21,27},{22,24},{23,25}} | collective-permute-start | bytes 196616 | tf_op jit(solution)/shard_map/ppermute | solution.py:64
  112.1 45.5 %collective-permute-start.79 = (bf16[32,1024]{1,0:T(8,128)(2,1)S(1)}, bf16[32,1024]{1,0:T(8,128)(2,1)S(1)}, u32[]{:S(2)}, u32[]{:S(2)}) collective-permute-start(bf16[32,1024]{1,0:T(8,128)(2,1)S(1)} %get-tuple-element.165), channel_id=1, source_target_pairs={{16,28},{17,29},{18,30},{19,31},{20,24},{21,25},{22,26},{23,27}} | collective-permute-start | bytes 196616 | tf_op jit(solution)/shard_map/ppermute | solution.py:64
  113.4 45.0 %collective-permute-start.81 = (bf16[32,1024]{1,0:T(8,128)(2,1)S(1)}, bf16[32,1024]{1,0:T(8,128)(2,1)S(1)}, u32[]{:S(2)}, u32[]{:S(2)}) collective-permute-start(bf16[32,1024]{1,0:T(8,128)(2,1)S(1)} %get-tuple-element.165), channel_id=1, source_target_pairs={{16,26},{17,27},{18,24},{19,25},{20,30},{21,31},{22,28},{23,29}} | collective-permute-start | bytes 196616 | tf_op jit(solution)/shard_map/ppermute | solution.py:64
  114.7 43.8 %collective-permute-start.83 = (bf16[32,1024]{1,0:T(8,128)(2,1)S(1)}, bf16[32,1024]{1,0:T(8,128)(2,1)S(1)}, u32[]{:S(2)}, u32[]{:S(2)}) collective-permute-start(bf16[32,1024]{1,0:T(8,128)(2,1)S(1)} %get-tuple-element.165), channel_id=1, source_target_pairs={{16,24},{17,25},{18,26},{19,27},{20,28},{21,29},{22,30},{23,31}} | collective-permute-start | bytes 196616 | tf_op jit(solution)/shard_map/ppermute | solution.py:64
  153.4 5.5 %collective-permute-start.78 = (bf16[32,1024]{1,0:T(8,128)(2,1)S(1)}, bf16[32,1024]{1,0:T(8,128)(2,1)S(1)}, u32[]{:S(2)}, u32[]{:S(2)}) collective-permute-start(bf16[32,1024]{1,0:T(8,128)(2,1)S(1)} %collective-permute-done.77.refs_1_), channel_id=1, source_target_pairs={{0,1},{1,0},{2,3},{3,2},{4,5},{5,4},{6,7},{7,6},{8,9},{9,8},{10,11... | collective-permute-start | bytes 196616 | tf_op jit(solution)/shard_map/ppermute | solution.py:31
  161.1 8.3 %collective-permute-start.86 = (bf16[16,1152]{1,0:T(8,128)(2,1)S(1)}, bf16[16,1152]{1,0:T(8,128)(2,1)S(1)}, u32[]{:S(2)}, u32[]{:S(2)}) collective-permute-start(bf16[16,1152]{1,0:T(8,128)(2,1)S(1)} %get-tuple-element.168), channel_id=1, source_target_pairs={{0,6},{1,7},{2,4},{3,5},{4,2},{5,3},{6,0},{7,1},{8,14},{9,15},{10,... | collective-permute-start | bytes 110600 | tf_op jit(solution)/shard_map/ppermute | solution.py:31
  162.9 6.5 %collective-permute-start.87 = (bf16[16,1152]{1,0:T(8,128)(2,1)S(1)}, bf16[16,1152]{1,0:T(8,128)(2,1)S(1)}, u32[]{:S(2)}, u32[]{:S(2)}) collective-permute-start(bf16[16,1152]{1,0:T(8,128)(2,1)S(1)} %get-tuple-element.169), channel_id=1, source_target_pairs={{0,4},{1,5},{2,6},{3,7},{4,0},{5,1},{6,2},{7,3},{8,12},{9,13},{10,... | collective-permute-start | bytes 110600 | tf_op jit(solution)/shard_map/ppermute | solution.py:31
  163.3 6.1 %collective-permute-start.88 = (bf16[16,1152]{1,0:T(8,128)(2,1)S(1)}, bf16[16,1152]{1,0:T(8,128)(2,1)S(1)}, u32[]{:S(2)}, u32[]{:S(2)}) collective-permute-start(bf16[16,1152]{1,0:T(8,128)(2,1)S(1)} %get-tuple-element.170), channel_id=1, source_target_pairs={{0,2},{1,3},{2,0},{3,1},{4,6},{5,7},{6,4},{7,5},{8,10},{9,11},{10,... | collective-permute-start | bytes 110600 | tf_op jit(solution)/shard_map/ppermute | solution.py:31
  171.7 4.5 %collective-permute-start.92 = (bf16[8,1280]{1,0:T(8,128)(2,1)S(1)}, bf16[8,1280]{1,0:T(8,128)(2,1)S(1)}, u32[]{:S(2)}, u32[]{:S(2)}) collective-permute-start(bf16[8,1280]{1,0:T(8,128)(2,1)S(1)} %get-tuple-element.174), channel_id=1, source_target_pairs={{0,6},{1,7},{2,4},{3,5},{4,2},{5,3},{6,0},{7,1},{8,14},{9,15},{10,... | collective-permute-start | bytes 61448 | tf_op jit(solution)/shard_map/ppermute | solution.py:31
  173.5 3.8 %collective-permute-start.93 = (bf16[8,1280]{1,0:T(8,128)(2,1)S(1)}, bf16[8,1280]{1,0:T(8,128)(2,1)S(1)}, u32[]{:S(2)}, u32[]{:S(2)}) collective-permute-start(bf16[8,1280]{1,0:T(8,128)(2,1)S(1)} %get-tuple-element.175), channel_id=1, source_target_pairs={{0,4},{1,5},{2,6},{3,7},{4,0},{5,1},{6,2},{7,3},{8,12},{9,13},{10,... | collective-permute-start | bytes 61448 | tf_op jit(solution)/shard_map/ppermute | solution.py:31
  173.5 3.8 %collective-permute-start.94 = (bf16[8,1280]{1,0:T(8,128)(2,1)S(1)}, bf16[8,1280]{1,0:T(8,128)(2,1)S(1)}, u32[]{:S(2)}, u32[]{:S(2)}) collective-permute-start(bf16[8,1280]{1,0:T(8,128)(2,1)S(1)} %get-tuple-element.176), channel_id=1, source_target_pairs={{0,2},{1,3},{2,0},{3,1},{4,6},{5,7},{6,4},{7,5},{8,10},{9,11},{10,... | collective-permute-start | bytes 61448 | tf_op jit(solution)/shard_map/ppermute | solution.py:31
  179.6 5.8 %collective-permute-start.100 = (bf16[64,512]{1,0:T(8,128)(2,1)S(1)}, bf16[64,512]{1,0:T(8,128)(2,1)S(1)}, u32[]{:S(2)}, u32[]{:S(2)}) collective-permute-start(bf16[64,512]{1,0:T(8,128)(2,1)S(1)} %attend.7.refs_0_), channel_id=1, source_target_pairs={{0,6},{1,7},{2,4},{3,5},{4,2},{5,3},{6,0},{7,1},{8,14},{9,15},{10,... | collective-permute-start | bytes 196616 | tf_op jit(solution)/shard_map/ppermute | solution.py:31
  181.3 6.3 %collective-permute-start.96 = (bf16[64,512]{1,0:T(8,128)(2,1)S(1)}, bf16[64,512]{1,0:T(8,128)(2,1)S(1)}, u32[]{:S(2)}, u32[]{:S(2)}) collective-permute-start(bf16[64,512]{1,0:T(8,128)(2,1)S(1)} %attend.7.refs_0_), channel_id=1, source_target_pairs={{0,2},{1,3},{2,0},{3,1},{4,6},{5,7},{6,4},{7,5},{8,10},{9,11},{10,... | collective-permute-start | bytes 196616 | tf_op jit(solution)/shard_map/ppermute | solution.py:31
  181.3 6.5 %collective-permute-start.98 = (bf16[64,512]{1,0:T(8,128)(2,1)S(1)}, bf16[64,512]{1,0:T(8,128)(2,1)S(1)}, u32[]{:S(2)}, u32[]{:S(2)}) collective-permute-start(bf16[64,512]{1,0:T(8,128)(2,1)S(1)} %attend.7.refs_0_), channel_id=1, source_target_pairs={{0,4},{1,5},{2,6},{3,7},{4,0},{5,1},{6,2},{7,3},{8,12},{9,13},{10,... | collective-permute-start | bytes 196616 | tf_op jit(solution)/shard_map/ppermute | solution.py:31
  183.2 6.4 %collective-permute-start.95 = (bf16[64,512]{1,0:T(8,128)(2,1)S(1)}, bf16[64,512]{1,0:T(8,128)(2,1)S(1)}, u32[]{:S(2)}, u32[]{:S(2)}) collective-permute-start(bf16[64,512]{1,0:T(8,128)(2,1)S(1)} %attend.7.refs_0_), channel_id=1, source_target_pairs={{0,1},{1,0},{2,3},{3,2},{4,5},{5,4},{6,7},{7,6},{8,9},{9,8},{10,11... | collective-permute-start | bytes 196616 | tf_op jit(solution)/shard_map/ppermute | solution.py:31
  185.4 4.2 %collective-permute-start.101 = (bf16[64,512]{1,0:T(8,128)(2,1)S(1)}, bf16[64,512]{1,0:T(8,128)(2,1)S(1)}, u32[]{:S(2)}, u32[]{:S(2)}) collective-permute-start(bf16[64,512]{1,0:T(8,128)(2,1)S(1)} %collective-permute-done.100.refs_6_), channel_id=1, source_target_pairs={{0,1},{1,0},{2,3},{3,2},{4,5},{5,4},{6,7},{7,6},{8,9},{9,8},{10,11... | collective-permute-start | bytes 196616 | tf_op jit(solution)/shard_map/ppermute | solution.py:31
  194.6 4.7 %collective-permute-start.102 = (bf16[8,1024]{1,0:T(8,128)(2,1)S(1)}, bf16[8,1024]{1,0:T(8,128)(2,1)S(1)}, u32[]{:S(2)}, u32[]{:S(2)}) collective-permute-start(bf16[8,1024]{1,0:T(8,128)(2,1)S(1)} %get-tuple-element.179), channel_id=1, source_target_pairs={{0,6},{1,7},{2,4},{3,5},{4,2},{5,3},{6,0},{7,1},{8,14},{9,15},{10,... | collective-permute-start | bytes 49160 | tf_op jit(solution)/shard_map/ppermute | solution.py:31
  195.5 5.0 %collective-permute-start.104 = (bf16[8,1024]{1,0:T(8,128)(2,1)S(1)}, bf16[8,1024]{1,0:T(8,128)(2,1)S(1)}, u32[]{:S(2)}, u32[]{:S(2)}) collective-permute-start(bf16[8,1024]{1,0:T(8,128)(2,1)S(1)} %get-tuple-element.180), channel_id=1, source_target_pairs={{0,4},{1,5},{2,6},{3,7},{4,0},{5,1},{6,2},{7,3},{8,12},{9,13},{10,... | collective-permute-start | bytes 49160 | tf_op jit(solution)/shard_map/ppermute | solution.py:31
  196.0 4.8 %collective-permute-start.106 = (bf16[8,1024]{1,0:T(8,128)(2,1)S(1)}, bf16[8,1024]{1,0:T(8,128)(2,1)S(1)}, u32[]{:S(2)}, u32[]{:S(2)}) collective-permute-start(bf16[8,1024]{1,0:T(8,128)(2,1)S(1)} %get-tuple-element.181), channel_id=1, source_target_pairs={{0,2},{1,3},{2,0},{3,1},{4,6},{5,7},{6,4},{7,5},{8,10},{9,11},{10,... | collective-permute-start | bytes 49160 | tf_op jit(solution)/shard_map/ppermute | solution.py:31
  198.1 2.9 %collective-permute-start.108 = (bf16[8,1024]{1,0:T(8,128)(2,1)S(1)}, bf16[8,1024]{1,0:T(8,128)(2,1)S(1)}, u32[]{:S(2)}, u32[]{:S(2)}) collective-permute-start(bf16[8,1024]{1,0:T(8,128)(2,1)S(1)} %get-tuple-element.182.refs_7_), channel_id=1, source_target_pairs={{0,1},{1,0},{2,3},{3,2},{4,5},{5,4},{6,7},{7,6},{8,9},{9,8},{10,11... | collective-permute-start | bytes 49160 | tf_op jit(solution)/shard_map/ppermute | solution.py:31
  (49 other events, 91.3 us)
where the time goes:
time: 203 us
  starting transfers between devices  104 us (51%)
  waiting for transfers between devices  62.5 us (31%)
  Pallas kernels  34.9 us (17%)
    ppermute x97, starting transfers between devices, swapped(): return lax.ppermute(value, 'wide', [(i, i ^ bits) for i in range(count)])  93.5 us
    ppermute x12, waiting for transfers between devices, shifted(): return lax.ppermute(value, ('segment', 'wide'), pairs)  40.6 us
    ppermute x97, waiting for transfers between devices, swapped(): return lax.ppermute(value, 'wide', [(i, i ^ bits) for i in range(count)])  21.9 us
    pallas_call x25, Pallas kernels, call(): pl.pallas_call(inner, out_shape=outs + [pltpu.VMEM(array.shape, array.dty...  15.7 us
    pallas_call x2, Pallas kernels, loaded(): pl.pallas_call(functools.partial(load_kernel, (len(sources), len(small),...  10.6 us
    ppermute x12, starting transfers between devices, shifted(): return lax.ppermute(value, ('segment', 'wide'), pairs)  10.5 us
    pallas_call x1, Pallas kernels, project_first(): pl.pallas_call(functools.partial(project_first_kernel, query_first, tick)...  4.92 us
  transfers between devices with their start and end apart: 109, of which 45 were waited for; matrix products, arithmetic and copies ran while one was open for 0% of the time, Pallas kernels for 11%

commit v1 on v0

--- a/solution.py
+++ b/solution.py
@@ -22,6 +22,11 @@
 GROUP = HEADS // KVH
 MIB = 1 << 20
 STEP = 256
+HOP_ORDER = (2, 3, 1, 0)
+WORK_ORDER = (1, 0, 2)
+HEAD_ORDER = (2, 3, 1, 0)
+ROW_ORDER = (0, 2, 1, 3)
+LAST_ORDER = (3, 2, 1, 0)
 VMEM = pl.BlockSpec(memory_space=pltpu.VMEM)
 SMEM = pl.BlockSpec(memory_space=pltpu.SMEM)
 
@@ -35,7 +40,7 @@
     if work is None:
         return arrays, None
     done = work()
-    arrays = arrays[::-1]
+    arrays = [arrays[k] for k in WORK_ORDER]
     arrays = pl.pallas_call(
         lambda *refs: None,
         out_shape=[jax.ShapeDtypeStruct(array.shape, array.dtype) for array in arrays],
@@ -45,7 +50,7 @@
         compiler_params=pltpu.CompilerParams(vmem_limit_bytes=MIB),
         name="then",
     )(*arrays, done)
-    return arrays[::-1], done
+    return [arrays[WORK_ORDER.index(k)] for k in range(len(WORK_ORDER))], done
 
 
 def gathered(value, work=None):
@@ -295,7 +300,9 @@
 
 
 def norm_kernel(count, capacity, *refs):
-    chunks, rest = refs[:count][::-1], refs[count:]
+    chunks, rest = [None] * count, refs[count:]
+    for i, j in enumerate([2 * p + c for p in HOP_ORDER for c in (1, 0)]):
+        chunks[j] = refs[i]
     ident, gain, *adapters, normed = rest[:6]
     correction = rest[6:]
     owner = lax.axis_index("wide")
@@ -391,7 +398,7 @@
 
 
 def attend_kernel(chips, lengths, near_lengths, *refs):
-    arrived, rest = refs[:chips][::-1], refs[chips:]
+    arrived, rest = [refs[HEAD_ORDER.index(k)] for k in range(chips)], refs[chips:]
     cosine, sine, keys, values, near_keys, near_values, out, scores, weights = rest
     chip = lax.axis_index("wide") // 2
     own_rows, span = keys.shape[:2]
@@ -506,7 +513,9 @@
 
 
 def leave_kernel(count, own_rows, tick, *refs):
-    chunks, rest = refs[:count], refs[count:]
+    chunks, rest = [None] * count, refs[count:]
+    for i, j in enumerate([2 * p + c for p in ROW_ORDER for c in (0, 1)]):
+        chunks[j] = refs[i]
     held, result = rest[0], rest[1] if tick else None
     matrix, out, kept, *outs, rows_ref = rest[2 if tick else 1 :]
     kept[...] = result[...] if tick else jnp.zeros_like(kept)
@@ -527,7 +536,9 @@
 
 
 def join_kernel(count, *refs):
-    blocks, out = refs[:count][::-1], refs[count]
+    blocks, out = [None] * count, refs[count]
+    for i, j in enumerate([2 * p + c for p in LAST_ORDER for c in (1, 0)]):
+        blocks[j] = refs[i]
     for j, block in enumerate(blocks):
         rows = block.shape[0] // 2
         half = block[(j % 2) * rows : (j % 2 + 1) * rows, :]
@@ -640,7 +651,8 @@
             normed, *found = call(
                 while_live(tick, functools.partial(norm_kernel, count, capacity)),
                 [normed_shape] + correction_shapes,
-                [(c, VMEM) for c in chunks[::-1]] + [(ident, VMEM), (gain, VMEM)],
+                [(chunks[2 * p + c], VMEM) for p in HOP_ORDER for c in (1, 0)]
+                + [(ident, VMEM), (gain, VMEM)],
                 kept=adapters,
                 name="norm",
             )
@@ -737,7 +749,7 @@
             while_live(tick, functools.partial(attend_kernel, chips)),
             [jax.ShapeDtypeStruct((GROUP * 2 * own_rows, head_lanes), jnp.bfloat16)],
             [(lengths, SMEM), (near_lengths, SMEM)]
-            + [(a, VMEM) for a in [*arrived[::-1], *angles]],
+            + [(a, VMEM) for a in [*[arrived[k] for k in HEAD_ORDER], *angles]],
             [
                 pltpu.VMEM((chips * GROUP * 2 * own_rows, span), jnp.float32),
                 pltpu.VMEM((chips * GROUP * 2 * own_rows, span), jnp.bfloat16),
@@ -750,7 +762,7 @@
         held, result, *found = call(
             functools.partial(leave_kernel, count, own_rows, tick),
             [held_shape, held_shape] + (blocks_of(own_rows, part) if last else []),
-            [(c, VMEM) for c in chunks]
+            [(chunks[2 * p + c], VMEM) for p in ROW_ORDER for c in (0, 1)]
             + [(held, VMEM)] + ([(result, VMEM)] if tick else []),
             [pltpu.VMEM((rows, width), jnp.bfloat16)],
             kept=output_parts,
@@ -762,7 +774,7 @@
     (joined,) = call(
         functools.partial(join_kernel, count),
         [jax.ShapeDtypeStruct((1, micro, local_rows, width), jnp.bfloat16)],
-        [(one, VMEM) for one in far[::-1]],
+        [(far[2 * p + c], VMEM) for p in LAST_ORDER for c in (1, 0)],
         name="join",
     )
     return joined

time: 203 us -> 198 us (0.975)
  waiting for transfers between devices: 62.5 us -> 59.3 us
    ppermute x12, waiting for transfers between devices: 40.6 us -> 35.5 us  [shifted(): return lax.ppermute(value, ('segment', 'wide'), pairs)]
    ppermute x97, starting transfers between devices: 93.5 us -> 91.3 us  [swapped(): return lax.ppermute(value, 'wide', [(i, i ^ bits) for i in range(count)])]
  transfers between devices with their start and end apart: 109 -> 109, of which waited for: 45 -> 45; matrix products, arithmetic and copies ran while one was open for 0% -> 0% of each run, Pallas kernels for 11% -> 12%
where the time goes in v1:
time: 198 us; the launch traced here: 197 us
  starting transfers between devices  102 us (52%)
  waiting for transfers between devices  59.3 us (30%)
  Pallas kernels  34.9 us (18%)
    ppermute x97, starting transfers between devices, swapped(): return lax.ppermute(value, 'wide', [(i, i ^ bits) for i in range(count)])  91.3 us
    ppermute x12, waiting for transfers between devices, shifted(): return lax.ppermute(value, ('segment', 'wide'), pairs)  35.5 us
    ppermute x97, waiting for transfers between devices, swapped(): return lax.ppermute(value, 'wide', [(i, i ^ bits) for i in range(count)])  23.8 us
    pallas_call x25, Pallas kernels, call(): pl.pallas_call(inner, out_shape=outs + [pltpu.VMEM(array.shape, array.dty...  15.8 us
    pallas_call x2, Pallas kernels, loaded(): pl.pallas_call(functools.partial(load_kernel, (len(sources), len(small),...  10.6 us
    ppermute x12, starting transfers between devices, shifted(): return lax.ppermute(value, ('segment', 'wide'), pairs)  10.4 us
    pallas_call x1, Pallas kernels, project_first(): pl.pallas_call(functools.partial(project_first_kernel, query_first, tick)...  4.92 us
  transfers between devices with their start and end apart: 109, of which 45 were waited for; matrix products, arithmetic and copies ran while one was open for 0% of the time, Pallas kernels for 12%

profile of v1, /device:TPU:7, one launch (start us, length us, event | category | flops | bytes accessed | tf_op | source)
XLA Modules:
  0.0 197.4 jit_solution(17955133294772825295)
XLA Ops:
  1.6 2.4 %collective-permute-start.2 = (bf16[32,1152]{1,0:T(8,128)(2,1)S(1)}, bf16[32,1152]{1,0:T(8,128)(2,1)S(1)}, u32[]{:S(2)}, u32[]{:S(2)}) collective-permute-start(bf16[32,1152]{1,0:T(8,128)(2,1)S(1)} %open.1.refs_8_.refs_0_), channel_id=1, source_target_pairs={{0,4},{1,5},{2,6},{3,7},{4,0},{5,1},{6,2},{7,3},{8,12},{9,13},{10,... | collective-permute-start | bytes 221192 | tf_op jit(solution)/shard_map/ppermute | solution.py:36
  3.9 1.3 collective-permute-start.3
  5.2 1.5 collective-permute-start.1
  6.7 5.5 %load.3 = (bf16[1,8192,128]{2,1,0:T(8,128)(2,1)S(1)}, bf16[1,64,8192]{2,1,0:T(8,128)(2,1)S(1)}, bf16[1,64,1024]{2,1,0:T(8,128)(2,1)S(1)}, bf16[8192,128]{1,0:T(8...) custom-call(bf16[1,8192,128]{2,1,0:T(8,128)(2,1)} %bitcast.20, ...), custom_call_target="tpu_custom_call" | custom-call | bytes 27394048 | tf_op jit(solution)/shard_map/load/pallas_call | solution.py:128
  13.3 0.9 collective-permute-done.refs_8_.refs_4_.refs_1_
  15.5 2.9 %collective-permute-start.11 = (bf16[16,1152]{1,0:T(8,128)(2,1)S(1)}, bf16[16,1152]{1,0:T(8,128)(2,1)S(1)}, u32[]{:S(2)}, u32[]{:S(2)}) collective-permute-start(bf16[16,1152]{1,0:T(8,128)(2,1)S(1)} %get-tuple-element.112), channel_id=1, source_target_pairs={{0,6},{1,7},{2,4},{3,5},{4,2},{5,3},{6,0},{7,1},{8,14},{9,15},{10,... | collective-permute-start | bytes 110600 | tf_op jit(solution)/shard_map/ppermute | solution.py:36
  19.6 4.9 %project.4 = (f32[32,1024]{1,0:T(8,128)S(1)}, bf16[8192,1024]{1,0:T(8,128)(2,1)S(1)}) custom-call(bf16[32,8192]{1,0:T(8,128)(2,1)S(1)} %get-tuple-element.103.normed.refs_0_, bf16[8192,1024]{1,0:T(8,128)(2,1)} %bitcast.13, bf16[8192,1024]{1,0:T(8,128)(2,1)S(1)} %get-tuple-element.104._), custom_call_target="tpu_custom_call", output_to_operand_aliasing={{1}: (2, {})} | custom-call | bytes 16777216 | tf_op jit(solution)/shard_map/project/pallas_call | solution.py:672
  26.4 2.1 %collective-permute-start.15 = (bf16[8,1280]{1,0:T(8,128)(2,1)S(1)}, bf16[8,1280]{1,0:T(8,128)(2,1)S(1)}, u32[]{:S(2)}, u32[]{:S(2)}) collective-permute-start(bf16[8,1280]{1,0:T(8,128)(2,1)S(1)} %get-tuple-element.116), channel_id=1, source_target_pairs={{0,4},{1,5},{2,6},{3,7},{4,0},{5,1},{6,2},{7,3},{8,12},{9,13},{10,... | collective-permute-start | bytes 61448 | tf_op jit(solution)/shard_map/ppermute | solution.py:36
  28.4 1.3 collective-permute-start.16
  29.9 5.1 %load.4 = (bf16[8192,1024]{1,0:T(8,128)(2,1)S(1)}, bf16[4,384,512]{2,1,0:T(8,128)(2,1)S(1)}, bf16[4,384,512]{2,1,0:T(8,128)(2,1)S(1)}, f32[64,128]{1,0:T(8,128)S(1)}, f32[64,128]{1,0:T(8,128)S(1)}) custom-call(bf16[8192,1024]{1,0:T(8,128)(2,1)} %bitcast.14, bf16[4,384,1024]{2,1,0:T(8,128)(2,1)} %bitcast.17, bf16[4,384,1024]{2,1,0:T(8,128)(2,1)} %bitcast.19, ...), custom_call_target="tpu_custom_call" | custom-call | bytes 19922944 | tf_op jit(solution)/shard_map/load/pallas_call | solution.py:128
  35.7 1.2 collective-permute-start.21
  37.0 2.2 %collective-permute-start.22 = (bf16[64,512]{1,0:T(8,128)(2,1)S(1)}, bf16[64,512]{1,0:T(8,128)(2,1)S(1)}, u32[]{:S(2)}, u32[]{:S(2)}) collective-permute-start(bf16[64,512]{1,0:T(8,128)(2,1)S(1)} %attend.4.after.refs_0_), channel_id=1, source_target_pairs={{0,2},{1,3},{2,0},{3,1},{4,6},{5,7},{6,4},{7,5},{8,10},{9,11},{10,... | collective-permute-start | bytes 196616 | tf_op jit(solution)/shard_map/ppermute | solution.py:36
  39.3 1.8 collective-permute-start.20
  41.2 3.6 %load.5 = (bf16[8192,1024]{1,0:T(8,128)(2,1)S(1)}, f32[8,128]{1,0:T(8,128)S(1)}) custom-call(bf16[8192,1024]{1,0:T(8,128)(2,1)} %bitcast.15, bf16[64,512]{1,0:T(8,128)(2,1)S(1)} %attend.4.after.refs_0_, bf16[8192,1024]{1,0:T(8,128)(2,1)S(1)} %get-tuple-element.129._), custom_call_target="tpu_custom_call", output_to_operand_aliasing={{0}: (2, {})} | custom-call | bytes 8388608 | tf_op jit(solution)/shard_map/load/pallas_call | solution.py:728
  44.8 2.0 %collective-permute-start.24 = (bf16[64,512]{1,0:T(8,128)(2,1)S(1)}, bf16[64,512]{1,0:T(8,128)(2,1)S(1)}, u32[]{:S(2)}, u32[]{:S(2)}) collective-permute-start(bf16[64,512]{1,0:T(8,128)(2,1)S(1)} %get-tuple-element.131.refs_2_), channel_id=1, source_target_pairs={{0,1},{1,0},{2,3},{3,2},{4,5},{5,4},{6,7},{7,6},{8,9},{9,8},{10,11... | collective-permute-start | bytes 196616 | tf_op jit(solution)/shard_map/ppermute | solution.py:36
  53.2 1.5 collective-permute-start.37
  54.7 1.9 collective-permute-start.38
  56.6 1.0 collective-permute-start.35
  57.6 1.7 collective-permute-done.38.refs_2_
  59.3 2.1 %collective-permute-start.39 = (bf16[16,1152]{1,0:T(8,128)(2,1)S(1)}, bf16[16,1152]{1,0:T(8,128)(2,1)S(1)}, u32[]{:S(2)}, u32[]{:S(2)}) collective-permute-start(bf16[16,1152]{1,0:T(8,128)(2,1)S(1)} %get-tuple-element.143.refs_5_), channel_id=1, source_target_pairs={{0,1},{1,0},{2,3},{3,2},{4,5},{5,4},{6,7},{7,6},{8,9},{9,8},{10,11... | collective-permute-start | bytes 110600 | tf_op jit(solution)/shard_map/ppermute | solution.py:36
  62.8 1.7 collective-permute-start.43
  65.4 1.0 collective-permute-done.42.refs_2_
  70.0 2.1 %collective-permute-start.50 = (bf16[64,512]{1,0:T(8,128)(2,1)S(1)}, bf16[64,512]{1,0:T(8,128)(2,1)S(1)}, u32[]{:S(2)}, u32[]{:S(2)}) collective-permute-start(bf16[64,512]{1,0:T(8,128)(2,1)S(1)} %attend.5.refs_0_), channel_id=1, source_target_pairs={{0,6},{1,7},{2,4},{3,5},{4,2},{5,3},{6,0},{7,1},{8,14},{9,15},{10,... | collective-permute-start | bytes 196616 | tf_op jit(solution)/shard_map/ppermute | solution.py:36
  72.0 1.9 collective-permute-start.45
  73.9 2.7 %collective-permute-start.47 = (bf16[64,512]{1,0:T(8,128)(2,1)S(1)}, bf16[64,512]{1,0:T(8,128)(2,1)S(1)}, u32[]{:S(2)}, u32[]{:S(2)}) collective-permute-start(bf16[64,512]{1,0:T(8,128)(2,1)S(1)} %collective-permute-done.46.refs_2_), channel_id=1, source_target_pairs={{0,1},{1,0},{2,3},{3,2},{4,5},{5,4},{6,7},{7,6},{8,9},{9,8},{10,11... | collective-permute-start | bytes 196616 | tf_op jit(solution)/shard_map/ppermute | solution.py:36
  76.7 1.5 collective-permute-start.51
  84.0 1.8 collective-permute-start.62
  85.8 1.7 collective-permute-start.63
  87.5 1.0 collective-permute-start.60
  88.6 1.9 collective-permute-done.63.refs_2_
  90.4 1.9 collective-permute-start.64
  93.7 1.7 collective-permute-start.68
  96.3 1.0 collective-permute-done.67.refs_2_
  100.9 2.1 %collective-permute-start.75 = (bf16[64,512]{1,0:T(8,128)(2,1)S(1)}, bf16[64,512]{1,0:T(8,128)(2,1)S(1)}, u32[]{:S(2)}, u32[]{:S(2)}) collective-permute-start(bf16[64,512]{1,0:T(8,128)(2,1)S(1)} %attend.6.refs_0_), channel_id=1, source_target_pairs={{0,6},{1,7},{2,4},{3,5},{4,2},{5,3},{6,0},{7,1},{8,14},{9,15},{10,... | collective-permute-start | bytes 196616 | tf_op jit(solution)/shard_map/ppermute | solution.py:36
  102.9 1.9 collective-permute-start.70
  104.9 2.7 %collective-permute-start.72 = (bf16[64,512]{1,0:T(8,128)(2,1)S(1)}, bf16[64,512]{1,0:T(8,128)(2,1)S(1)}, u32[]{:S(2)}, u32[]{:S(2)}) collective-permute-start(bf16[64,512]{1,0:T(8,128)(2,1)S(1)} %collective-permute-done.71.refs_2_), channel_id=1, source_target_pairs={{0,1},{1,0},{2,3},{3,2},{4,5},{5,4},{6,7},{7,6},{8,9},{9,8},{10,11... | collective-permute-start | bytes 196616 | tf_op jit(solution)/shard_map/ppermute | solution.py:36
  107.6 1.5 collective-permute-start.76
  110.0 1.3 collective-permute-start.77
  111.3 1.3 collective-permute-start.79
  112.6 1.3 collective-permute-start.81
  113.9 1.3 collective-permute-start.83
  115.2 32.1 %collective-permute-done.77.refs_1_ = bf16[32,1024]{1,0:T(8,128)(2,1)S(1)} collective-permute-done((bf16[32,1024]{1,0:T(8,128)(2,1)S(1)}, bf16[32,1024]{1,0:T(8,128)(2,1)S(1)}, u32[]{:S(2)}, u32[]{:S(2)}) %collective-permute-start.77) | collective-permute-done | bytes 65568 | tf_op jit(solution)/shard_map/ppermute | solution.py:69
  147.3 1.0 collective-permute-start.78
  148.3 2.8 %collective-permute-done.79.refs_3_ = bf16[32,1024]{1,0:T(8,128)(2,1)S(1)} collective-permute-done((bf16[32,1024]{1,0:T(8,128)(2,1)S(1)}, bf16[32,1024]{1,0:T(8,128)(2,1)S(1)}, u32[]{:S(2)}, u32[]{:S(2)}) %collective-permute-start.79) | collective-permute-done | bytes 65568 | tf_op jit(solution)/shard_map/ppermute | solution.py:69
  151.1 1.0 collective-permute-start.80
  154.2 1.2 norm.5
  155.4 1.3 collective-permute-start.86
  157.4 1.7 collective-permute-start.88
  159.1 3.4 %project.7.refs_3_.refs_0_ = f32[32,1024]{1,0:T(8,128)S(1)} custom-call(bf16[32,8192]{1,0:T(8,128)(2,1)S(1)} %get-tuple-element.166.refs_0_, bf16[8192,1024]{1,0:T(8,128)(2,1)S(1)} %get-tuple-element.138.refs_1_), custom_call_target="tpu_custom_call" | custom-call | bytes 16777216 | tf_op jit(solution)/shard_map/project/pallas_call | solution.py:95
  162.5 1.2 collective-permute-start.85
  166.5 1.6 collective-permute-start.93
  169.7 1.3 collective-permute-done.93.refs_3_
  171.3 2.3 %attend.7.refs_0_ = bf16[64,512]{1,0:T(8,128)(2,1)S(1)} custom-call(s32[2,2]{1,0:T(2,128)S(1)} %copy-done.2, s32[2,2]{1,0:T(2,128)S(1)} %collective-permute-done.refs_8_.refs_4_.refs_1_, bf16[8,1280]{1,0:T(8,128)(2,1)S(1)} %collective-permute-done.92.refs_2_, bf16[8,1280]{1,0:T(8,128)(2,1)S(1)} %collective-permute-done.93.refs_3_, ...), custom_call_target="tpu_custom_call" | custom-call | bytes 1048576 | tf_op jit(solution)/shard_map/attend/pallas_call | solution.py:95
  173.6 1.7 collective-permute-start.100
  175.3 1.9 collective-permute-start.98
  177.2 2.3 %collective-permute-start.95 = (bf16[64,512]{1,0:T(8,128)(2,1)S(1)}, bf16[64,512]{1,0:T(8,128)(2,1)S(1)}, u32[]{:S(2)}, u32[]{:S(2)}) collective-permute-start(bf16[64,512]{1,0:T(8,128)(2,1)S(1)} %attend.7.refs_0_), channel_id=1, source_target_pairs={{0,1},{1,0},{2,3},{3,2},{4,5},{5,4},{6,7},{7,6},{8,9},{9,8},{10,11... | collective-permute-start | bytes 196616 | tf_op jit(solution)/shard_map/ppermute | solution.py:36
  179.4 2.3 %collective-permute-start.101 = (bf16[64,512]{1,0:T(8,128)(2,1)S(1)}, bf16[64,512]{1,0:T(8,128)(2,1)S(1)}, u32[]{:S(2)}, u32[]{:S(2)}) collective-permute-start(bf16[64,512]{1,0:T(8,128)(2,1)S(1)} %collective-permute-done.100.refs_6_), channel_id=1, source_target_pairs={{0,1},{1,0},{2,3},{3,2},{4,5},{5,4},{6,7},{7,6},{8,9},{9,8},{10,11... | collective-permute-start | bytes 196616 | tf_op jit(solution)/shard_map/ppermute | solution.py:36
  182.4 1.1 collective-permute-start.97
  184.7 4.1 %leave.7 = (bf16[32,1024]{1,0:T(8,128)(2,1)}, bf16[32,1024]{1,0:T(8,128)(2,1)}, bf16[8,1024]{1,0:T(8,128)(2,1)S(1)}, bf16[8,1024]{1,0:T(8,128)(2,1)S(1)}, bf16[8...) custom-call(bf16[64,512]{1,0:T(8,128)(2,1)S(1)} %attend.7.refs_0_, ...), custom_call_target="tpu_custom_call" | custom-call | bytes 1048576 | tf_op jit(solution)/shard_map/leave/pallas_call | solution.py:95
  188.8 1.7 collective-permute-start.102
  190.5 1.9 collective-permute-start.106
  192.4 1.0 collective-permute-start.108
  193.4 1.1 collective-permute-start.103
  194.5 1.0 collective-permute-start.105
  (198 shorter events, 43.4 us)
Async XLA Ops:
  1.6 10.6 %collective-permute-start.2 = (bf16[32,1152]{1,0:T(8,128)(2,1)S(1)}, bf16[32,1152]{1,0:T(8,128)(2,1)S(1)}, u32[]{:S(2)}, u32[]{:S(2)}) collective-permute-start(bf16[32,1152]{1,0:T(8,128)(2,1)S(1)} %open.1.refs_8_.refs_0_), channel_id=1, source_target_pairs={{0,4},{1,5},{2,6},{3,7},{4,0},{5,1},{6,2},{7,3},{8,12},{9,13},{10,... | collective-permute-start | bytes 221192 | tf_op jit(solution)/shard_map/ppermute | solution.py:36
  3.9 8.3 %collective-permute-start.3 = (bf16[32,1152]{1,0:T(8,128)(2,1)S(1)}, bf16[32,1152]{1,0:T(8,128)(2,1)S(1)}, u32[]{:S(2)}, u32[]{:S(2)}) collective-permute-start(bf16[32,1152]{1,0:T(8,128)(2,1)S(1)} %open.1.refs_8_.refs_0_), channel_id=1, source_target_pairs={{0,2},{1,3},{2,0},{3,1},{4,6},{5,7},{6,4},{7,5},{8,10},{9,11},{10,... | collective-permute-start | bytes 221192 | tf_op jit(solution)/shard_map/ppermute | solution.py:36
  5.2 7.0 %collective-permute-start.4 = (bf16[32,1152]{1,0:T(8,128)(2,1)S(1)}, bf16[32,1152]{1,0:T(8,128)(2,1)S(1)}, u32[]{:S(2)}, u32[]{:S(2)}) collective-permute-start(bf16[32,1152]{1,0:T(8,128)(2,1)S(1)} %open.1.refs_8_.refs_0_), channel_id=1, source_target_pairs={{0,6},{1,7},{2,4},{3,5},{4,2},{5,3},{6,0},{7,1},{8,14},{9,15},{10,... | collective-permute-start | bytes 221192 | tf_op jit(solution)/shard_map/ppermute | solution.py:36
  5.2 9.0 %collective-permute-start.1 = (bf16[32,1152]{1,0:T(8,128)(2,1)S(1)}, bf16[32,1152]{1,0:T(8,128)(2,1)S(1)}, u32[]{:S(2)}, u32[]{:S(2)}) collective-permute-start(bf16[32,1152]{1,0:T(8,128)(2,1)S(1)} %open.1.refs_8_.refs_0_), channel_id=1, source_target_pairs={{0,1},{1,0},{2,3},{3,2},{4,5},{5,4},{6,7},{7,6},{8,9},{9,8},{10,11... | collective-permute-start | bytes 221192 | tf_op jit(solution)/shard_map/ppermute | solution.py:36
  14.7 20.4 %collective-permute-start.18 = (bf16[4,384,512]{2,1,0:T(8,128)(2,1)S(1)}, bf16[4,384,512]{2,1,0:T(8,128)(2,1)S(1)}, u32[]{:S(2)}, u32[]{:S(2)}) collective-permute-start(bf16[4,384,512]{2,1,0:T(8,128)(2,1)S(1)} %get-tuple-element.127), channel_id=1, source_target_pairs={{0,1},{1,0},{2,3},{3,2},{4,5},{5,4},{6,7},{7,6},{8,9},{9,8},{10,11... | collective-permute-start | bytes 4718600 | tf_op jit(solution)/shard_map/ppermute | solution.py:36
  14.9 20.2 %collective-permute-start.19 = (bf16[4,384,512]{2,1,0:T(8,128)(2,1)S(1)}, bf16[4,384,512]{2,1,0:T(8,128)(2,1)S(1)}, u32[]{:S(2)}, u32[]{:S(2)}) collective-permute-start(bf16[4,384,512]{2,1,0:T(8,128)(2,1)S(1)} %get-tuple-element.128), channel_id=1, source_target_pairs={{0,1},{1,0},{2,3},{3,2},{4,5},{5,4},{6,7},{7,6},{8,9},{9,8},{10,11... | collective-permute-start | bytes 4718600 | tf_op jit(solution)/shard_map/ppermute | solution.py:36
  15.2 3.5 %collective-permute-start.10 = (bf16[16,1152]{1,0:T(8,128)(2,1)S(1)}, bf16[16,1152]{1,0:T(8,128)(2,1)S(1)}, u32[]{:S(2)}, u32[]{:S(2)}) collective-permute-start(bf16[16,1152]{1,0:T(8,128)(2,1)S(1)} %get-tuple-element.111), channel_id=1, source_target_pairs={{0,2},{1,3},{2,0},{3,1},{4,6},{5,7},{6,4},{7,5},{8,10},{9,11},{10,... | collective-permute-start | bytes 110600 | tf_op jit(solution)/shard_map/ppermute | solution.py:36
  15.5 9.0 %collective-permute-start.11 = (bf16[16,1152]{1,0:T(8,128)(2,1)S(1)}, bf16[16,1152]{1,0:T(8,128)(2,1)S(1)}, u32[]{:S(2)}, u32[]{:S(2)}) collective-permute-start(bf16[16,1152]{1,0:T(8,128)(2,1)S(1)} %get-tuple-element.112), channel_id=1, source_target_pairs={{0,6},{1,7},{2,4},{3,5},{4,2},{5,3},{6,0},{7,1},{8,14},{9,15},{10,... | collective-permute-start | bytes 110600 | tf_op jit(solution)/shard_map/ppermute | solution.py:36
  18.4 6.1 %collective-permute-start.9 = (bf16[16,1152]{1,0:T(8,128)(2,1)S(1)}, bf16[16,1152]{1,0:T(8,128)(2,1)S(1)}, u32[]{:S(2)}, u32[]{:S(2)}) collective-permute-start(bf16[16,1152]{1,0:T(8,128)(2,1)S(1)} %get-tuple-element.110), channel_id=1, source_target_pairs={{0,4},{1,5},{2,6},{3,7},{4,0},{5,1},{6,2},{7,3},{8,12},{9,13},{10,... | collective-permute-start | bytes 110600 | tf_op jit(solution)/shard_map/ppermute | solution.py:36
  18.7 6.4 %collective-permute-start.8 = (bf16[16,1152]{1,0:T(8,128)(2,1)S(1)}, bf16[16,1152]{1,0:T(8,128)(2,1)S(1)}, u32[]{:S(2)}, u32[]{:S(2)}) collective-permute-start(bf16[16,1152]{1,0:T(8,128)(2,1)S(1)} %get-tuple-element.109.refs_3_), channel_id=1, source_target_pairs={{0,1},{1,0},{2,3},{3,2},{4,5},{5,4},{6,7},{7,6},{8,9},{9,8},{10,11... | collective-permute-start | bytes 110600 | tf_op jit(solution)/shard_map/ppermute | solution.py:36
  26.4 8.7 %collective-permute-start.15 = (bf16[8,1280]{1,0:T(8,128)(2,1)S(1)}, bf16[8,1280]{1,0:T(8,128)(2,1)S(1)}, u32[]{:S(2)}, u32[]{:S(2)}) collective-permute-start(bf16[8,1280]{1,0:T(8,128)(2,1)S(1)} %get-tuple-element.116), channel_id=1, source_target_pairs={{0,4},{1,5},{2,6},{3,7},{4,0},{5,1},{6,2},{7,3},{8,12},{9,13},{10,... | collective-permute-start | bytes 61448 | tf_op jit(solution)/shard_map/ppermute | solution.py:36
  28.4 6.6 %collective-permute-start.16 = (bf16[8,1280]{1,0:T(8,128)(2,1)S(1)}, bf16[8,1280]{1,0:T(8,128)(2,1)S(1)}, u32[]{:S(2)}, u32[]{:S(2)}) collective-permute-start(bf16[8,1280]{1,0:T(8,128)(2,1)S(1)} %get-tuple-element.117), channel_id=1, source_target_pairs={{0,2},{1,3},{2,0},{3,1},{4,6},{5,7},{6,4},{7,5},{8,10},{9,11},{10,... | collective-permute-start | bytes 61448 | tf_op jit(solution)/shard_map/ppermute | solution.py:36
  29.8 5.3 %collective-permute-start.17 = (bf16[8,1280]{1,0:T(8,128)(2,1)S(1)}, bf16[8,1280]{1,0:T(8,128)(2,1)S(1)}, u32[]{:S(2)}, u32[]{:S(2)}) collective-permute-start(bf16[8,1280]{1,0:T(8,128)(2,1)S(1)} %get-tuple-element.118), channel_id=1, source_target_pairs={{0,6},{1,7},{2,4},{3,5},{4,2},{5,3},{6,0},{7,1},{8,14},{9,15},{10,... | collective-permute-start | bytes 61448 | tf_op jit(solution)/shard_map/ppermute | solution.py:36
  35.7 9.0 %collective-permute-start.21 = (bf16[64,512]{1,0:T(8,128)(2,1)S(1)}, bf16[64,512]{1,0:T(8,128)(2,1)S(1)}, u32[]{:S(2)}, u32[]{:S(2)}) collective-permute-start(bf16[64,512]{1,0:T(8,128)(2,1)S(1)} %attend.4.after.refs_0_), channel_id=1, source_target_pairs={{0,4},{1,5},{2,6},{3,7},{4,0},{5,1},{6,2},{7,3},{8,12},{9,13},{10,... | collective-permute-start | bytes 196616 | tf_op jit(solution)/shard_map/ppermute | solution.py:36
  37.0 7.8 %collective-permute-start.22 = (bf16[64,512]{1,0:T(8,128)(2,1)S(1)}, bf16[64,512]{1,0:T(8,128)(2,1)S(1)}, u32[]{:S(2)}, u32[]{:S(2)}) collective-permute-start(bf16[64,512]{1,0:T(8,128)(2,1)S(1)} %attend.4.after.refs_0_), channel_id=1, source_target_pairs={{0,2},{1,3},{2,0},{3,1},{4,6},{5,7},{6,4},{7,5},{8,10},{9,11},{10,... | collective-permute-start | bytes 196616 | tf_op jit(solution)/shard_map/ppermute | solution.py:36
  39.2 5.6 %collective-permute-start.23 = (bf16[64,512]{1,0:T(8,128)(2,1)S(1)}, bf16[64,512]{1,0:T(8,128)(2,1)S(1)}, u32[]{:S(2)}, u32[]{:S(2)}) collective-permute-start(bf16[64,512]{1,0:T(8,128)(2,1)S(1)} %attend.4.after.refs_0_), channel_id=1, source_target_pairs={{0,6},{1,7},{2,4},{3,5},{4,2},{5,3},{6,0},{7,1},{8,14},{9,15},{10,... | collective-permute-start | bytes 196616 | tf_op jit(solution)/shard_map/ppermute | solution.py:36
  39.3 8.0 %collective-permute-start.20 = (bf16[64,512]{1,0:T(8,128)(2,1)S(1)}, bf16[64,512]{1,0:T(8,128)(2,1)S(1)}, u32[]{:S(2)}, u32[]{:S(2)}) collective-permute-start(bf16[64,512]{1,0:T(8,128)(2,1)S(1)} %attend.4.after.refs_0_), channel_id=1, source_target_pairs={{0,1},{1,0},{2,3},{3,2},{4,5},{5,4},{6,7},{7,6},{8,9},{9,8},{10,11... | collective-permute-start | bytes 196616 | tf_op jit(solution)/shard_map/ppermute | solution.py:36
  44.8 2.9 %collective-permute-start.24 = (bf16[64,512]{1,0:T(8,128)(2,1)S(1)}, bf16[64,512]{1,0:T(8,128)(2,1)S(1)}, u32[]{:S(2)}, u32[]{:S(2)}) collective-permute-start(bf16[64,512]{1,0:T(8,128)(2,1)S(1)} %get-tuple-element.131.refs_2_), channel_id=1, source_target_pairs={{0,1},{1,0},{2,3},{3,2},{4,5},{5,4},{6,7},{7,6},{8,9},{9,8},{10,11... | collective-permute-start | bytes 196616 | tf_op jit(solution)/shard_map/ppermute | solution.py:36
  53.1 4.6 %collective-permute-start.36 = (bf16[16,1152]{1,0:T(8,128)(2,1)S(1)}, bf16[16,1152]{1,0:T(8,128)(2,1)S(1)}, u32[]{:S(2)}, u32[]{:S(2)}) collective-permute-start(bf16[16,1152]{1,0:T(8,128)(2,1)S(1)} %get-tuple-element.140), channel_id=1, source_target_pairs={{0,4},{1,5},{2,6},{3,7},{4,0},{5,1},{6,2},{7,3},{8,12},{9,13},{10,... | collective-permute-start | bytes 110600 | tf_op jit(solution)/shard_map/ppermute | solution.py:36
  53.2 4.4 %collective-permute-start.37 = (bf16[16,1152]{1,0:T(8,128)(2,1)S(1)}, bf16[16,1152]{1,0:T(8,128)(2,1)S(1)}, u32[]{:S(2)}, u32[]{:S(2)}) collective-permute-start(bf16[16,1152]{1,0:T(8,128)(2,1)S(1)} %get-tuple-element.141), channel_id=1, source_target_pairs={{0,2},{1,3},{2,0},{3,1},{4,6},{5,7},{6,4},{7,5},{8,10},{9,11},{10,... | collective-permute-start | bytes 110600 | tf_op jit(solution)/shard_map/ppermute | solution.py:36
  54.7 4.6 %collective-permute-start.38 = (bf16[16,1152]{1,0:T(8,128)(2,1)S(1)}, bf16[16,1152]{1,0:T(8,128)(2,1)S(1)}, u32[]{:S(2)}, u32[]{:S(2)}) collective-permute-start(bf16[16,1152]{1,0:T(8,128)(2,1)S(1)} %get-tuple-element.142), channel_id=1, source_target_pairs={{0,6},{1,7},{2,4},{3,5},{4,2},{5,3},{6,0},{7,1},{8,14},{9,15},{10,... | collective-permute-start | bytes 110600 | tf_op jit(solution)/shard_map/ppermute | solution.py:36
  56.6 5.3 %collective-permute-start.35 = (bf16[16,1152]{1,0:T(8,128)(2,1)S(1)}, bf16[16,1152]{1,0:T(8,128)(2,1)S(1)}, u32[]{:S(2)}, u32[]{:S(2)}) collective-permute-start(bf16[16,1152]{1,0:T(8,128)(2,1)S(1)} %get-tuple-element.139.refs_3_), channel_id=1, source_target_pairs={{0,1},{1,0},{2,3},{3,2},{4,5},{5,4},{6,7},{7,6},{8,9},{9,8},{10,11... | collective-permute-start | bytes 110600 | tf_op jit(solution)/shard_map/ppermute | solution.py:36
  59.3 2.9 %collective-permute-start.39 = (bf16[16,1152]{1,0:T(8,128)(2,1)S(1)}, bf16[16,1152]{1,0:T(8,128)(2,1)S(1)}, u32[]{:S(2)}, u32[]{:S(2)}) collective-permute-start(bf16[16,1152]{1,0:T(8,128)(2,1)S(1)} %get-tuple-element.143.refs_5_), channel_id=1, source_target_pairs={{0,1},{1,0},{2,3},{3,2},{4,5},{5,4},{6,7},{7,6},{8,9},{9,8},{10,11... | collective-permute-start | bytes 110600 | tf_op jit(solution)/shard_map/ppermute | solution.py:36
  62.8 3.7 %collective-permute-start.42 = (bf16[8,1280]{1,0:T(8,128)(2,1)S(1)}, bf16[8,1280]{1,0:T(8,128)(2,1)S(1)}, u32[]{:S(2)}, u32[]{:S(2)}) collective-permute-start(bf16[8,1280]{1,0:T(8,128)(2,1)S(1)} %get-tuple-element.146), channel_id=1, source_target_pairs={{0,4},{1,5},{2,6},{3,7},{4,0},{5,1},{6,2},{7,3},{8,12},{9,13},{10,... | collective-permute-start | bytes 61448 | tf_op jit(solution)/shard_map/ppermute | solution.py:36
  62.8 4.6 %collective-permute-start.43 = (bf16[8,1280]{1,0:T(8,128)(2,1)S(1)}, bf16[8,1280]{1,0:T(8,128)(2,1)S(1)}, u32[]{:S(2)}, u32[]{:S(2)}) collective-permute-start(bf16[8,1280]{1,0:T(8,128)(2,1)S(1)} %get-tuple-element.147), channel_id=1, source_target_pairs={{0,6},{1,7},{2,4},{3,5},{4,2},{5,3},{6,0},{7,1},{8,14},{9,15},{10,... | collective-permute-start | bytes 61448 | tf_op jit(solution)/shard_map/ppermute | solution.py:36
  64.5 3.3 %collective-permute-start.44 = (bf16[8,1280]{1,0:T(8,128)(2,1)S(1)}, bf16[8,1280]{1,0:T(8,128)(2,1)S(1)}, u32[]{:S(2)}, u32[]{:S(2)}) collective-permute-start(bf16[8,1280]{1,0:T(8,128)(2,1)S(1)} %get-tuple-element.148), channel_id=1, source_target_pairs={{0,2},{1,3},{2,0},{3,1},{4,6},{5,7},{6,4},{7,5},{8,10},{9,11},{10,... | collective-permute-start | bytes 61448 | tf_op jit(solution)/shard_map/ppermute | solution.py:36
  68.4 5.5 %collective-permute-start.46 = (bf16[64,512]{1,0:T(8,128)(2,1)S(1)}, bf16[64,512]{1,0:T(8,128)(2,1)S(1)}, u32[]{:S(2)}, u32[]{:S(2)}) collective-permute-start(bf16[64,512]{1,0:T(8,128)(2,1)S(1)} %attend.5.refs_0_), channel_id=1, source_target_pairs={{0,4},{1,5},{2,6},{3,7},{4,0},{5,1},{6,2},{7,3},{8,12},{9,13},{10,... | collective-permute-start | bytes 196616 | tf_op jit(solution)/shard_map/ppermute | solution.py:36
  69.2 7.5 %collective-permute-start.48 = (bf16[64,512]{1,0:T(8,128)(2,1)S(1)}, bf16[64,512]{1,0:T(8,128)(2,1)S(1)}, u32[]{:S(2)}, u32[]{:S(2)}) collective-permute-start(bf16[64,512]{1,0:T(8,128)(2,1)S(1)} %attend.5.refs_0_), channel_id=1, source_target_pairs={{0,2},{1,3},{2,0},{3,1},{4,6},{5,7},{6,4},{7,5},{8,10},{9,11},{10,... | collective-permute-start | bytes 196616 | tf_op jit(solution)/shard_map/ppermute | solution.py:36
  70.0 6.7 %collective-permute-start.50 = (bf16[64,512]{1,0:T(8,128)(2,1)S(1)}, bf16[64,512]{1,0:T(8,128)(2,1)S(1)}, u32[]{:S(2)}, u32[]{:S(2)}) collective-permute-start(bf16[64,512]{1,0:T(8,128)(2,1)S(1)} %attend.5.refs_0_), channel_id=1, source_target_pairs={{0,6},{1,7},{2,4},{3,5},{4,2},{5,3},{6,0},{7,1},{8,14},{9,15},{10,... | collective-permute-start | bytes 196616 | tf_op jit(solution)/shard_map/ppermute | solution.py:36
  72.0 6.2 %collective-permute-start.45 = (bf16[64,512]{1,0:T(8,128)(2,1)S(1)}, bf16[64,512]{1,0:T(8,128)(2,1)S(1)}, u32[]{:S(2)}, u32[]{:S(2)}) collective-permute-start(bf16[64,512]{1,0:T(8,128)(2,1)S(1)} %attend.5.refs_0_), channel_id=1, source_target_pairs={{0,1},{1,0},{2,3},{3,2},{4,5},{5,4},{6,7},{7,6},{8,9},{9,8},{10,11... | collective-permute-start | bytes 196616 | tf_op jit(solution)/shard_map/ppermute | solution.py:36
  73.9 4.3 %collective-permute-start.47 = (bf16[64,512]{1,0:T(8,128)(2,1)S(1)}, bf16[64,512]{1,0:T(8,128)(2,1)S(1)}, u32[]{:S(2)}, u32[]{:S(2)}) collective-permute-start(bf16[64,512]{1,0:T(8,128)(2,1)S(1)} %collective-permute-done.46.refs_2_), channel_id=1, source_target_pairs={{0,1},{1,0},{2,3},{3,2},{4,5},{5,4},{6,7},{7,6},{8,9},{9,8},{10,11... | collective-permute-start | bytes 196616 | tf_op jit(solution)/shard_map/ppermute | solution.py:36
  84.0 4.6 %collective-permute-start.61 = (bf16[16,1152]{1,0:T(8,128)(2,1)S(1)}, bf16[16,1152]{1,0:T(8,128)(2,1)S(1)}, u32[]{:S(2)}, u32[]{:S(2)}) collective-permute-start(bf16[16,1152]{1,0:T(8,128)(2,1)S(1)} %get-tuple-element.154), channel_id=1, source_target_pairs={{0,4},{1,5},{2,6},{3,7},{4,0},{5,1},{6,2},{7,3},{8,12},{9,13},{10,... | collective-permute-start | bytes 110600 | tf_op jit(solution)/shard_map/ppermute | solution.py:36
  84.0 4.6 %collective-permute-start.62 = (bf16[16,1152]{1,0:T(8,128)(2,1)S(1)}, bf16[16,1152]{1,0:T(8,128)(2,1)S(1)}, u32[]{:S(2)}, u32[]{:S(2)}) collective-permute-start(bf16[16,1152]{1,0:T(8,128)(2,1)S(1)} %get-tuple-element.155), channel_id=1, source_target_pairs={{0,2},{1,3},{2,0},{3,1},{4,6},{5,7},{6,4},{7,5},{8,10},{9,11},{10,... | collective-permute-start | bytes 110600 | tf_op jit(solution)/shard_map/ppermute | solution.py:36
  85.8 4.6 %collective-permute-start.63 = (bf16[16,1152]{1,0:T(8,128)(2,1)S(1)}, bf16[16,1152]{1,0:T(8,128)(2,1)S(1)}, u32[]{:S(2)}, u32[]{:S(2)}) collective-permute-start(bf16[16,1152]{1,0:T(8,128)(2,1)S(1)} %get-tuple-element.156), channel_id=1, source_target_pairs={{0,6},{1,7},{2,4},{3,5},{4,2},{5,3},{6,0},{7,1},{8,14},{9,15},{10,... | collective-permute-start | bytes 110600 | tf_op jit(solution)/shard_map/ppermute | solution.py:36
  87.5 5.3 %collective-permute-start.60 = (bf16[16,1152]{1,0:T(8,128)(2,1)S(1)}, bf16[16,1152]{1,0:T(8,128)(2,1)S(1)}, u32[]{:S(2)}, u32[]{:S(2)}) collective-permute-start(bf16[16,1152]{1,0:T(8,128)(2,1)S(1)} %get-tuple-element.153.refs_3_), channel_id=1, source_target_pairs={{0,1},{1,0},{2,3},{3,2},{4,5},{5,4},{6,7},{7,6},{8,9},{9,8},{10,11... | collective-permute-start | bytes 110600 | tf_op jit(solution)/shard_map/ppermute | solution.py:36
  93.7 3.7 %collective-permute-start.67 = (bf16[8,1280]{1,0:T(8,128)(2,1)S(1)}, bf16[8,1280]{1,0:T(8,128)(2,1)S(1)}, u32[]{:S(2)}, u32[]{:S(2)}) collective-permute-start(bf16[8,1280]{1,0:T(8,128)(2,1)S(1)} %get-tuple-element.160), channel_id=1, source_target_pairs={{0,4},{1,5},{2,6},{3,7},{4,0},{5,1},{6,2},{7,3},{8,12},{9,13},{10,... | collective-permute-start | bytes 61448 | tf_op jit(solution)/shard_map/ppermute | solution.py:36
  93.7 4.6 %collective-permute-start.68 = (bf16[8,1280]{1,0:T(8,128)(2,1)S(1)}, bf16[8,1280]{1,0:T(8,128)(2,1)S(1)}, u32[]{:S(2)}, u32[]{:S(2)}) collective-permute-start(bf16[8,1280]{1,0:T(8,128)(2,1)S(1)} %get-tuple-element.161), channel_id=1, source_target_pairs={{0,6},{1,7},{2,4},{3,5},{4,2},{5,3},{6,0},{7,1},{8,14},{9,15},{10,... | collective-permute-start | bytes 61448 | tf_op jit(solution)/shard_map/ppermute | solution.py:36
  95.4 3.3 %collective-permute-start.69 = (bf16[8,1280]{1,0:T(8,128)(2,1)S(1)}, bf16[8,1280]{1,0:T(8,128)(2,1)S(1)}, u32[]{:S(2)}, u32[]{:S(2)}) collective-permute-start(bf16[8,1280]{1,0:T(8,128)(2,1)S(1)} %get-tuple-element.162), channel_id=1, source_target_pairs={{0,2},{1,3},{2,0},{3,1},{4,6},{5,7},{6,4},{7,5},{8,10},{9,11},{10,... | collective-permute-start | bytes 61448 | tf_op jit(solution)/shard_map/ppermute | solution.py:36
  99.3 5.5 %collective-permute-start.71 = (bf16[64,512]{1,0:T(8,128)(2,1)S(1)}, bf16[64,512]{1,0:T(8,128)(2,1)S(1)}, u32[]{:S(2)}, u32[]{:S(2)}) collective-permute-start(bf16[64,512]{1,0:T(8,128)(2,1)S(1)} %attend.6.refs_0_), channel_id=1, source_target_pairs={{0,4},{1,5},{2,6},{3,7},{4,0},{5,1},{6,2},{7,3},{8,12},{9,13},{10,... | collective-permute-start | bytes 196616 | tf_op jit(solution)/shard_map/ppermute | solution.py:36
  100.1 7.5 %collective-permute-start.73 = (bf16[64,512]{1,0:T(8,128)(2,1)S(1)}, bf16[64,512]{1,0:T(8,128)(2,1)S(1)}, u32[]{:S(2)}, u32[]{:S(2)}) collective-permute-start(bf16[64,512]{1,0:T(8,128)(2,1)S(1)} %attend.6.refs_0_), channel_id=1, source_target_pairs={{0,2},{1,3},{2,0},{3,1},{4,6},{5,7},{6,4},{7,5},{8,10},{9,11},{10,... | collective-permute-start | bytes 196616 | tf_op jit(solution)/shard_map/ppermute | solution.py:36
  100.9 6.7 %collective-permute-start.75 = (bf16[64,512]{1,0:T(8,128)(2,1)S(1)}, bf16[64,512]{1,0:T(8,128)(2,1)S(1)}, u32[]{:S(2)}, u32[]{:S(2)}) collective-permute-start(bf16[64,512]{1,0:T(8,128)(2,1)S(1)} %attend.6.refs_0_), channel_id=1, source_target_pairs={{0,6},{1,7},{2,4},{3,5},{4,2},{5,3},{6,0},{7,1},{8,14},{9,15},{10,... | collective-permute-start | bytes 196616 | tf_op jit(solution)/shard_map/ppermute | solution.py:36
  102.9 6.2 %collective-permute-start.70 = (bf16[64,512]{1,0:T(8,128)(2,1)S(1)}, bf16[64,512]{1,0:T(8,128)(2,1)S(1)}, u32[]{:S(2)}, u32[]{:S(2)}) collective-permute-start(bf16[64,512]{1,0:T(8,128)(2,1)S(1)} %attend.6.refs_0_), channel_id=1, source_target_pairs={{0,1},{1,0},{2,3},{3,2},{4,5},{5,4},{6,7},{7,6},{8,9},{9,8},{10,11... | collective-permute-start | bytes 196616 | tf_op jit(solution)/shard_map/ppermute | solution.py:36
  104.9 4.3 %collective-permute-start.72 = (bf16[64,512]{1,0:T(8,128)(2,1)S(1)}, bf16[64,512]{1,0:T(8,128)(2,1)S(1)}, u32[]{:S(2)}, u32[]{:S(2)}) collective-permute-start(bf16[64,512]{1,0:T(8,128)(2,1)S(1)} %collective-permute-done.71.refs_2_), channel_id=1, source_target_pairs={{0,1},{1,0},{2,3},{3,2},{4,5},{5,4},{6,7},{7,6},{8,9},{9,8},{10,11... | collective-permute-start | bytes 196616 | tf_op jit(solution)/shard_map/ppermute | solution.py:36
  110.0 37.3 %collective-permute-start.77 = (bf16[32,1024]{1,0:T(8,128)(2,1)S(1)}, bf16[32,1024]{1,0:T(8,128)(2,1)S(1)}, u32[]{:S(2)}, u32[]{:S(2)}) collective-permute-start(bf16[32,1024]{1,0:T(8,128)(2,1)S(1)} %get-tuple-element.165), channel_id=1, source_target_pairs={{16,28},{17,29},{18,30},{19,31},{20,24},{21,25},{22,26},{23,27}} | collective-permute-start | bytes 196616 | tf_op jit(solution)/shard_map/ppermute | solution.py:69
  111.3 39.8 %collective-permute-start.79 = (bf16[32,1024]{1,0:T(8,128)(2,1)S(1)}, bf16[32,1024]{1,0:T(8,128)(2,1)S(1)}, u32[]{:S(2)}, u32[]{:S(2)}) collective-permute-start(bf16[32,1024]{1,0:T(8,128)(2,1)S(1)} %get-tuple-element.165), channel_id=1, source_target_pairs={{16,30},{17,31},{18,28},{19,29},{20,26},{21,27},{22,24},{23,25}} | collective-permute-start | bytes 196616 | tf_op jit(solution)/shard_map/ppermute | solution.py:69
  112.6 39.5 %collective-permute-start.81 = (bf16[32,1024]{1,0:T(8,128)(2,1)S(1)}, bf16[32,1024]{1,0:T(8,128)(2,1)S(1)}, u32[]{:S(2)}, u32[]{:S(2)}) collective-permute-start(bf16[32,1024]{1,0:T(8,128)(2,1)S(1)} %get-tuple-element.165), channel_id=1, source_target_pairs={{16,26},{17,27},{18,24},{19,25},{20,30},{21,31},{22,28},{23,29}} | collective-permute-start | bytes 196616 | tf_op jit(solution)/shard_map/ppermute | solution.py:69
  113.9 38.8 %collective-permute-start.83 = (bf16[32,1024]{1,0:T(8,128)(2,1)S(1)}, bf16[32,1024]{1,0:T(8,128)(2,1)S(1)}, u32[]{:S(2)}, u32[]{:S(2)}) collective-permute-start(bf16[32,1024]{1,0:T(8,128)(2,1)S(1)} %get-tuple-element.165), channel_id=1, source_target_pairs={{16,24},{17,25},{18,26},{19,27},{20,28},{21,29},{22,30},{23,31}} | collective-permute-start | bytes 196616 | tf_op jit(solution)/shard_map/ppermute | solution.py:69
  147.3 5.9 %collective-permute-start.78 = (bf16[32,1024]{1,0:T(8,128)(2,1)S(1)}, bf16[32,1024]{1,0:T(8,128)(2,1)S(1)}, u32[]{:S(2)}, u32[]{:S(2)}) collective-permute-start(bf16[32,1024]{1,0:T(8,128)(2,1)S(1)} %collective-permute-done.77.refs_1_), channel_id=1, source_target_pairs={{0,1},{1,0},{2,3},{3,2},{4,5},{5,4},{6,7},{7,6},{8,9},{9,8},{10,11... | collective-permute-start | bytes 196616 | tf_op jit(solution)/shard_map/ppermute | solution.py:36
  155.4 8.3 %collective-permute-start.86 = (bf16[16,1152]{1,0:T(8,128)(2,1)S(1)}, bf16[16,1152]{1,0:T(8,128)(2,1)S(1)}, u32[]{:S(2)}, u32[]{:S(2)}) collective-permute-start(bf16[16,1152]{1,0:T(8,128)(2,1)S(1)} %get-tuple-element.168), channel_id=1, source_target_pairs={{0,4},{1,5},{2,6},{3,7},{4,0},{5,1},{6,2},{7,3},{8,12},{9,13},{10,... | collective-permute-start | bytes 110600 | tf_op jit(solution)/shard_map/ppermute | solution.py:36
  156.8 6.9 %collective-permute-start.87 = (bf16[16,1152]{1,0:T(8,128)(2,1)S(1)}, bf16[16,1152]{1,0:T(8,128)(2,1)S(1)}, u32[]{:S(2)}, u32[]{:S(2)}) collective-permute-start(bf16[16,1152]{1,0:T(8,128)(2,1)S(1)} %get-tuple-element.169), channel_id=1, source_target_pairs={{0,2},{1,3},{2,0},{3,1},{4,6},{5,7},{6,4},{7,5},{8,10},{9,11},{10,... | collective-permute-start | bytes 110600 | tf_op jit(solution)/shard_map/ppermute | solution.py:36
  157.4 6.3 %collective-permute-start.88 = (bf16[16,1152]{1,0:T(8,128)(2,1)S(1)}, bf16[16,1152]{1,0:T(8,128)(2,1)S(1)}, u32[]{:S(2)}, u32[]{:S(2)}) collective-permute-start(bf16[16,1152]{1,0:T(8,128)(2,1)S(1)} %get-tuple-element.170), channel_id=1, source_target_pairs={{0,6},{1,7},{2,4},{3,5},{4,2},{5,3},{6,0},{7,1},{8,14},{9,15},{10,... | collective-permute-start | bytes 110600 | tf_op jit(solution)/shard_map/ppermute | solution.py:36
  162.5 2.8 %collective-permute-start.85 = (bf16[16,1152]{1,0:T(8,128)(2,1)S(1)}, bf16[16,1152]{1,0:T(8,128)(2,1)S(1)}, u32[]{:S(2)}, u32[]{:S(2)}) collective-permute-start(bf16[16,1152]{1,0:T(8,128)(2,1)S(1)} %get-tuple-element.167.refs_3_), channel_id=1, source_target_pairs={{0,1},{1,0},{2,3},{3,2},{4,5},{5,4},{6,7},{7,6},{8,9},{9,8},{10,11... | collective-permute-start | bytes 110600 | tf_op jit(solution)/shard_map/ppermute | solution.py:36
  166.1 3.6 %collective-permute-start.92 = (bf16[8,1280]{1,0:T(8,128)(2,1)S(1)}, bf16[8,1280]{1,0:T(8,128)(2,1)S(1)}, u32[]{:S(2)}, u32[]{:S(2)}) collective-permute-start(bf16[8,1280]{1,0:T(8,128)(2,1)S(1)} %get-tuple-element.174), channel_id=1, source_target_pairs={{0,4},{1,5},{2,6},{3,7},{4,0},{5,1},{6,2},{7,3},{8,12},{9,13},{10,... | collective-permute-start | bytes 61448 | tf_op jit(solution)/shard_map/ppermute | solution.py:36
  166.5 4.5 %collective-permute-start.93 = (bf16[8,1280]{1,0:T(8,128)(2,1)S(1)}, bf16[8,1280]{1,0:T(8,128)(2,1)S(1)}, u32[]{:S(2)}, u32[]{:S(2)}) collective-permute-start(bf16[8,1280]{1,0:T(8,128)(2,1)S(1)} %get-tuple-element.175), channel_id=1, source_target_pairs={{0,6},{1,7},{2,4},{3,5},{4,2},{5,3},{6,0},{7,1},{8,14},{9,15},{10,... | collective-permute-start | bytes 61448 | tf_op jit(solution)/shard_map/ppermute | solution.py:36
  168.1 3.2 %collective-permute-start.94 = (bf16[8,1280]{1,0:T(8,128)(2,1)S(1)}, bf16[8,1280]{1,0:T(8,128)(2,1)S(1)}, u32[]{:S(2)}, u32[]{:S(2)}) collective-permute-start(bf16[8,1280]{1,0:T(8,128)(2,1)S(1)} %get-tuple-element.176), channel_id=1, source_target_pairs={{0,2},{1,3},{2,0},{3,1},{4,6},{5,7},{6,4},{7,5},{8,10},{9,11},{10,... | collective-permute-start | bytes 61448 | tf_op jit(solution)/shard_map/ppermute | solution.py:36
  173.6 5.9 %collective-permute-start.100 = (bf16[64,512]{1,0:T(8,128)(2,1)S(1)}, bf16[64,512]{1,0:T(8,128)(2,1)S(1)}, u32[]{:S(2)}, u32[]{:S(2)}) collective-permute-start(bf16[64,512]{1,0:T(8,128)(2,1)S(1)} %attend.7.refs_0_), channel_id=1, source_target_pairs={{0,6},{1,7},{2,4},{3,5},{4,2},{5,3},{6,0},{7,1},{8,14},{9,15},{10,... | collective-permute-start | bytes 196616 | tf_op jit(solution)/shard_map/ppermute | solution.py:36
  175.3 7.1 %collective-permute-start.96 = (bf16[64,512]{1,0:T(8,128)(2,1)S(1)}, bf16[64,512]{1,0:T(8,128)(2,1)S(1)}, u32[]{:S(2)}, u32[]{:S(2)}) collective-permute-start(bf16[64,512]{1,0:T(8,128)(2,1)S(1)} %attend.7.refs_0_), channel_id=1, source_target_pairs={{0,4},{1,5},{2,6},{3,7},{4,0},{5,1},{6,2},{7,3},{8,12},{9,13},{10,... | collective-permute-start | bytes 196616 | tf_op jit(solution)/shard_map/ppermute | solution.py:36
  175.3 8.2 %collective-permute-start.98 = (bf16[64,512]{1,0:T(8,128)(2,1)S(1)}, bf16[64,512]{1,0:T(8,128)(2,1)S(1)}, u32[]{:S(2)}, u32[]{:S(2)}) collective-permute-start(bf16[64,512]{1,0:T(8,128)(2,1)S(1)} %attend.7.refs_0_), channel_id=1, source_target_pairs={{0,2},{1,3},{2,0},{3,1},{4,6},{5,7},{6,4},{7,5},{8,10},{9,11},{10,... | collective-permute-start | bytes 196616 | tf_op jit(solution)/shard_map/ppermute | solution.py:36
  177.2 6.3 %collective-permute-start.95 = (bf16[64,512]{1,0:T(8,128)(2,1)S(1)}, bf16[64,512]{1,0:T(8,128)(2,1)S(1)}, u32[]{:S(2)}, u32[]{:S(2)}) collective-permute-start(bf16[64,512]{1,0:T(8,128)(2,1)S(1)} %attend.7.refs_0_), channel_id=1, source_target_pairs={{0,1},{1,0},{2,3},{3,2},{4,5},{5,4},{6,7},{7,6},{8,9},{9,8},{10,11... | collective-permute-start | bytes 196616 | tf_op jit(solution)/shard_map/ppermute | solution.py:36
  179.4 4.0 %collective-permute-start.101 = (bf16[64,512]{1,0:T(8,128)(2,1)S(1)}, bf16[64,512]{1,0:T(8,128)(2,1)S(1)}, u32[]{:S(2)}, u32[]{:S(2)}) collective-permute-start(bf16[64,512]{1,0:T(8,128)(2,1)S(1)} %collective-permute-done.100.refs_6_), channel_id=1, source_target_pairs={{0,1},{1,0},{2,3},{3,2},{4,5},{5,4},{6,7},{7,6},{8,9},{9,8},{10,11... | collective-permute-start | bytes 196616 | tf_op jit(solution)/shard_map/ppermute | solution.py:36
  188.8 4.5 %collective-permute-start.102 = (bf16[8,1024]{1,0:T(8,128)(2,1)S(1)}, bf16[8,1024]{1,0:T(8,128)(2,1)S(1)}, u32[]{:S(2)}, u32[]{:S(2)}) collective-permute-start(bf16[8,1024]{1,0:T(8,128)(2,1)S(1)} %get-tuple-element.179), channel_id=1, source_target_pairs={{0,6},{1,7},{2,4},{3,5},{4,2},{5,3},{6,0},{7,1},{8,14},{9,15},{10,... | collective-permute-start | bytes 49160 | tf_op jit(solution)/shard_map/ppermute | solution.py:36
  190.5 4.0 %collective-permute-start.104 = (bf16[8,1024]{1,0:T(8,128)(2,1)S(1)}, bf16[8,1024]{1,0:T(8,128)(2,1)S(1)}, u32[]{:S(2)}, u32[]{:S(2)}) collective-permute-start(bf16[8,1024]{1,0:T(8,128)(2,1)S(1)} %get-tuple-element.180), channel_id=1, source_target_pairs={{0,4},{1,5},{2,6},{3,7},{4,0},{5,1},{6,2},{7,3},{8,12},{9,13},{10,... | collective-permute-start | bytes 49160 | tf_op jit(solution)/shard_map/ppermute | solution.py:36
  190.5 5.1 %collective-permute-start.106 = (bf16[8,1024]{1,0:T(8,128)(2,1)S(1)}, bf16[8,1024]{1,0:T(8,128)(2,1)S(1)}, u32[]{:S(2)}, u32[]{:S(2)}) collective-permute-start(bf16[8,1024]{1,0:T(8,128)(2,1)S(1)} %get-tuple-element.181), channel_id=1, source_target_pairs={{0,2},{1,3},{2,0},{3,1},{4,6},{5,7},{6,4},{7,5},{8,10},{9,11},{10,... | collective-permute-start | bytes 49160 | tf_op jit(solution)/shard_map/ppermute | solution.py:36
  192.4 3.2 %collective-permute-start.108 = (bf16[8,1024]{1,0:T(8,128)(2,1)S(1)}, bf16[8,1024]{1,0:T(8,128)(2,1)S(1)}, u32[]{:S(2)}, u32[]{:S(2)}) collective-permute-start(bf16[8,1024]{1,0:T(8,128)(2,1)S(1)} %get-tuple-element.182.refs_7_), channel_id=1, source_target_pairs={{0,1},{1,0},{2,3},{3,2},{4,5},{5,4},{6,7},{7,6},{8,9},{9,8},{10,11... | collective-permute-start | bytes 49160 | tf_op jit(solution)/shard_map/ppermute | solution.py:36
  (49 other events, 93.2 us)

commit v2 on v1

--- a/solution.py
+++ b/solution.py
@@ -323,7 +323,7 @@
     def store(columns, product):
         out[:, columns] = product
 
-    matmul_into(store, normed, query, STEP)
+    matmul_into(store, normed, query, 2 * STEP)
 
 
 def narrow_kernel(normed, key, value, out):

time: 198 us -> 197 us (level)
  transfers between devices with their start and end apart: 109 -> 109, of which waited for: 45 -> 46; matrix products, arithmetic and copies ran while one was open for 0% -> 0% of each run, Pallas kernels for 12% -> 12%
where the time goes in v2:
time: 197 us
  starting transfers between devices  102 us (52%)
  waiting for transfers between devices  58.7 us (30%)
  Pallas kernels  34.6 us (18%)
    ppermute x97, starting transfers between devices, swapped(): return lax.ppermute(value, 'wide', [(i, i ^ bits) for i in range(count)])  91.6 us
    ppermute x12, waiting for transfers between devices, shifted(): return lax.ppermute(value, ('segment', 'wide'), pairs)  35.1 us
    ppermute x97, waiting for transfers between devices, swapped(): return lax.ppermute(value, 'wide', [(i, i ^ bits) for i in range(count)])  23.5 us
    pallas_call x25, Pallas kernels, call(): pl.pallas_call(inner, out_shape=outs + [pltpu.VMEM(array.shape, array.dty...  15.5 us
    pallas_call x2, Pallas kernels, loaded(): pl.pallas_call(functools.partial(load_kernel, (len(sources), len(small),...  10.6 us
    ppermute x12, starting transfers between devices, shifted(): return lax.ppermute(value, ('segment', 'wide'), pairs)  10.4 us
    pallas_call x1, Pallas kernels, project_first(): pl.pallas_call(functools.partial(project_first_kernel, query_first, tick)...  4.92 us
  transfers between devices with their start and end apart: 109, of which 46 were waited for; matrix products, arithmetic and copies ran while one was open for 0% of the time, Pallas kernels for 12%

profile of v2, /device:TPU:7, one launch (start us, length us, event | category | flops | bytes accessed | tf_op | source)
XLA Modules:
  0.0 196.7 jit_solution(15865774786833580856)
XLA Ops:
  1.6 2.4 %collective-permute-start.2 = (bf16[32,1152]{1,0:T(8,128)(2,1)S(1)}, bf16[32,1152]{1,0:T(8,128)(2,1)S(1)}, u32[]{:S(2)}, u32[]{:S(2)}) collective-permute-start(bf16[32,1152]{1,0:T(8,128)(2,1)S(1)} %open.1.refs_8_.refs_0_), channel_id=1, source_target_pairs={{0,4},{1,5},{2,6},{3,7},{4,0},{5,1},{6,2},{7,3},{8,12},{9,13},{10,... | collective-permute-start | bytes 221192 | tf_op jit(solution)/shard_map/ppermute | solution.py:36
  3.9 1.3 collective-permute-start.3
  5.2 1.5 collective-permute-start.1
  6.7 5.5 %load.3 = (bf16[1,8192,128]{2,1,0:T(8,128)(2,1)S(1)}, bf16[1,64,8192]{2,1,0:T(8,128)(2,1)S(1)}, bf16[1,64,1024]{2,1,0:T(8,128)(2,1)S(1)}, bf16[8192,128]{1,0:T(8...) custom-call(bf16[1,8192,128]{2,1,0:T(8,128)(2,1)} %bitcast.20, ...), custom_call_target="tpu_custom_call" | custom-call | bytes 27394048 | tf_op jit(solution)/shard_map/load/pallas_call | solution.py:128
  13.3 0.9 collective-permute-done.refs_8_.refs_4_.refs_1_
  15.5 2.9 %collective-permute-start.11 = (bf16[16,1152]{1,0:T(8,128)(2,1)S(1)}, bf16[16,1152]{1,0:T(8,128)(2,1)S(1)}, u32[]{:S(2)}, u32[]{:S(2)}) collective-permute-start(bf16[16,1152]{1,0:T(8,128)(2,1)S(1)} %get-tuple-element.112), channel_id=1, source_target_pairs={{0,6},{1,7},{2,4},{3,5},{4,2},{5,3},{6,0},{7,1},{8,14},{9,15},{10,... | collective-permute-start | bytes 110600 | tf_op jit(solution)/shard_map/ppermute | solution.py:36
  19.6 4.9 %project.4 = (f32[32,1024]{1,0:T(8,128)S(1)}, bf16[8192,1024]{1,0:T(8,128)(2,1)S(1)}) custom-call(bf16[32,8192]{1,0:T(8,128)(2,1)S(1)} %get-tuple-element.103.normed.refs_0_, bf16[8192,1024]{1,0:T(8,128)(2,1)} %bitcast.13, bf16[8192,1024]{1,0:T(8,128)(2,1)S(1)} %get-tuple-element.104._), custom_call_target="tpu_custom_call", output_to_operand_aliasing={{1}: (2, {})} | custom-call | bytes 16777216 | tf_op jit(solution)/shard_map/project/pallas_call | solution.py:672
  26.4 2.1 %collective-permute-start.15 = (bf16[8,1280]{1,0:T(8,128)(2,1)S(1)}, bf16[8,1280]{1,0:T(8,128)(2,1)S(1)}, u32[]{:S(2)}, u32[]{:S(2)}) collective-permute-start(bf16[8,1280]{1,0:T(8,128)(2,1)S(1)} %get-tuple-element.116), channel_id=1, source_target_pairs={{0,4},{1,5},{2,6},{3,7},{4,0},{5,1},{6,2},{7,3},{8,12},{9,13},{10,... | collective-permute-start | bytes 61448 | tf_op jit(solution)/shard_map/ppermute | solution.py:36
  28.4 1.3 collective-permute-start.16
  29.9 5.1 %load.4 = (bf16[8192,1024]{1,0:T(8,128)(2,1)S(1)}, bf16[4,384,512]{2,1,0:T(8,128)(2,1)S(1)}, bf16[4,384,512]{2,1,0:T(8,128)(2,1)S(1)}, f32[64,128]{1,0:T(8,128)S(1)}, f32[64,128]{1,0:T(8,128)S(1)}) custom-call(bf16[8192,1024]{1,0:T(8,128)(2,1)} %bitcast.14, bf16[4,384,1024]{2,1,0:T(8,128)(2,1)} %bitcast.17, bf16[4,384,1024]{2,1,0:T(8,128)(2,1)} %bitcast.19, ...), custom_call_target="tpu_custom_call" | custom-call | bytes 19922944 | tf_op jit(solution)/shard_map/load/pallas_call | solution.py:128
  35.7 1.2 collective-permute-start.21
  37.0 2.2 %collective-permute-start.22 = (bf16[64,512]{1,0:T(8,128)(2,1)S(1)}, bf16[64,512]{1,0:T(8,128)(2,1)S(1)}, u32[]{:S(2)}, u32[]{:S(2)}) collective-permute-start(bf16[64,512]{1,0:T(8,128)(2,1)S(1)} %attend.4.after.refs_0_), channel_id=1, source_target_pairs={{0,2},{1,3},{2,0},{3,1},{4,6},{5,7},{6,4},{7,5},{8,10},{9,11},{10,... | collective-permute-start | bytes 196616 | tf_op jit(solution)/shard_map/ppermute | solution.py:36
  39.3 1.8 collective-permute-start.20
  41.2 3.6 %load.5 = (bf16[8192,1024]{1,0:T(8,128)(2,1)S(1)}, f32[8,128]{1,0:T(8,128)S(1)}) custom-call(bf16[8192,1024]{1,0:T(8,128)(2,1)} %bitcast.15, bf16[64,512]{1,0:T(8,128)(2,1)S(1)} %attend.4.after.refs_0_, bf16[8192,1024]{1,0:T(8,128)(2,1)S(1)} %get-tuple-element.129._), custom_call_target="tpu_custom_call", output_to_operand_aliasing={{0}: (2, {})} | custom-call | bytes 8388608 | tf_op jit(solution)/shard_map/load/pallas_call | solution.py:728
  44.8 2.0 %collective-permute-start.24 = (bf16[64,512]{1,0:T(8,128)(2,1)S(1)}, bf16[64,512]{1,0:T(8,128)(2,1)S(1)}, u32[]{:S(2)}, u32[]{:S(2)}) collective-permute-start(bf16[64,512]{1,0:T(8,128)(2,1)S(1)} %get-tuple-element.131.refs_2_), channel_id=1, source_target_pairs={{0,1},{1,0},{2,3},{3,2},{4,5},{5,4},{6,7},{7,6},{8,9},{9,8},{10,11... | collective-permute-start | bytes 196616 | tf_op jit(solution)/shard_map/ppermute | solution.py:36
  53.2 1.5 collective-permute-start.37
  54.7 1.9 collective-permute-start.38
  56.6 1.0 collective-permute-start.35
  57.6 1.7 collective-permute-done.38.refs_2_
  59.3 2.1 %collective-permute-start.39 = (bf16[16,1152]{1,0:T(8,128)(2,1)S(1)}, bf16[16,1152]{1,0:T(8,128)(2,1)S(1)}, u32[]{:S(2)}, u32[]{:S(2)}) collective-permute-start(bf16[16,1152]{1,0:T(8,128)(2,1)S(1)} %get-tuple-element.143.refs_5_), channel_id=1, source_target_pairs={{0,1},{1,0},{2,3},{3,2},{4,5},{5,4},{6,7},{7,6},{8,9},{9,8},{10,11... | collective-permute-start | bytes 110600 | tf_op jit(solution)/shard_map/ppermute | solution.py:36
  62.8 1.7 collective-permute-start.43
  65.4 1.0 collective-permute-done.42.refs_2_
  66.4 0.9 collective-permute-done.43.refs_3_
  70.0 2.1 %collective-permute-start.50 = (bf16[64,512]{1,0:T(8,128)(2,1)S(1)}, bf16[64,512]{1,0:T(8,128)(2,1)S(1)}, u32[]{:S(2)}, u32[]{:S(2)}) collective-permute-start(bf16[64,512]{1,0:T(8,128)(2,1)S(1)} %attend.5.refs_0_), channel_id=1, source_target_pairs={{0,6},{1,7},{2,4},{3,5},{4,2},{5,3},{6,0},{7,1},{8,14},{9,15},{10,... | collective-permute-start | bytes 196616 | tf_op jit(solution)/shard_map/ppermute | solution.py:36
  72.0 1.9 collective-permute-start.45
  73.9 2.7 %collective-permute-start.47 = (bf16[64,512]{1,0:T(8,128)(2,1)S(1)}, bf16[64,512]{1,0:T(8,128)(2,1)S(1)}, u32[]{:S(2)}, u32[]{:S(2)}) collective-permute-start(bf16[64,512]{1,0:T(8,128)(2,1)S(1)} %collective-permute-done.46.refs_2_), channel_id=1, source_target_pairs={{0,1},{1,0},{2,3},{3,2},{4,5},{5,4},{6,7},{7,6},{8,9},{9,8},{10,11... | collective-permute-start | bytes 196616 | tf_op jit(solution)/shard_map/ppermute | solution.py:36
  76.7 1.5 collective-permute-start.51
  84.0 1.8 collective-permute-start.62
  85.8 1.7 collective-permute-start.63
  87.5 1.0 collective-permute-start.60
  88.6 1.9 collective-permute-done.63.refs_2_
  90.4 1.9 collective-permute-start.64
  93.7 1.7 collective-permute-start.68
  96.3 1.0 collective-permute-done.67.refs_2_
  100.9 2.1 %collective-permute-start.75 = (bf16[64,512]{1,0:T(8,128)(2,1)S(1)}, bf16[64,512]{1,0:T(8,128)(2,1)S(1)}, u32[]{:S(2)}, u32[]{:S(2)}) collective-permute-start(bf16[64,512]{1,0:T(8,128)(2,1)S(1)} %attend.6.refs_0_), channel_id=1, source_target_pairs={{0,6},{1,7},{2,4},{3,5},{4,2},{5,3},{6,0},{7,1},{8,14},{9,15},{10,... | collective-permute-start | bytes 196616 | tf_op jit(solution)/shard_map/ppermute | solution.py:36
  102.9 1.9 collective-permute-start.70
  104.9 2.7 %collective-permute-start.72 = (bf16[64,512]{1,0:T(8,128)(2,1)S(1)}, bf16[64,512]{1,0:T(8,128)(2,1)S(1)}, u32[]{:S(2)}, u32[]{:S(2)}) collective-permute-start(bf16[64,512]{1,0:T(8,128)(2,1)S(1)} %collective-permute-done.71.refs_2_), channel_id=1, source_target_pairs={{0,1},{1,0},{2,3},{3,2},{4,5},{5,4},{6,7},{7,6},{8,9},{9,8},{10,11... | collective-permute-start | bytes 196616 | tf_op jit(solution)/shard_map/ppermute | solution.py:36
  107.6 1.5 collective-permute-start.76
  110.0 1.3 collective-permute-start.77
  111.3 1.3 collective-permute-start.79
  112.6 1.3 collective-permute-start.81
  113.9 1.3 collective-permute-start.83
  115.2 31.9 %collective-permute-done.77.refs_1_ = bf16[32,1024]{1,0:T(8,128)(2,1)S(1)} collective-permute-done((bf16[32,1024]{1,0:T(8,128)(2,1)S(1)}, bf16[32,1024]{1,0:T(8,128)(2,1)S(1)}, u32[]{:S(2)}, u32[]{:S(2)}) %collective-permute-start.77) | collective-permute-done | bytes 65568 | tf_op jit(solution)/shard_map/ppermute | solution.py:69
  147.1 1.0 collective-permute-start.78
  148.1 2.5 %collective-permute-done.79.refs_3_ = bf16[32,1024]{1,0:T(8,128)(2,1)S(1)} collective-permute-done((bf16[32,1024]{1,0:T(8,128)(2,1)S(1)}, bf16[32,1024]{1,0:T(8,128)(2,1)S(1)}, u32[]{:S(2)}, u32[]{:S(2)}) %collective-permute-start.79) | collective-permute-done | bytes 65568 | tf_op jit(solution)/shard_map/ppermute | solution.py:69
  150.7 1.0 collective-permute-start.80
  153.8 1.2 norm.5
  155.0 1.6 collective-permute-start.86
  157.1 1.5 collective-permute-start.88
  158.6 3.1 %project.7.refs_3_.refs_0_ = f32[32,1024]{1,0:T(8,128)S(1)} custom-call(bf16[32,8192]{1,0:T(8,128)(2,1)S(1)} %get-tuple-element.166.refs_0_, bf16[8192,1024]{1,0:T(8,128)(2,1)S(1)} %get-tuple-element.138.refs_1_), custom_call_target="tpu_custom_call" | custom-call | bytes 16777216 | tf_op jit(solution)/shard_map/project/pallas_call | solution.py:95
  161.8 1.2 collective-permute-start.85
  166.0 1.7 collective-permute-start.93
  169.3 1.2 collective-permute-done.93.refs_3_
  170.9 2.3 %attend.7.refs_0_ = bf16[64,512]{1,0:T(8,128)(2,1)S(1)} custom-call(s32[2,2]{1,0:T(2,128)S(1)} %copy-done.2, s32[2,2]{1,0:T(2,128)S(1)} %collective-permute-done.refs_8_.refs_4_.refs_1_, bf16[8,1280]{1,0:T(8,128)(2,1)S(1)} %collective-permute-done.92.refs_2_, bf16[8,1280]{1,0:T(8,128)(2,1)S(1)} %collective-permute-done.93.refs_3_, ...), custom_call_target="tpu_custom_call" | custom-call | bytes 1048576 | tf_op jit(solution)/shard_map/attend/pallas_call | solution.py:95
  173.2 1.4 collective-permute-start.100
  174.9 1.8 collective-permute-start.98
  176.7 2.2 %collective-permute-start.95 = (bf16[64,512]{1,0:T(8,128)(2,1)S(1)}, bf16[64,512]{1,0:T(8,128)(2,1)S(1)}, u32[]{:S(2)}, u32[]{:S(2)}) collective-permute-start(bf16[64,512]{1,0:T(8,128)(2,1)S(1)} %attend.7.refs_0_), channel_id=1, source_target_pairs={{0,1},{1,0},{2,3},{3,2},{4,5},{5,4},{6,7},{7,6},{8,9},{9,8},{10,11... | collective-permute-start | bytes 196616 | tf_op jit(solution)/shard_map/ppermute | solution.py:36
  179.0 2.2 %collective-permute-start.101 = (bf16[64,512]{1,0:T(8,128)(2,1)S(1)}, bf16[64,512]{1,0:T(8,128)(2,1)S(1)}, u32[]{:S(2)}, u32[]{:S(2)}) collective-permute-start(bf16[64,512]{1,0:T(8,128)(2,1)S(1)} %collective-permute-done.100.refs_6_), channel_id=1, source_target_pairs={{0,1},{1,0},{2,3},{3,2},{4,5},{5,4},{6,7},{7,6},{8,9},{9,8},{10,11... | collective-permute-start | bytes 196616 | tf_op jit(solution)/shard_map/ppermute | solution.py:36
  181.6 1.4 collective-permute-start.97
  184.3 4.1 %leave.7 = (bf16[32,1024]{1,0:T(8,128)(2,1)}, bf16[32,1024]{1,0:T(8,128)(2,1)}, bf16[8,1024]{1,0:T(8,128)(2,1)S(1)}, bf16[8,1024]{1,0:T(8,128)(2,1)S(1)}, bf16[8...) custom-call(bf16[64,512]{1,0:T(8,128)(2,1)S(1)} %attend.7.refs_0_, ...), custom_call_target="tpu_custom_call" | custom-call | bytes 1048576 | tf_op jit(solution)/shard_map/leave/pallas_call | solution.py:95
  188.4 1.3 collective-permute-start.102
  189.7 2.2 %collective-permute-start.106 = (bf16[8,1024]{1,0:T(8,128)(2,1)S(1)}, bf16[8,1024]{1,0:T(8,128)(2,1)S(1)}, u32[]{:S(2)}, u32[]{:S(2)}) collective-permute-start(bf16[8,1024]{1,0:T(8,128)(2,1)S(1)} %get-tuple-element.181), channel_id=1, source_target_pairs={{0,2},{1,3},{2,0},{3,1},{4,6},{5,7},{6,4},{7,5},{8,10},{9,11},{10,... | collective-permute-start | bytes 49160 | tf_op jit(solution)/shard_map/ppermute | solution.py:36
  191.9 1.0 collective-permute-start.108
  192.9 1.2 collective-permute-start.103
  (198 shorter events, 43.8 us)
Async XLA Ops:
  1.6 10.6 %collective-permute-start.2 = (bf16[32,1152]{1,0:T(8,128)(2,1)S(1)}, bf16[32,1152]{1,0:T(8,128)(2,1)S(1)}, u32[]{:S(2)}, u32[]{:S(2)}) collective-permute-start(bf16[32,1152]{1,0:T(8,128)(2,1)S(1)} %open.1.refs_8_.refs_0_), channel_id=1, source_target_pairs={{0,4},{1,5},{2,6},{3,7},{4,0},{5,1},{6,2},{7,3},{8,12},{9,13},{10,... | collective-permute-start | bytes 221192 | tf_op jit(solution)/shard_map/ppermute | solution.py:36
  3.9 8.3 %collective-permute-start.3 = (bf16[32,1152]{1,0:T(8,128)(2,1)S(1)}, bf16[32,1152]{1,0:T(8,128)(2,1)S(1)}, u32[]{:S(2)}, u32[]{:S(2)}) collective-permute-start(bf16[32,1152]{1,0:T(8,128)(2,1)S(1)} %open.1.refs_8_.refs_0_), channel_id=1, source_target_pairs={{0,2},{1,3},{2,0},{3,1},{4,6},{5,7},{6,4},{7,5},{8,10},{9,11},{10,... | collective-permute-start | bytes 221192 | tf_op jit(solution)/shard_map/ppermute | solution.py:36
  5.2 7.0 %collective-permute-start.4 = (bf16[32,1152]{1,0:T(8,128)(2,1)S(1)}, bf16[32,1152]{1,0:T(8,128)(2,1)S(1)}, u32[]{:S(2)}, u32[]{:S(2)}) collective-permute-start(bf16[32,1152]{1,0:T(8,128)(2,1)S(1)} %open.1.refs_8_.refs_0_), channel_id=1, source_target_pairs={{0,6},{1,7},{2,4},{3,5},{4,2},{5,3},{6,0},{7,1},{8,14},{9,15},{10,... | collective-permute-start | bytes 221192 | tf_op jit(solution)/shard_map/ppermute | solution.py:36
  5.2 9.0 %collective-permute-start.1 = (bf16[32,1152]{1,0:T(8,128)(2,1)S(1)}, bf16[32,1152]{1,0:T(8,128)(2,1)S(1)}, u32[]{:S(2)}, u32[]{:S(2)}) collective-permute-start(bf16[32,1152]{1,0:T(8,128)(2,1)S(1)} %open.1.refs_8_.refs_0_), channel_id=1, source_target_pairs={{0,1},{1,0},{2,3},{3,2},{4,5},{5,4},{6,7},{7,6},{8,9},{9,8},{10,11... | collective-permute-start | bytes 221192 | tf_op jit(solution)/shard_map/ppermute | solution.py:36
  14.7 20.4 %collective-permute-start.18 = (bf16[4,384,512]{2,1,0:T(8,128)(2,1)S(1)}, bf16[4,384,512]{2,1,0:T(8,128)(2,1)S(1)}, u32[]{:S(2)}, u32[]{:S(2)}) collective-permute-start(bf16[4,384,512]{2,1,0:T(8,128)(2,1)S(1)} %get-tuple-element.127), channel_id=1, source_target_pairs={{0,1},{1,0},{2,3},{3,2},{4,5},{5,4},{6,7},{7,6},{8,9},{9,8},{10,11... | collective-permute-start | bytes 4718600 | tf_op jit(solution)/shard_map/ppermute | solution.py:36
  14.9 20.2 %collective-permute-start.19 = (bf16[4,384,512]{2,1,0:T(8,128)(2,1)S(1)}, bf16[4,384,512]{2,1,0:T(8,128)(2,1)S(1)}, u32[]{:S(2)}, u32[]{:S(2)}) collective-permute-start(bf16[4,384,512]{2,1,0:T(8,128)(2,1)S(1)} %get-tuple-element.128), channel_id=1, source_target_pairs={{0,1},{1,0},{2,3},{3,2},{4,5},{5,4},{6,7},{7,6},{8,9},{9,8},{10,11... | collective-permute-start | bytes 4718600 | tf_op jit(solution)/shard_map/ppermute | solution.py:36
  15.2 3.5 %collective-permute-start.10 = (bf16[16,1152]{1,0:T(8,128)(2,1)S(1)}, bf16[16,1152]{1,0:T(8,128)(2,1)S(1)}, u32[]{:S(2)}, u32[]{:S(2)}) collective-permute-start(bf16[16,1152]{1,0:T(8,128)(2,1)S(1)} %get-tuple-element.111), channel_id=1, source_target_pairs={{0,2},{1,3},{2,0},{3,1},{4,6},{5,7},{6,4},{7,5},{8,10},{9,11},{10,... | collective-permute-start | bytes 110600 | tf_op jit(solution)/shard_map/ppermute | solution.py:36
  15.5 9.0 %collective-permute-start.11 = (bf16[16,1152]{1,0:T(8,128)(2,1)S(1)}, bf16[16,1152]{1,0:T(8,128)(2,1)S(1)}, u32[]{:S(2)}, u32[]{:S(2)}) collective-permute-start(bf16[16,1152]{1,0:T(8,128)(2,1)S(1)} %get-tuple-element.112), channel_id=1, source_target_pairs={{0,6},{1,7},{2,4},{3,5},{4,2},{5,3},{6,0},{7,1},{8,14},{9,15},{10,... | collective-permute-start | bytes 110600 | tf_op jit(solution)/shard_map/ppermute | solution.py:36
  18.4 6.1 %collective-permute-start.9 = (bf16[16,1152]{1,0:T(8,128)(2,1)S(1)}, bf16[16,1152]{1,0:T(8,128)(2,1)S(1)}, u32[]{:S(2)}, u32[]{:S(2)}) collective-permute-start(bf16[16,1152]{1,0:T(8,128)(2,1)S(1)} %get-tuple-element.110), channel_id=1, source_target_pairs={{0,4},{1,5},{2,6},{3,7},{4,0},{5,1},{6,2},{7,3},{8,12},{9,13},{10,... | collective-permute-start | bytes 110600 | tf_op jit(solution)/shard_map/ppermute | solution.py:36
  18.7 6.4 %collective-permute-start.8 = (bf16[16,1152]{1,0:T(8,128)(2,1)S(1)}, bf16[16,1152]{1,0:T(8,128)(2,1)S(1)}, u32[]{:S(2)}, u32[]{:S(2)}) collective-permute-start(bf16[16,1152]{1,0:T(8,128)(2,1)S(1)} %get-tuple-element.109.refs_3_), channel_id=1, source_target_pairs={{0,1},{1,0},{2,3},{3,2},{4,5},{5,4},{6,7},{7,6},{8,9},{9,8},{10,11... | collective-permute-start | bytes 110600 | tf_op jit(solution)/shard_map/ppermute | solution.py:36
  26.4 8.7 %collective-permute-start.15 = (bf16[8,1280]{1,0:T(8,128)(2,1)S(1)}, bf16[8,1280]{1,0:T(8,128)(2,1)S(1)}, u32[]{:S(2)}, u32[]{:S(2)}) collective-permute-start(bf16[8,1280]{1,0:T(8,128)(2,1)S(1)} %get-tuple-element.116), channel_id=1, source_target_pairs={{0,4},{1,5},{2,6},{3,7},{4,0},{5,1},{6,2},{7,3},{8,12},{9,13},{10,... | collective-permute-start | bytes 61448 | tf_op jit(solution)/shard_map/ppermute | solution.py:36
  28.4 6.6 %collective-permute-start.16 = (bf16[8,1280]{1,0:T(8,128)(2,1)S(1)}, bf16[8,1280]{1,0:T(8,128)(2,1)S(1)}, u32[]{:S(2)}, u32[]{:S(2)}) collective-permute-start(bf16[8,1280]{1,0:T(8,128)(2,1)S(1)} %get-tuple-element.117), channel_id=1, source_target_pairs={{0,2},{1,3},{2,0},{3,1},{4,6},{5,7},{6,4},{7,5},{8,10},{9,11},{10,... | collective-permute-start | bytes 61448 | tf_op jit(solution)/shard_map/ppermute | solution.py:36
  29.8 5.3 %collective-permute-start.17 = (bf16[8,1280]{1,0:T(8,128)(2,1)S(1)}, bf16[8,1280]{1,0:T(8,128)(2,1)S(1)}, u32[]{:S(2)}, u32[]{:S(2)}) collective-permute-start(bf16[8,1280]{1,0:T(8,128)(2,1)S(1)} %get-tuple-element.118), channel_id=1, source_target_pairs={{0,6},{1,7},{2,4},{3,5},{4,2},{5,3},{6,0},{7,1},{8,14},{9,15},{10,... | collective-permute-start | bytes 61448 | tf_op jit(solution)/shard_map/ppermute | solution.py:36
  35.7 9.0 %collective-permute-start.21 = (bf16[64,512]{1,0:T(8,128)(2,1)S(1)}, bf16[64,512]{1,0:T(8,128)(2,1)S(1)}, u32[]{:S(2)}, u32[]{:S(2)}) collective-permute-start(bf16[64,512]{1,0:T(8,128)(2,1)S(1)} %attend.4.after.refs_0_), channel_id=1, source_target_pairs={{0,4},{1,5},{2,6},{3,7},{4,0},{5,1},{6,2},{7,3},{8,12},{9,13},{10,... | collective-permute-start | bytes 196616 | tf_op jit(solution)/shard_map/ppermute | solution.py:36
  37.0 7.8 %collective-permute-start.22 = (bf16[64,512]{1,0:T(8,128)(2,1)S(1)}, bf16[64,512]{1,0:T(8,128)(2,1)S(1)}, u32[]{:S(2)}, u32[]{:S(2)}) collective-permute-start(bf16[64,512]{1,0:T(8,128)(2,1)S(1)} %attend.4.after.refs_0_), channel_id=1, source_target_pairs={{0,2},{1,3},{2,0},{3,1},{4,6},{5,7},{6,4},{7,5},{8,10},{9,11},{10,... | collective-permute-start | bytes 196616 | tf_op jit(solution)/shard_map/ppermute | solution.py:36
  39.2 5.6 %collective-permute-start.23 = (bf16[64,512]{1,0:T(8,128)(2,1)S(1)}, bf16[64,512]{1,0:T(8,128)(2,1)S(1)}, u32[]{:S(2)}, u32[]{:S(2)}) collective-permute-start(bf16[64,512]{1,0:T(8,128)(2,1)S(1)} %attend.4.after.refs_0_), channel_id=1, source_target_pairs={{0,6},{1,7},{2,4},{3,5},{4,2},{5,3},{6,0},{7,1},{8,14},{9,15},{10,... | collective-permute-start | bytes 196616 | tf_op jit(solution)/shard_map/ppermute | solution.py:36
  39.3 8.0 %collective-permute-start.20 = (bf16[64,512]{1,0:T(8,128)(2,1)S(1)}, bf16[64,512]{1,0:T(8,128)(2,1)S(1)}, u32[]{:S(2)}, u32[]{:S(2)}) collective-permute-start(bf16[64,512]{1,0:T(8,128)(2,1)S(1)} %attend.4.after.refs_0_), channel_id=1, source_target_pairs={{0,1},{1,0},{2,3},{3,2},{4,5},{5,4},{6,7},{7,6},{8,9},{9,8},{10,11... | collective-permute-start | bytes 196616 | tf_op jit(solution)/shard_map/ppermute | solution.py:36
  44.8 2.9 %collective-permute-start.24 = (bf16[64,512]{1,0:T(8,128)(2,1)S(1)}, bf16[64,512]{1,0:T(8,128)(2,1)S(1)}, u32[]{:S(2)}, u32[]{:S(2)}) collective-permute-start(bf16[64,512]{1,0:T(8,128)(2,1)S(1)} %get-tuple-element.131.refs_2_), channel_id=1, source_target_pairs={{0,1},{1,0},{2,3},{3,2},{4,5},{5,4},{6,7},{7,6},{8,9},{9,8},{10,11... | collective-permute-start | bytes 196616 | tf_op jit(solution)/shard_map/ppermute | solution.py:36
  53.1 4.6 %collective-permute-start.36 = (bf16[16,1152]{1,0:T(8,128)(2,1)S(1)}, bf16[16,1152]{1,0:T(8,128)(2,1)S(1)}, u32[]{:S(2)}, u32[]{:S(2)}) collective-permute-start(bf16[16,1152]{1,0:T(8,128)(2,1)S(1)} %get-tuple-element.140), channel_id=1, source_target_pairs={{0,4},{1,5},{2,6},{3,7},{4,0},{5,1},{6,2},{7,3},{8,12},{9,13},{10,... | collective-permute-start | bytes 110600 | tf_op jit(solution)/shard_map/ppermute | solution.py:36
  53.2 4.4 %collective-permute-start.37 = (bf16[16,1152]{1,0:T(8,128)(2,1)S(1)}, bf16[16,1152]{1,0:T(8,128)(2,1)S(1)}, u32[]{:S(2)}, u32[]{:S(2)}) collective-permute-start(bf16[16,1152]{1,0:T(8,128)(2,1)S(1)} %get-tuple-element.141), channel_id=1, source_target_pairs={{0,2},{1,3},{2,0},{3,1},{4,6},{5,7},{6,4},{7,5},{8,10},{9,11},{10,... | collective-permute-start | bytes 110600 | tf_op jit(solution)/shard_map/ppermute | solution.py:36
  54.7 4.6 %collective-permute-start.38 = (bf16[16,1152]{1,0:T(8,128)(2,1)S(1)}, bf16[16,1152]{1,0:T(8,128)(2,1)S(1)}, u32[]{:S(2)}, u32[]{:S(2)}) collective-permute-start(bf16[16,1152]{1,0:T(8,128)(2,1)S(1)} %get-tuple-element.142), channel_id=1, source_target_pairs={{0,6},{1,7},{2,4},{3,5},{4,2},{5,3},{6,0},{7,1},{8,14},{9,15},{10,... | collective-permute-start | bytes 110600 | tf_op jit(solution)/shard_map/ppermute | solution.py:36
  56.6 5.3 %collective-permute-start.35 = (bf16[16,1152]{1,0:T(8,128)(2,1)S(1)}, bf16[16,1152]{1,0:T(8,128)(2,1)S(1)}, u32[]{:S(2)}, u32[]{:S(2)}) collective-permute-start(bf16[16,1152]{1,0:T(8,128)(2,1)S(1)} %get-tuple-element.139.refs_3_), channel_id=1, source_target_pairs={{0,1},{1,0},{2,3},{3,2},{4,5},{5,4},{6,7},{7,6},{8,9},{9,8},{10,11... | collective-permute-start | bytes 110600 | tf_op jit(solution)/shard_map/ppermute | solution.py:36
  59.3 2.9 %collective-permute-start.39 = (bf16[16,1152]{1,0:T(8,128)(2,1)S(1)}, bf16[16,1152]{1,0:T(8,128)(2,1)S(1)}, u32[]{:S(2)}, u32[]{:S(2)}) collective-permute-start(bf16[16,1152]{1,0:T(8,128)(2,1)S(1)} %get-tuple-element.143.refs_5_), channel_id=1, source_target_pairs={{0,1},{1,0},{2,3},{3,2},{4,5},{5,4},{6,7},{7,6},{8,9},{9,8},{10,11... | collective-permute-start | bytes 110600 | tf_op jit(solution)/shard_map/ppermute | solution.py:36
  62.8 3.7 %collective-permute-start.42 = (bf16[8,1280]{1,0:T(8,128)(2,1)S(1)}, bf16[8,1280]{1,0:T(8,128)(2,1)S(1)}, u32[]{:S(2)}, u32[]{:S(2)}) collective-permute-start(bf16[8,1280]{1,0:T(8,128)(2,1)S(1)} %get-tuple-element.146), channel_id=1, source_target_pairs={{0,4},{1,5},{2,6},{3,7},{4,0},{5,1},{6,2},{7,3},{8,12},{9,13},{10,... | collective-permute-start | bytes 61448 | tf_op jit(solution)/shard_map/ppermute | solution.py:36
  62.8 4.6 %collective-permute-start.43 = (bf16[8,1280]{1,0:T(8,128)(2,1)S(1)}, bf16[8,1280]{1,0:T(8,128)(2,1)S(1)}, u32[]{:S(2)}, u32[]{:S(2)}) collective-permute-start(bf16[8,1280]{1,0:T(8,128)(2,1)S(1)} %get-tuple-element.147), channel_id=1, source_target_pairs={{0,6},{1,7},{2,4},{3,5},{4,2},{5,3},{6,0},{7,1},{8,14},{9,15},{10,... | collective-permute-start | bytes 61448 | tf_op jit(solution)/shard_map/ppermute | solution.py:36
  64.5 3.3 %collective-permute-start.44 = (bf16[8,1280]{1,0:T(8,128)(2,1)S(1)}, bf16[8,1280]{1,0:T(8,128)(2,1)S(1)}, u32[]{:S(2)}, u32[]{:S(2)}) collective-permute-start(bf16[8,1280]{1,0:T(8,128)(2,1)S(1)} %get-tuple-element.148), channel_id=1, source_target_pairs={{0,2},{1,3},{2,0},{3,1},{4,6},{5,7},{6,4},{7,5},{8,10},{9,11},{10,... | collective-permute-start | bytes 61448 | tf_op jit(solution)/shard_map/ppermute | solution.py:36
  68.4 5.5 %collective-permute-start.46 = (bf16[64,512]{1,0:T(8,128)(2,1)S(1)}, bf16[64,512]{1,0:T(8,128)(2,1)S(1)}, u32[]{:S(2)}, u32[]{:S(2)}) collective-permute-start(bf16[64,512]{1,0:T(8,128)(2,1)S(1)} %attend.5.refs_0_), channel_id=1, source_target_pairs={{0,4},{1,5},{2,6},{3,7},{4,0},{5,1},{6,2},{7,3},{8,12},{9,13},{10,... | collective-permute-start | bytes 196616 | tf_op jit(solution)/shard_map/ppermute | solution.py:36
  69.2 7.5 %collective-permute-start.48 = (bf16[64,512]{1,0:T(8,128)(2,1)S(1)}, bf16[64,512]{1,0:T(8,128)(2,1)S(1)}, u32[]{:S(2)}, u32[]{:S(2)}) collective-permute-start(bf16[64,512]{1,0:T(8,128)(2,1)S(1)} %attend.5.refs_0_), channel_id=1, source_target_pairs={{0,2},{1,3},{2,0},{3,1},{4,6},{5,7},{6,4},{7,5},{8,10},{9,11},{10,... | collective-permute-start | bytes 196616 | tf_op jit(solution)/shard_map/ppermute | solution.py:36
  70.0 6.7 %collective-permute-start.50 = (bf16[64,512]{1,0:T(8,128)(2,1)S(1)}, bf16[64,512]{1,0:T(8,128)(2,1)S(1)}, u32[]{:S(2)}, u32[]{:S(2)}) collective-permute-start(bf16[64,512]{1,0:T(8,128)(2,1)S(1)} %attend.5.refs_0_), channel_id=1, source_target_pairs={{0,6},{1,7},{2,4},{3,5},{4,2},{5,3},{6,0},{7,1},{8,14},{9,15},{10,... | collective-permute-start | bytes 196616 | tf_op jit(solution)/shard_map/ppermute | solution.py:36
  72.0 6.2 %collective-permute-start.45 = (bf16[64,512]{1,0:T(8,128)(2,1)S(1)}, bf16[64,512]{1,0:T(8,128)(2,1)S(1)}, u32[]{:S(2)}, u32[]{:S(2)}) collective-permute-start(bf16[64,512]{1,0:T(8,128)(2,1)S(1)} %attend.5.refs_0_), channel_id=1, source_target_pairs={{0,1},{1,0},{2,3},{3,2},{4,5},{5,4},{6,7},{7,6},{8,9},{9,8},{10,11... | collective-permute-start | bytes 196616 | tf_op jit(solution)/shard_map/ppermute | solution.py:36
  73.9 4.3 %collective-permute-start.47 = (bf16[64,512]{1,0:T(8,128)(2,1)S(1)}, bf16[64,512]{1,0:T(8,128)(2,1)S(1)}, u32[]{:S(2)}, u32[]{:S(2)}) collective-permute-start(bf16[64,512]{1,0:T(8,128)(2,1)S(1)} %collective-permute-done.46.refs_2_), channel_id=1, source_target_pairs={{0,1},{1,0},{2,3},{3,2},{4,5},{5,4},{6,7},{7,6},{8,9},{9,8},{10,11... | collective-permute-start | bytes 196616 | tf_op jit(solution)/shard_map/ppermute | solution.py:36
  84.0 4.6 %collective-permute-start.61 = (bf16[16,1152]{1,0:T(8,128)(2,1)S(1)}, bf16[16,1152]{1,0:T(8,128)(2,1)S(1)}, u32[]{:S(2)}, u32[]{:S(2)}) collective-permute-start(bf16[16,1152]{1,0:T(8,128)(2,1)S(1)} %get-tuple-element.154), channel_id=1, source_target_pairs={{0,4},{1,5},{2,6},{3,7},{4,0},{5,1},{6,2},{7,3},{8,12},{9,13},{10,... | collective-permute-start | bytes 110600 | tf_op jit(solution)/shard_map/ppermute | solution.py:36
  84.0 4.6 %collective-permute-start.62 = (bf16[16,1152]{1,0:T(8,128)(2,1)S(1)}, bf16[16,1152]{1,0:T(8,128)(2,1)S(1)}, u32[]{:S(2)}, u32[]{:S(2)}) collective-permute-start(bf16[16,1152]{1,0:T(8,128)(2,1)S(1)} %get-tuple-element.155), channel_id=1, source_target_pairs={{0,2},{1,3},{2,0},{3,1},{4,6},{5,7},{6,4},{7,5},{8,10},{9,11},{10,... | collective-permute-start | bytes 110600 | tf_op jit(solution)/shard_map/ppermute | solution.py:36
  85.8 4.6 %collective-permute-start.63 = (bf16[16,1152]{1,0:T(8,128)(2,1)S(1)}, bf16[16,1152]{1,0:T(8,128)(2,1)S(1)}, u32[]{:S(2)}, u32[]{:S(2)}) collective-permute-start(bf16[16,1152]{1,0:T(8,128)(2,1)S(1)} %get-tuple-element.156), channel_id=1, source_target_pairs={{0,6},{1,7},{2,4},{3,5},{4,2},{5,3},{6,0},{7,1},{8,14},{9,15},{10,... | collective-permute-start | bytes 110600 | tf_op jit(solution)/shard_map/ppermute | solution.py:36
  87.5 5.3 %collective-permute-start.60 = (bf16[16,1152]{1,0:T(8,128)(2,1)S(1)}, bf16[16,1152]{1,0:T(8,128)(2,1)S(1)}, u32[]{:S(2)}, u32[]{:S(2)}) collective-permute-start(bf16[16,1152]{1,0:T(8,128)(2,1)S(1)} %get-tuple-element.153.refs_3_), channel_id=1, source_target_pairs={{0,1},{1,0},{2,3},{3,2},{4,5},{5,4},{6,7},{7,6},{8,9},{9,8},{10,11... | collective-permute-start | bytes 110600 | tf_op jit(solution)/shard_map/ppermute | solution.py:36
  93.7 3.7 %collective-permute-start.67 = (bf16[8,1280]{1,0:T(8,128)(2,1)S(1)}, bf16[8,1280]{1,0:T(8,128)(2,1)S(1)}, u32[]{:S(2)}, u32[]{:S(2)}) collective-permute-start(bf16[8,1280]{1,0:T(8,128)(2,1)S(1)} %get-tuple-element.160), channel_id=1, source_target_pairs={{0,4},{1,5},{2,6},{3,7},{4,0},{5,1},{6,2},{7,3},{8,12},{9,13},{10,... | collective-permute-start | bytes 61448 | tf_op jit(solution)/shard_map/ppermute | solution.py:36
  93.7 4.6 %collective-permute-start.68 = (bf16[8,1280]{1,0:T(8,128)(2,1)S(1)}, bf16[8,1280]{1,0:T(8,128)(2,1)S(1)}, u32[]{:S(2)}, u32[]{:S(2)}) collective-permute-start(bf16[8,1280]{1,0:T(8,128)(2,1)S(1)} %get-tuple-element.161), channel_id=1, source_target_pairs={{0,6},{1,7},{2,4},{3,5},{4,2},{5,3},{6,0},{7,1},{8,14},{9,15},{10,... | collective-permute-start | bytes 61448 | tf_op jit(solution)/shard_map/ppermute | solution.py:36
  95.4 3.3 %collective-permute-start.69 = (bf16[8,1280]{1,0:T(8,128)(2,1)S(1)}, bf16[8,1280]{1,0:T(8,128)(2,1)S(1)}, u32[]{:S(2)}, u32[]{:S(2)}) collective-permute-start(bf16[8,1280]{1,0:T(8,128)(2,1)S(1)} %get-tuple-element.162), channel_id=1, source_target_pairs={{0,2},{1,3},{2,0},{3,1},{4,6},{5,7},{6,4},{7,5},{8,10},{9,11},{10,... | collective-permute-start | bytes 61448 | tf_op jit(solution)/shard_map/ppermute | solution.py:36
  99.3 5.5 %collective-permute-start.71 = (bf16[64,512]{1,0:T(8,128)(2,1)S(1)}, bf16[64,512]{1,0:T(8,128)(2,1)S(1)}, u32[]{:S(2)}, u32[]{:S(2)}) collective-permute-start(bf16[64,512]{1,0:T(8,128)(2,1)S(1)} %attend.6.refs_0_), channel_id=1, source_target_pairs={{0,4},{1,5},{2,6},{3,7},{4,0},{5,1},{6,2},{7,3},{8,12},{9,13},{10,... | collective-permute-start | bytes 196616 | tf_op jit(solution)/shard_map/ppermute | solution.py:36
  100.1 7.5 %collective-permute-start.73 = (bf16[64,512]{1,0:T(8,128)(2,1)S(1)}, bf16[64,512]{1,0:T(8,128)(2,1)S(1)}, u32[]{:S(2)}, u32[]{:S(2)}) collective-permute-start(bf16[64,512]{1,0:T(8,128)(2,1)S(1)} %attend.6.refs_0_), channel_id=1, source_target_pairs={{0,2},{1,3},{2,0},{3,1},{4,6},{5,7},{6,4},{7,5},{8,10},{9,11},{10,... | collective-permute-start | bytes 196616 | tf_op jit(solution)/shard_map/ppermute | solution.py:36
  100.9 6.7 %collective-permute-start.75 = (bf16[64,512]{1,0:T(8,128)(2,1)S(1)}, bf16[64,512]{1,0:T(8,128)(2,1)S(1)}, u32[]{:S(2)}, u32[]{:S(2)}) collective-permute-start(bf16[64,512]{1,0:T(8,128)(2,1)S(1)} %attend.6.refs_0_), channel_id=1, source_target_pairs={{0,6},{1,7},{2,4},{3,5},{4,2},{5,3},{6,0},{7,1},{8,14},{9,15},{10,... | collective-permute-start | bytes 196616 | tf_op jit(solution)/shard_map/ppermute | solution.py:36
  102.9 6.2 %collective-permute-start.70 = (bf16[64,512]{1,0:T(8,128)(2,1)S(1)}, bf16[64,512]{1,0:T(8,128)(2,1)S(1)}, u32[]{:S(2)}, u32[]{:S(2)}) collective-permute-start(bf16[64,512]{1,0:T(8,128)(2,1)S(1)} %attend.6.refs_0_), channel_id=1, source_target_pairs={{0,1},{1,0},{2,3},{3,2},{4,5},{5,4},{6,7},{7,6},{8,9},{9,8},{10,11... | collective-permute-start | bytes 196616 | tf_op jit(solution)/shard_map/ppermute | solution.py:36
  104.9 4.3 %collective-permute-start.72 = (bf16[64,512]{1,0:T(8,128)(2,1)S(1)}, bf16[64,512]{1,0:T(8,128)(2,1)S(1)}, u32[]{:S(2)}, u32[]{:S(2)}) collective-permute-start(bf16[64,512]{1,0:T(8,128)(2,1)S(1)} %collective-permute-done.71.refs_2_), channel_id=1, source_target_pairs={{0,1},{1,0},{2,3},{3,2},{4,5},{5,4},{6,7},{7,6},{8,9},{9,8},{10,11... | collective-permute-start | bytes 196616 | tf_op jit(solution)/shard_map/ppermute | solution.py:36
  110.0 37.1 %collective-permute-start.77 = (bf16[32,1024]{1,0:T(8,128)(2,1)S(1)}, bf16[32,1024]{1,0:T(8,128)(2,1)S(1)}, u32[]{:S(2)}, u32[]{:S(2)}) collective-permute-start(bf16[32,1024]{1,0:T(8,128)(2,1)S(1)} %get-tuple-element.165), channel_id=1, source_target_pairs={{16,28},{17,29},{18,30},{19,31},{20,24},{21,25},{22,26},{23,27}} | collective-permute-start | bytes 196616 | tf_op jit(solution)/shard_map/ppermute | solution.py:69
  111.3 39.4 %collective-permute-start.79 = (bf16[32,1024]{1,0:T(8,128)(2,1)S(1)}, bf16[32,1024]{1,0:T(8,128)(2,1)S(1)}, u32[]{:S(2)}, u32[]{:S(2)}) collective-permute-start(bf16[32,1024]{1,0:T(8,128)(2,1)S(1)} %get-tuple-element.165), channel_id=1, source_target_pairs={{16,30},{17,31},{18,28},{19,29},{20,26},{21,27},{22,24},{23,25}} | collective-permute-start | bytes 196616 | tf_op jit(solution)/shard_map/ppermute | solution.py:69
  112.6 39.1 %collective-permute-start.81 = (bf16[32,1024]{1,0:T(8,128)(2,1)S(1)}, bf16[32,1024]{1,0:T(8,128)(2,1)S(1)}, u32[]{:S(2)}, u32[]{:S(2)}) collective-permute-start(bf16[32,1024]{1,0:T(8,128)(2,1)S(1)} %get-tuple-element.165), channel_id=1, source_target_pairs={{16,26},{17,27},{18,24},{19,25},{20,30},{21,31},{22,28},{23,29}} | collective-permute-start | bytes 196616 | tf_op jit(solution)/shard_map/ppermute | solution.py:69
  113.9 38.4 %collective-permute-start.83 = (bf16[32,1024]{1,0:T(8,128)(2,1)S(1)}, bf16[32,1024]{1,0:T(8,128)(2,1)S(1)}, u32[]{:S(2)}, u32[]{:S(2)}) collective-permute-start(bf16[32,1024]{1,0:T(8,128)(2,1)S(1)} %get-tuple-element.165), channel_id=1, source_target_pairs={{16,24},{17,25},{18,26},{19,27},{20,28},{21,29},{22,30},{23,31}} | collective-permute-start | bytes 196616 | tf_op jit(solution)/shard_map/ppermute | solution.py:69
  147.1 5.7 %collective-permute-start.78 = (bf16[32,1024]{1,0:T(8,128)(2,1)S(1)}, bf16[32,1024]{1,0:T(8,128)(2,1)S(1)}, u32[]{:S(2)}, u32[]{:S(2)}) collective-permute-start(bf16[32,1024]{1,0:T(8,128)(2,1)S(1)} %collective-permute-done.77.refs_1_), channel_id=1, source_target_pairs={{0,1},{1,0},{2,3},{3,2},{4,5},{5,4},{6,7},{7,6},{8,9},{9,8},{10,11... | collective-permute-start | bytes 196616 | tf_op jit(solution)/shard_map/ppermute | solution.py:36
  155.0 8.0 %collective-permute-start.86 = (bf16[16,1152]{1,0:T(8,128)(2,1)S(1)}, bf16[16,1152]{1,0:T(8,128)(2,1)S(1)}, u32[]{:S(2)}, u32[]{:S(2)}) collective-permute-start(bf16[16,1152]{1,0:T(8,128)(2,1)S(1)} %get-tuple-element.168), channel_id=1, source_target_pairs={{0,4},{1,5},{2,6},{3,7},{4,0},{5,1},{6,2},{7,3},{8,12},{9,13},{10,... | collective-permute-start | bytes 110600 | tf_op jit(solution)/shard_map/ppermute | solution.py:36
  156.6 6.4 %collective-permute-start.87 = (bf16[16,1152]{1,0:T(8,128)(2,1)S(1)}, bf16[16,1152]{1,0:T(8,128)(2,1)S(1)}, u32[]{:S(2)}, u32[]{:S(2)}) collective-permute-start(bf16[16,1152]{1,0:T(8,128)(2,1)S(1)} %get-tuple-element.169), channel_id=1, source_target_pairs={{0,2},{1,3},{2,0},{3,1},{4,6},{5,7},{6,4},{7,5},{8,10},{9,11},{10,... | collective-permute-start | bytes 110600 | tf_op jit(solution)/shard_map/ppermute | solution.py:36
  157.1 5.9 %collective-permute-start.88 = (bf16[16,1152]{1,0:T(8,128)(2,1)S(1)}, bf16[16,1152]{1,0:T(8,128)(2,1)S(1)}, u32[]{:S(2)}, u32[]{:S(2)}) collective-permute-start(bf16[16,1152]{1,0:T(8,128)(2,1)S(1)} %get-tuple-element.170), channel_id=1, source_target_pairs={{0,6},{1,7},{2,4},{3,5},{4,2},{5,3},{6,0},{7,1},{8,14},{9,15},{10,... | collective-permute-start | bytes 110600 | tf_op jit(solution)/shard_map/ppermute | solution.py:36
  161.8 3.2 %collective-permute-start.85 = (bf16[16,1152]{1,0:T(8,128)(2,1)S(1)}, bf16[16,1152]{1,0:T(8,128)(2,1)S(1)}, u32[]{:S(2)}, u32[]{:S(2)}) collective-permute-start(bf16[16,1152]{1,0:T(8,128)(2,1)S(1)} %get-tuple-element.167.refs_3_), channel_id=1, source_target_pairs={{0,1},{1,0},{2,3},{3,2},{4,5},{5,4},{6,7},{7,6},{8,9},{9,8},{10,11... | collective-permute-start | bytes 110600 | tf_op jit(solution)/shard_map/ppermute | solution.py:36
  165.7 3.6 %collective-permute-start.92 = (bf16[8,1280]{1,0:T(8,128)(2,1)S(1)}, bf16[8,1280]{1,0:T(8,128)(2,1)S(1)}, u32[]{:S(2)}, u32[]{:S(2)}) collective-permute-start(bf16[8,1280]{1,0:T(8,128)(2,1)S(1)} %get-tuple-element.174), channel_id=1, source_target_pairs={{0,4},{1,5},{2,6},{3,7},{4,0},{5,1},{6,2},{7,3},{8,12},{9,13},{10,... | collective-permute-start | bytes 61448 | tf_op jit(solution)/shard_map/ppermute | solution.py:36
  166.0 4.5 %collective-permute-start.93 = (bf16[8,1280]{1,0:T(8,128)(2,1)S(1)}, bf16[8,1280]{1,0:T(8,128)(2,1)S(1)}, u32[]{:S(2)}, u32[]{:S(2)}) collective-permute-start(bf16[8,1280]{1,0:T(8,128)(2,1)S(1)} %get-tuple-element.175), channel_id=1, source_target_pairs={{0,6},{1,7},{2,4},{3,5},{4,2},{5,3},{6,0},{7,1},{8,14},{9,15},{10,... | collective-permute-start | bytes 61448 | tf_op jit(solution)/shard_map/ppermute | solution.py:36
  167.7 3.2 %collective-permute-start.94 = (bf16[8,1280]{1,0:T(8,128)(2,1)S(1)}, bf16[8,1280]{1,0:T(8,128)(2,1)S(1)}, u32[]{:S(2)}, u32[]{:S(2)}) collective-permute-start(bf16[8,1280]{1,0:T(8,128)(2,1)S(1)} %get-tuple-element.176), channel_id=1, source_target_pairs={{0,2},{1,3},{2,0},{3,1},{4,6},{5,7},{6,4},{7,5},{8,10},{9,11},{10,... | collective-permute-start | bytes 61448 | tf_op jit(solution)/shard_map/ppermute | solution.py:36
  173.2 5.8 %collective-permute-start.100 = (bf16[64,512]{1,0:T(8,128)(2,1)S(1)}, bf16[64,512]{1,0:T(8,128)(2,1)S(1)}, u32[]{:S(2)}, u32[]{:S(2)}) collective-permute-start(bf16[64,512]{1,0:T(8,128)(2,1)S(1)} %attend.7.refs_0_), channel_id=1, source_target_pairs={{0,6},{1,7},{2,4},{3,5},{4,2},{5,3},{6,0},{7,1},{8,14},{9,15},{10,... | collective-permute-start | bytes 196616 | tf_op jit(solution)/shard_map/ppermute | solution.py:36
  174.5 7.1 %collective-permute-start.96 = (bf16[64,512]{1,0:T(8,128)(2,1)S(1)}, bf16[64,512]{1,0:T(8,128)(2,1)S(1)}, u32[]{:S(2)}, u32[]{:S(2)}) collective-permute-start(bf16[64,512]{1,0:T(8,128)(2,1)S(1)} %attend.7.refs_0_), channel_id=1, source_target_pairs={{0,4},{1,5},{2,6},{3,7},{4,0},{5,1},{6,2},{7,3},{8,12},{9,13},{10,... | collective-permute-start | bytes 196616 | tf_op jit(solution)/shard_map/ppermute | solution.py:36
  174.9 8.1 %collective-permute-start.98 = (bf16[64,512]{1,0:T(8,128)(2,1)S(1)}, bf16[64,512]{1,0:T(8,128)(2,1)S(1)}, u32[]{:S(2)}, u32[]{:S(2)}) collective-permute-start(bf16[64,512]{1,0:T(8,128)(2,1)S(1)} %attend.7.refs_0_), channel_id=1, source_target_pairs={{0,2},{1,3},{2,0},{3,1},{4,6},{5,7},{6,4},{7,5},{8,10},{9,11},{10,... | collective-permute-start | bytes 196616 | tf_op jit(solution)/shard_map/ppermute | solution.py:36
  176.7 6.3 %collective-permute-start.95 = (bf16[64,512]{1,0:T(8,128)(2,1)S(1)}, bf16[64,512]{1,0:T(8,128)(2,1)S(1)}, u32[]{:S(2)}, u32[]{:S(2)}) collective-permute-start(bf16[64,512]{1,0:T(8,128)(2,1)S(1)} %attend.7.refs_0_), channel_id=1, source_target_pairs={{0,1},{1,0},{2,3},{3,2},{4,5},{5,4},{6,7},{7,6},{8,9},{9,8},{10,11... | collective-permute-start | bytes 196616 | tf_op jit(solution)/shard_map/ppermute | solution.py:36
  179.0 4.1 %collective-permute-start.101 = (bf16[64,512]{1,0:T(8,128)(2,1)S(1)}, bf16[64,512]{1,0:T(8,128)(2,1)S(1)}, u32[]{:S(2)}, u32[]{:S(2)}) collective-permute-start(bf16[64,512]{1,0:T(8,128)(2,1)S(1)} %collective-permute-done.100.refs_6_), channel_id=1, source_target_pairs={{0,1},{1,0},{2,3},{3,2},{4,5},{5,4},{6,7},{7,6},{8,9},{9,8},{10,11... | collective-permute-start | bytes 196616 | tf_op jit(solution)/shard_map/ppermute | solution.py:36
  188.4 4.5 %collective-permute-start.102 = (bf16[8,1024]{1,0:T(8,128)(2,1)S(1)}, bf16[8,1024]{1,0:T(8,128)(2,1)S(1)}, u32[]{:S(2)}, u32[]{:S(2)}) collective-permute-start(bf16[8,1024]{1,0:T(8,128)(2,1)S(1)} %get-tuple-element.179), channel_id=1, source_target_pairs={{0,6},{1,7},{2,4},{3,5},{4,2},{5,3},{6,0},{7,1},{8,14},{9,15},{10,... | collective-permute-start | bytes 49160 | tf_op jit(solution)/shard_map/ppermute | solution.py:36
  189.7 4.4 %collective-permute-start.104 = (bf16[8,1024]{1,0:T(8,128)(2,1)S(1)}, bf16[8,1024]{1,0:T(8,128)(2,1)S(1)}, u32[]{:S(2)}, u32[]{:S(2)}) collective-permute-start(bf16[8,1024]{1,0:T(8,128)(2,1)S(1)} %get-tuple-element.180), channel_id=1, source_target_pairs={{0,4},{1,5},{2,6},{3,7},{4,0},{5,1},{6,2},{7,3},{8,12},{9,13},{10,... | collective-permute-start | bytes 49160 | tf_op jit(solution)/shard_map/ppermute | solution.py:36
  189.7 5.1 %collective-permute-start.106 = (bf16[8,1024]{1,0:T(8,128)(2,1)S(1)}, bf16[8,1024]{1,0:T(8,128)(2,1)S(1)}, u32[]{:S(2)}, u32[]{:S(2)}) collective-permute-start(bf16[8,1024]{1,0:T(8,128)(2,1)S(1)} %get-tuple-element.181), channel_id=1, source_target_pairs={{0,2},{1,3},{2,0},{3,1},{4,6},{5,7},{6,4},{7,5},{8,10},{9,11},{10,... | collective-permute-start | bytes 49160 | tf_op jit(solution)/shard_map/ppermute | solution.py:36
  191.9 2.9 %collective-permute-start.108 = (bf16[8,1024]{1,0:T(8,128)(2,1)S(1)}, bf16[8,1024]{1,0:T(8,128)(2,1)S(1)}, u32[]{:S(2)}, u32[]{:S(2)}) collective-permute-start(bf16[8,1024]{1,0:T(8,128)(2,1)S(1)} %get-tuple-element.182.refs_7_), channel_id=1, source_target_pairs={{0,1},{1,0},{2,3},{3,2},{4,5},{5,4},{6,7},{7,6},{8,9},{9,8},{10,11... | collective-permute-start | bytes 49160 | tf_op jit(solution)/shard_map/ppermute | solution.py:36
  (49 other events, 93.6 us)
